TPU v7x, 32 devices: a whole 2x2x4 slice. The times are simulated.
32 devices in a mesh: stream: 2 (over core), dp: 16 (over z, y, x).
Axes of the slice: x: 2, y: 2, z: 4, core: 2. Of those that a mesh axis runs over, the one named last changes fastest.
Arguments:
- tokens: bfloat16 [2, 16, 256, 1152], P('stream', 'dp'), may hold values from -6 to 6
- condition: float32 [2, 16, 1152], P('stream', 'dp'), may hold values from -6 to 6
- kept_index: int32 [16, 256], P('dp'), may hold values from 0 to 255, as said below
- kept_count: int32 [16], P('dp'), may hold values from 160 to 200, as said below
- cotangent: bfloat16 [2, 16, 256, 1152], P('stream', 'dp'), may hold values from -6 to 6
- w_ada: bfloat16 [1152, 6912], P('dp'), may hold values from -0.1875 to 0.1875
- w_qkv: bfloat16 [1152, 3456], P('dp'), may hold values from -0.1875 to 0.1875
- w_proj: bfloat16 [1152, 1152], P('dp'), may hold values from -1.5 to 1.5
- w_fc1: bfloat16 [1152, 4608], P('dp'), may hold values from -0.1875 to 0.1875
- w_fc2: bfloat16 [4608, 1152], P('dp'), may hold values from -0.09375 to 0.09375
- b_ada: float32 [6912], replicated, may hold values from -3 to 3
- b_qv: float32 [2304], replicated, may hold values from -3 to 3
- b_proj: float32 [1152], replicated, may hold values from -3 to 3
- b_fc1: float32 [4608], replicated, may hold values from -3 to 3
- b_fc2: float32 [1152], replicated, may hold values from -3 to 3
- rel_table: float32 [961, 16], replicated, may hold values from -5 to 5
Outputs:
- out_tokens: bfloat16 [2, 16, 256, 1152], P('stream', 'dp')
- grad_tokens: bfloat16 [2, 16, 256, 1152], P('stream', 'dp')
- grad_condition: float32 [2, 16, 1152], P('stream', 'dp')
- grad_w_ada: float32 [1152, 6912], P('dp')
- grad_w_qkv: float32 [1152, 3456], P('dp')
- grad_w_proj: float32 [1152, 1152], P('dp')
- grad_w_fc1: float32 [1152, 4608], P('dp')
- grad_w_fc2: float32 [4608, 1152], P('dp')
- grad_b_ada: float32 [6912], replicated
- grad_b_qv: float32 [2304], replicated
- grad_b_proj: float32 [1152], replicated
- grad_b_fc1: float32 [4608], replicated
- grad_b_fc2: float32 [1152], replicated
- grad_rel_table: float32 [961, 16], replicated
Inputs may be any that keep to these rules, and one draw needn't show every extreme that they name: kept_count takes 200 on the first sample and 160 on the last. `kept_index`: the first kept_count entries of a row are distinct and increasing; the rest are 0.
All inputs are finite; a program needn't handle non-finite values.
Results may differ from a plain program's by a relative error of at most 0.015.
The roundings to bfloat16 on the way count: a program that leaves them out, or rounds other values in their place, can miss the bound.
Values may be sent and summed in bfloat16 or wider, within the bound.
No kernel may reach another device: no remote copies, remote signals or barrier semaphores. Data moves between devices by JAX's collectives and lax.ppermute only.
A program may use at most 384 MiB of HBM per device.

v0:
```python
import functools
import math

import jax
import jax.numpy as jnp
from jax import lax
from jax.experimental import pallas as pl
from jax.experimental.pallas import tpu as pltpu
from jax.sharding import PartitionSpec as P

HEADS = 16
GRID = 16
BF = jnp.bfloat16
F32 = jnp.float32


def swap(v, bit, n):
    return lax.ppermute(v, "dp", [(i, i ^ bit) for i in range(n)])


def swap_stream(v):
    return lax.ppermute(v, "stream", [(0, 1), (1, 0)])


def axis_bits(n):
    k = n.bit_length() - 1
    s = k // 3
    xs = [1 << i for i in range(s)]
    ys = [1 << (s + i) for i in range(s)]
    zs = [1 << i for i in range(2 * s, k)]
    return xs, ys, zs


def all_bits(n):
    return [1 << i for i in range(n.bit_length() - 1)]


def orders_out(n):
    xs, ys, zs = axis_bits(n)
    near = zs[:1]
    return zs[1:][::-1], (near + ys + xs, xs + near + ys, ys + xs + near)


def trade(v):
    return lax.all_to_all(v, "dp", 0, 0, tiled=True)


def mm(a, b):
    return lax.dot_general(a, b, (((1,), (0,)), ((), ())), preferred_element_type=F32)


def mm_nt(a, b):
    return lax.dot_general(a, b, (((1,), (1,)), ((), ())), preferred_element_type=F32)


def mm_tn(a, b):
    return lax.dot_general(a, b, (((0,), (0,)), ((), ())), preferred_element_type=F32)


def normal(v):
    center = v - jnp.mean(v, axis=-1, keepdims=True)
    inv = lax.rsqrt(jnp.mean(center * center, axis=-1, keepdims=True) + 1e-06)
    return center * inv, inv


def normal_back(g, n, inv):
    return inv * (g - jnp.mean(g, axis=-1, keepdims=True) - n * jnp.mean(g * n, axis=-1, keepdims=True))


def bias_windows(table):
    w = 2 * GRID - 1
    t = jnp.transpose(table.reshape(w, w, HEADS)[::-1, ::-1], (2, 0, 1))
    t = jnp.pad(t, ((0, 0), (0, 1), (0, 1))).reshape(HEADS, w + 1, 2, GRID)
    return t[:, :, 0].reshape(HEADS, -1), t[:, :, 1].reshape(HEADS, -1)


def table_of(lo, hi):
    w = 2 * GRID - 1
    t = jnp.stack([lo.reshape(HEADS, w + 1, GRID), hi.reshape(HEADS, w + 1, GRID)], axis=2)
    t = t.reshape(HEADS, w + 1, 2 * GRID)[:, :w, :w]
    return jnp.transpose(t, (1, 2, 0))[::-1, ::-1].reshape(w * w, HEADS)


def gelu_parts(x):
    k = math.sqrt(2.0 / math.pi)
    th = jnp.tanh(k * (x + 0.044715 * x * x * x))
    value = 0.5 * x * (1.0 + th)
    slope = 0.5 * (1.0 + th) + 0.5 * x * (1.0 - th * th) * k * (1.0 + 3 * 0.044715 * x * x)
    return value, slope


VMEM_BYTES = 56 * 1024 * 1024
SUM_ROWS = 200
WHOLE = pl.BlockSpec(memory_space=pltpu.VMEM)
HBM = pl.BlockSpec(memory_space=pl.ANY)
SCALAR = pl.BlockSpec(memory_space=pltpu.SMEM)


def shape(dims, dtype):
    return jax.ShapeDtypeStruct(dims, dtype)


def params():
    return pltpu.CompilerParams(vmem_limit_bytes=VMEM_BYTES)


def cost(flops, size):
    return pl.CostEstimate(flops=int(flops), bytes_accessed=int(size), transcendentals=0)


def strips(total, tile, body):
    def step(i, carry):
        body(pl.multiple_of(i * tile, tile))
        return carry

    lax.fori_loop(0, total // tile, step, 0)


def fetch_halves(side_ref, own_ref, other_ref, w_ref, sem):
    side = side_ref[0]
    mine = pltpu.make_async_copy(own_ref, w_ref.at[side], sem.at[side])
    twin = pltpu.make_async_copy(other_ref, w_ref.at[1 - side], sem.at[1 - side])
    mine.start()
    twin.start()

    def wait(slot):
        pltpu.make_async_copy(own_ref, w_ref.at[slot], sem.at[slot]).wait()

    return wait


def pieces(n, rows, cut, s):
    half = cut // 2
    for part in range(2):
        for k in range(n):
            yield (k * 2 + s) * cut + part * half, (part * n + k) * half, half


def fc1_rows_kernel(n, side_ref, own_ref, other_ref, out_ref):
    rows, ff = out_ref.shape
    cut = ff // (2 * n)
    for s in range(2):

        @pl.when(side_ref[0] == s)
        def _():
            for half, ref in ((s, own_ref), (1 - s, other_ref)):
                for src, dst, w in pieces(n, rows, cut, half):
                    out_ref[:, src : src + w] = ref[:, dst : dst + w]


def fc1_rows(n, side, own, other):
    return pl.pallas_call(
        functools.partial(fc1_rows_kernel, n),
        out_shape=shape((own.shape[0], 2 * own.shape[1]), F32),
        in_specs=[SCALAR, WHOLE, WHOLE],
        out_specs=WHOLE,
        compiler_params=params(),
        name="fc1_rows",
    )(side, own, other)


def strip_kernel(lo_ref, hi_ref, out_ref):
    lanes = lo_ref.shape[1]
    lo, hi = lo_ref[...], hi_ref[...]
    j = lax.broadcasted_iota(jnp.int32, lo.shape, 1) % GRID
    for i in range(GRID):
        k = GRID - 1 - i
        a = pltpu.roll(lo, lanes - k, 1) if k else lo
        out_ref[:, i, :] = jnp.where(j < GRID - k, a, pltpu.roll(hi, GRID - k, 1))


def bias_strip(table):
    lo, hi = bias_windows(table)
    return pl.pallas_call(
        strip_kernel,
        out_shape=shape((HEADS, GRID, lo.shape[1]), F32),
        in_specs=[WHOLE, WHOLE],
        out_specs=WHOLE,
        name="bias_strip",
    )(lo, hi)


def bias_of(strip):
    return jnp.concatenate(
        [strip[:, (GRID - 1 - y) * GRID : (2 * GRID - 1 - y) * GRID] for y in range(GRID)], axis=0
    )


def put(i, pos):
    return (i >> pos) << (pos + 1) | (i & ((1 << pos) - 1))


def attn_shard_kernel(side_ref, qkv_ref, proj_ref, out_ref):
    width = proj_ref.shape[1]
    for s in range(2):

        @pl.when(side_ref[0] == s)
        def _():
            if s == 0:
                out_ref[0] = qkv_ref[:, 0 : 2 * width]
            else:
                out_ref[0, :, 0:width] = qkv_ref[:, 2 * width :]
                out_ref[0, :, width:] = proj_ref[...]


def mlp_shard_kernel(n, side_ref, f1_ref, f2_ref, *rest):
    out_ref = rest[-1]
    rows, ff = f1_ref.shape
    width = f2_ref.shape[1]
    cut = ff // (2 * n)
    for s in range(2):

        @pl.when(side_ref[0] == s)
        def _():
            for src, dst, w in pieces(n, rows, cut, s):
                out_ref[0, :, dst : dst + w] = f1_ref[:, src : src + w]
            for part in range(2):
                lo = s * cut + part * rows
                cols = slice(ff // 2 + part * width, ff // 2 + (part + 1) * width)
                out_ref[0, :, cols] = f2_ref[lo : lo + rows, :]


def mlp_shard(n, side, f1, f2, after=()):
    return pl.pallas_call(
        functools.partial(mlp_shard_kernel, n),
        out_shape=shape((1,) + f1.shape, BF),
        in_specs=[SCALAR, WHOLE, WHOLE] + [HBM] * len(after),
        out_specs=WHOLE,
        compiler_params=params(),
        name="mlp_shard",
    )(side, f1, f2, *after)


def attn_shard(side, w_qkv, w_proj):
    rows, width = w_proj.shape
    return pl.pallas_call(
        attn_shard_kernel,
        out_shape=shape((1, rows, 2 * width), BF),
        in_specs=[SCALAR, WHOLE, WHOLE],
        out_specs=WHOLE,
        compiler_params=params(),
        name="attn_shard",
    )(side, w_qkv, w_proj)


def join_kernel(jobs, chip_ref, *refs):
    outs = refs[-sum(len(cols) for _, cols in jobs) :]
    at = 0
    for k, (bit, cols) in enumerate(jobs):
        v_ref, r_ref = refs[2 * k], refs[2 * k + 1]
        m = v_ref.shape[0]
        up = (chip_ref[0] & bit) // bit
        lo = 0
        for c in cols:
            for i in range(m):
                outs[at][up * m + i] = v_ref[i, :, lo : lo + c]
                outs[at][(1 - up) * m + i] = r_ref[i, :, lo : lo + c]
            lo += c
            at += 1


def join(chip, jobs, after=()):
    flat = [t for v, r, _, _ in jobs for t in (v, r)]
    return pl.pallas_call(
        functools.partial(join_kernel, [(bit, cols) for _, _, bit, cols in jobs]),
        out_shape=tuple(
            shape((2 * v.shape[0], v.shape[1], c), v.dtype) for v, _, _, cols in jobs for c in cols
        ),
        in_specs=[SCALAR] + [WHOLE] * len(flat) + [HBM] * len(after),
        out_specs=(WHOLE,) * sum(len(cols) for _, _, _, cols in jobs),
        compiler_params=params(),
        name="join",
    )(chip, *flat, *after)


def assemble_kernel(orders, chip_ref, *refs):
    out_ref = refs[-1]
    lo = 0
    m = out_ref.shape[0] // 2
    for k, bits in enumerate(orders):
        v_ref, r_ref = refs[2 * k], refs[2 * k + 1]
        c = v_ref.shape[2]
        last = bits[-1]
        up = (chip_ref[0] & last) // last
        lead = bits[:-1][::-1]
        for i in range(m):
            base = sum(b for j, b in enumerate(lead) if (i >> (len(lead) - 1 - j)) & 1)
            out_ref[base + up * last, :, lo : lo + c] = v_ref[i]
            out_ref[base + (1 - up) * last, :, lo : lo + c] = r_ref[i]
        lo += c


def assemble(chip, orders, pairs, after=()):
    flat = [t for pair in pairs for t in pair]
    m, rows = 1 << (len(orders[0]) - 1), flat[0].shape[1]
    cols = sum(v.shape[2] for v, _ in pairs)
    out = pl.pallas_call(
        functools.partial(assemble_kernel, orders),
        out_shape=shape((2 * m, rows, cols), BF),
        in_specs=[SCALAR] + [WHOLE] * len(flat) + [HBM] * len(after),
        out_specs=WHOLE,
        compiler_params=params(),
        name="assemble",
    )(chip, *flat, *after)
    return out.reshape(2 * m * rows, cols)


class Gathering:
    def __init__(self, chip, v, n):
        first, parts = orders_out(n)
        self.chip, self.n = chip, n
        self.orders = [first + part for part in parts]
        self.turn, self.cut_at = 0, len(first)
        self.parts = [v]
        self.exchange()

    def exchange(self):
        self.came = [swap(v, self.orders[k][self.turn], self.n) for k, v in enumerate(self.parts)]
        self.turn += 1

    def step(self, *after):
        jobs = []
        for k, (v, r) in enumerate(zip(self.parts, self.came)):
            c = v.shape[2]
            cut = (c // 3,) * 3 if self.turn == self.cut_at else (c,)
            jobs.append((v, r, self.orders[k][self.turn - 1], cut))
        self.parts = list(join(self.chip, jobs, after))
        self.exchange()
        return tuple(self.parts)

    def done(self):
        return self.turn == len(self.orders[0])

    def result(self, *after):
        return assemble(self.chip, self.orders, tuple(zip(self.parts, self.came)), after=after)


def merge_kernel(bits, mates, chip_ref, *refs):
    small, (v_ref, r_ref), outs = refs[:6], refs[6:8], refs[-3:]
    up = lambda bit: (chip_ref[0] & bit) // bit
    m = small[0].shape[0]
    c = small[0].shape[2]
    far = v_ref.shape[0]
    for k in range(3):
        for ref, side in ((small[2 * k], up(bits[k])), (small[2 * k + 1], 1 - up(bits[k]))):
            for i in range(m):
                outs[k][side * m + i] = ref[i]
    for k in range(3):
        out_ref = outs[mates[k]]
        wide = v_ref.shape[2] // 3
        for ref, side in ((v_ref, up(bits[3])), (r_ref, 1 - up(bits[3]))):
            for h in range(wide // c):
                for i in range(far):
                    lo = k * wide + h * c
                    out_ref[2 * m + h * 2 * far + side * far + i] = ref[i, :, lo : lo + c]


def cross_kernel(bits, skip, chip_ref, *refs):
    outs = refs[-3:]
    for k, bit in enumerate(bits):
        v_ref, r_ref, out_ref = refs[2 * k], refs[2 * k + 1], outs[k]
        up = (chip_ref[0] & bit) // bit
        c = v_ref.shape[2]
        m = out_ref.shape[0] // 2
        for ref, side in ((v_ref, up), (r_ref, 1 - up)):
            for h in range(out_ref.shape[2] // c):
                for i in range(m):
                    out_ref[side * m + i, :, h * c : (h + 1) * c] = ref[skip + h * m + i]


def merge_steps(small, large, *after):
    n, turn = small.n, len(small.orders[0]) - 1
    next_small = [order[turn] for order in small.orders]
    next_large = [order[large.cut_at] for order in large.orders]
    mates = [next_small.index(bit) for bit in next_large]
    bits = [order[turn - 1] for order in small.orders] + [large.orders[0][large.cut_at - 1]]
    v, r = large.parts[0], large.came[0]
    _, rows, c = small.parts[0].shape
    m = 2 * small.parts[0].shape[0]
    far = 2 * v.shape[0]
    wide = v.shape[2] // 3
    flat = [t for pair in zip(small.parts, small.came) for t in pair]
    outs = pl.pallas_call(
        functools.partial(merge_kernel, bits, mates),
        out_shape=(shape((m + far * (wide // c), rows, c), BF),) * 3,
        in_specs=[SCALAR] + [WHOLE] * 8 + [HBM] * len(after),
        out_specs=(WHOLE,) * 3,
        compiler_params=params(),
        name="merge",
    )(small.chip, *flat, v, r, *after)
    came = [swap(t, bit, n) for t, bit in zip(outs, next_small)]

    def small_result(*after):
        return assemble(small.chip, small.orders, tuple(zip(outs, came)), after=after)

    def large_on(*after):
        pairs = [t for k in range(3) for t in (outs[mates[k]], came[mates[k]])]
        parts = pl.pallas_call(
            functools.partial(cross_kernel, next_large, m),
            out_shape=(shape((2 * far, rows, wide), BF),) * 3,
            in_specs=[SCALAR] + [WHOLE] * 6 + [HBM] * len(after),
            out_specs=(WHOLE,) * 3,
            compiler_params=params(),
            name="cross",
        )(large.chip, *pairs, *after)
        large.parts = list(parts)
        large.turn = large.cut_at + 1
        large.exchange()
        return tuple(parts)

    return outs, small_result, large_on


def product_kernel(n, firsts, steps, half_step, count, chip_ref, l0_ref, l1_ref, *rest):
    turned_ref = rest[-1]
    r_refs = rest[:count]
    outs = rest[-7:-1]
    t = pl.program_id(0)
    length = l0_ref.shape[0]
    width = turned_ref.shape[1]
    rows = width // n

    @pl.when(t == 0)
    def _():
        for k in range(turned_ref.shape[0]):
            cols = slice(k * width, (k + 1) * width)
            turned_ref[k, :, 0:length] = l0_ref[:, cols].T
            turned_ref[k, :, length:] = l1_ref[:, cols].T

    slot = jnp.where(t >= half_step, turned_ref.shape[0] - 1, 0)
    value, at = 0.0, 0
    for r_ref in r_refs:
        rows_here = r_ref.shape[0]
        value = value + mm(turned_ref[slot, :, at : at + rows_here], r_ref[...])
        at += rows_here
    for part, (bit, (lo, hi)) in enumerate(zip(firsts, steps)):
        pos = bit.bit_length() - 1
        for up in range(2):

            @pl.when((t >= lo) & (t < hi) & ((chip_ref[0] & bit) // bit == up))
            def _():
                for i in range(n // 2):
                    at = put(i, pos)
                    for goes, ref in ((up, outs[2 * part]), (1 - up, outs[2 * part + 1])):
                        k = at + goes * bit
                        ref[i] = value[k * rows : (k + 1) * rows].astype(BF)


def product(chip, l0, l1, r0, r1, width, n, firsts, after=()):
    length = l0.shape[0]
    tile = width // 3
    per = width // tile
    rights = (r0,) + (r1 if isinstance(r1, tuple) else (r1,))
    two_l, two_r = l0.shape[1] > width, r0.shape[1] > width
    cols = (2 * width // 3,) * 3
    steps = []
    for c in cols:
        lo = steps[-1][1] if steps else 0
        steps.append((lo, lo + c // tile))
    left = pl.BlockSpec(l0.shape, lambda t: (0, 0))
    right = [pl.BlockSpec((r.shape[0], tile), lambda t: (0, t if two_r else t % per)) for r in rights]
    spec = lambda lo, hi: pl.BlockSpec(
        (n // 2, width // n, tile), lambda t: (0, 0, jnp.clip(t - lo, 0, hi - lo - 1))
    )
    out = pl.pallas_call(
        functools.partial(product_kernel, n, firsts, steps, per, len(rights)),
        grid=(2 * per,),
        out_shape=tuple(shape((n // 2, width // n, c), BF) for c in cols for _ in range(2)),
        in_specs=[SCALAR, left, left] + right + [HBM] * len(after),
        out_specs=tuple(spec(*s) for s in steps for _ in range(2)),
        scratch_shapes=[pltpu.VMEM((1 + two_l, width, 2 * length), BF)],
        compiler_params=params(),
        cost_estimate=cost(8 * length * width * width, 12e6),
        name="product",
    )(chip, l0, l1, *rights, *after)
    return tuple((out[2 * k], out[2 * k + 1]) for k in range(3))


def split_kernel(jobs, chip_ref, *refs):
    outs = refs[-2 * len(jobs) :]
    at = 0
    for k, (bit, pos, count) in enumerate(jobs):
        keep_ref, send_ref = outs[2 * k], outs[2 * k + 1]
        up = (chip_ref[0] & bit) // bit
        lo = 0
        for _ in range(count):
            v_ref, r_ref = refs[at], refs[at + 1]
            at += 2
            c = v_ref.shape[2]
            for i in range(keep_ref.shape[0]):
                for out_ref, goes in ((send_ref, 1 - up), (keep_ref, up)):
                    j = put(i, pos) + goes * (1 << pos)
                    total = v_ref[j].astype(F32) + r_ref[j].astype(F32)
                    out_ref[i, :, lo : lo + c] = total.astype(BF)
            lo += c


def split(chip, jobs, after=()):
    flat = [t for pairs, _, _ in jobs for pair in pairs for t in pair]
    outs, plan = [], []
    for pairs, bit, left in jobs:
        m, rows, _ = pairs[0][0].shape
        cols = sum(v.shape[2] for v, _ in pairs)
        outs += [shape((m // 2, rows, cols), BF)] * 2
        plan.append((bit, len(left) - 1 - left.index(bit), len(pairs)))
    out = pl.pallas_call(
        functools.partial(split_kernel, plan),
        out_shape=tuple(outs),
        in_specs=[SCALAR] + [WHOLE] * len(flat) + [HBM] * len(after),
        out_specs=(WHOLE,) * len(outs),
        compiler_params=params(),
        name="split",
    )(chip, *flat, *after)
    return [(out[2 * k], out[2 * k + 1]) for k in range(len(jobs))]


def finish_kernel(v_ref, r_ref, *rest):
    rest[-1][...] = v_ref[0].astype(F32) + r_ref[0].astype(F32)


def finish(v, r, after=()):
    return pl.pallas_call(
        finish_kernel,
        out_shape=shape(v.shape[1:], F32),
        in_specs=[WHOLE] * 2 + [HBM] * len(after),
        out_specs=WHOLE,
        compiler_params=params(),
        name="finish",
    )(v, r, *after)


def meet_kernel(bit, rows, chip_ref, v_ref, r_ref, *rest):
    out_ref = rest[-1]
    out_ref[0:SUM_ROWS, :] = v_ref[0:SUM_ROWS, :] + r_ref[0:SUM_ROWS, :]
    up = (chip_ref[0] & bit) // bit
    for i in range((v_ref.shape[0] - SUM_ROWS) // rows):
        src = slice(SUM_ROWS + i * rows, SUM_ROWS + (i + 1) * rows)
        for ref, side in ((v_ref, up), (r_ref, 1 - up)):
            at = pl.multiple_of(SUM_ROWS + (2 * i + side) * rows, 8)
            out_ref[pl.ds(at, rows), :] = ref[src, :]


def meet(chip, v, r, bit, rows, after=()):
    total = 2 * v.shape[0] - SUM_ROWS
    return pl.pallas_call(
        functools.partial(meet_kernel, bit, rows),
        out_shape=shape((total, v.shape[1]), F32),
        in_specs=[SCALAR, WHOLE, WHOLE] + [HBM] * len(after),
        out_specs=WHOLE,
        compiler_params=params(),
        name="meet",
    )(chip, v, r, *after)


class Reduction:
    def __init__(self, chip, parts, n):
        last, orders = orders_out(n)
        self.chip, self.n = chip, n
        self.orders = [part[::-1] for part in orders]
        self.tail = last[::-1]
        self.left = [all_bits(n)[::-1] for _ in range(3)]
        self.pairs = [
            (keep, self.exchange(k, self.orders[k].pop(0), send)) for k, (keep, send) in enumerate(parts)
        ]

    def exchange(self, k, bit, send):
        self.left[k] = [b for b in self.left[k] if b != bit]
        return swap(send, bit, self.n)

    def plan(self):
        chains = [[k] for k in range(len(self.pairs))]
        if len(self.pairs) == 3 and not self.orders[0]:
            chains = [[0, 1, 2]]
            self.orders = [list(self.tail)]
        bits = [self.orders[chain[0]].pop(0) for chain in chains]
        return [
            ([self.pairs[j] for j in chain], bit, list(self.left[chain[0]]))
            for chain, bit in zip(chains, bits)
        ]

    def go(self, jobs, outs):
        self.pairs = [
            (keep, self.exchange(k, bit, send))
            for k, ((_, bit, _), (keep, send)) in enumerate(zip(jobs, outs))
        ]

    def done(self):
        return len(self.pairs) == 1 and not self.orders[0]

    def result(self, *after):
        return finish(*self.pairs[0], after)


def step(sums, *after):
    plans = [s.plan() for s in sums]
    outs = split(sums[0].chip, [job for jobs in plans for job in jobs], after)
    kept = tuple(keep for keep, _ in outs)
    for s, jobs in zip(sums, plans):
        s.go(jobs, outs[: len(jobs)])
        outs = outs[len(jobs) :]
    return kept


def fc2_rows_kernel(side_ref, own_ref, other_ref, out_ref):
    rows = own_ref.shape[0]
    width = out_ref.shape[1]
    for s in range(2):

        @pl.when(side_ref[0] == s)
        def _():
            for half, ref in ((s, own_ref), (1 - s, other_ref)):
                for part in range(2):
                    lo = (2 * half + part) * rows
                    out_ref[lo : lo + rows, :] = ref[:, part * width : (part + 1) * width]


def fc2_rows(side, own, other):
    return pl.pallas_call(
        fc2_rows_kernel,
        out_shape=shape((4 * own.shape[0], own.shape[1] // 2), F32),
        in_specs=[SCALAR, WHOLE, WHOLE],
        out_specs=WHOLE,
        compiler_params=params(),
        name="fc2_rows",
    )(side, own, other)


def attn_rows_kernel(side_ref, own_ref, other_ref, qkv_ref, proj_ref):
    width = proj_ref.shape[1]
    for s in range(2):

        @pl.when(side_ref[0] == s)
        def _():
            low, high = (own_ref, other_ref) if s == 0 else (other_ref, own_ref)
            qkv_ref[:, 0 : 2 * width] = low[...]
            qkv_ref[:, 2 * width :] = high[:, 0:width]
            proj_ref[...] = high[:, width:]


def attn_rows(side, own, other):
    rows, width = own.shape[0], own.shape[1] // 2
    return pl.pallas_call(
        attn_rows_kernel,
        out_shape=(shape((rows, 3 * width), F32), shape((rows, width), F32)),
        in_specs=[SCALAR, WHOLE, WHOLE],
        out_specs=(WHOLE, WHOLE),
        compiler_params=params(),
        name="attn_rows",
    )(side, own, other)


def hold_kernel(*refs):
    pass


def hold(values, *after):
    many = isinstance(values, tuple)
    values = values if many else (values,)
    out = pl.pallas_call(
        hold_kernel,
        out_shape=tuple(shape(v.shape, v.dtype) for v in values),
        in_specs=[HBM] * (len(values) + len(after)),
        out_specs=(HBM,) * len(values),
        input_output_aliases={k: k for k in range(len(values))},
        name="hold",
    )(*values, *after)
    return out if many else out[0]


def attention_kernel(
    side_ref,
    own_ref,
    other_ref,
    normed_ref,
    bqv_ref,
    strip_ref,
    keep_ref,
    x_ref,
    mod_ref,
    bproj_ref,
    qh_ref,
    kh_ref,
    vh_ref,
    mine_ref,
    theirs_ref,
    attended_ref,
    middle_ref,
    normed_two_ref,
    w_out_ref,
    w_ref,
    flat_ref,
    mix_ref,
    sem,
):
    length, width = x_ref.shape
    hd = width // HEADS
    tile = 384
    wait = fetch_halves(side_ref, own_ref, other_ref, w_ref, sem)
    normed = normed_ref[...]

    def project(slot, lo, cols, at, bias_at):
        def body(o):
            y = mm(normed, w_ref[slot, :, pl.ds(lo + o, tile)])
            if bias_at is not None:
                y = y + bqv_ref[:, pl.ds(bias_at + o, tile)]
            flat_ref[:, pl.ds(at + o, tile)] = y.astype(BF)

        strips(cols, tile, body)

    wait(0)
    project(0, 0, width, 0, 0)
    project(0, width, width, width, None)
    wait(1)
    keep_out = pltpu.make_async_copy(w_ref.at[1, :, pl.ds(width, width)], w_out_ref, sem.at[2])
    keep_out.start()
    project(1, 0, width, 2 * width, width)
    for h in range(HEADS):
        qh_ref[h] = flat_ref[:, h * hd : (h + 1) * hd]
        kh_ref[h] = flat_ref[:, width + h * hd : width + (h + 1) * hd]
        vh_ref[h] = flat_ref[:, 2 * width + h * hd : 2 * width + (h + 1) * hd]
    keep = keep_ref[...] > 0.0

    def head(h, carry):
        sc = mm_nt(qh_ref[h], kh_ref[h]) * (hd**-0.5) + bias_of(strip_ref[h])
        sc = jnp.where(keep, sc, -1e30)
        ex = jnp.exp(sc - jnp.max(sc, axis=-1, keepdims=True))
        soft = ex / jnp.sum(ex, axis=-1, keepdims=True)
        mix_ref[h] = mm(soft.astype(BF), vh_ref[h]).astype(BF)
        return carry

    lax.fori_loop(0, HEADS, head, 0)
    for h in range(HEADS):
        flat_ref[:, h * hd : (h + 1) * hd] = mix_ref[h]
    mixed = flat_ref[:, 0:width]
    mine_ref[:, 0:width] = normed
    theirs_ref[:, 0:width] = normed
    for s, (normed_at, mixed_at) in enumerate(((mine_ref, theirs_ref), (theirs_ref, mine_ref))):

        @pl.when(side_ref[0] == s)
        def _():
            normed_at[:, width:] = normed
            mixed_at[:, width:] = mixed

    def out(o):
        y = mm(mixed, w_ref[1, :, pl.ds(width + o, tile)]) + bproj_ref[:, pl.ds(o, tile)]
        attended_ref[:, pl.ds(o, tile)] = y

    strips(width, tile, out)
    middle = x_ref[...] + mod_ref[2:3, :] * attended_ref[...]
    middle_ref[...] = middle
    n2, _ = normal(middle)
    normed_two_ref[...] = (n2 * (1.0 + mod_ref[4:5, :]) + mod_ref[3:4, :]).astype(BF)
    keep_out.wait()


def attention(side, own, other, normed, b_qv, bias, keep, x, mod, b_proj):
    length, width = x.shape
    hd = width // HEADS
    per_head = shape((HEADS, length, hd), BF)
    return pl.pallas_call(
        attention_kernel,
        out_shape=(
            per_head,
            per_head,
            per_head,
            shape((length, 2 * width), BF),
            shape((length, 2 * width), BF),
            shape((length, width), F32),
            shape((length, width), F32),
            shape((length, width), BF),
            shape((width, width), BF),
        ),
        in_specs=[SCALAR, HBM, HBM] + [WHOLE] * 7,
        out_specs=(WHOLE,) * 8 + (HBM,),
        scratch_shapes=[
            pltpu.VMEM((2, width, 2 * width), BF),
            pltpu.VMEM((length, 3 * width), BF),
            pltpu.VMEM((HEADS, length, hd), BF),
            pltpu.SemaphoreType.DMA((3,)),
        ],
        compiler_params=params(),
        cost_estimate=cost(8 * length * width * width + 4 * length * length * width, 24e6),
        name="attention",
    )(side, own, other, normed, b_qv, bias, keep, x, mod, b_proj)


def fc2_tiles(width, half, tile):
    part = tile // 2
    per = width // part
    at = lambda q: (q % per, half // width + q // per)
    return [pl.BlockSpec((part, width), lambda t, k=k: at(2 * t + k)) for k in range(2)]


def mlp_half(normed_two_ref, b_ref, c0_ref, c1_ref, bf1_ref, hid_ref, slope_ref):
    act, slope = gelu_parts(mm(normed_two_ref[...], b_ref[...]) + bf1_ref[...])
    hid = act.astype(BF)
    hid_ref[...] = hid
    slope_ref[...] = slope
    return mm(hid, jnp.concatenate([c0_ref[...], c1_ref[...]], axis=0))


def mlp_first_kernel(normed_two_ref, b_ref, c0_ref, c1_ref, bf1_ref, hid_ref, slope_ref, part_ref):
    total = mlp_half(normed_two_ref, b_ref, c0_ref, c1_ref, bf1_ref, hid_ref, slope_ref)

    @pl.when(pl.program_id(0) == 0)
    def _():
        part_ref[...] = total

    @pl.when(pl.program_id(0) > 0)
    def _():
        part_ref[...] += total


def mlp_last_kernel(
    normed_two_ref,
    b_ref,
    c0_ref,
    c1_ref,
    bf1_ref,
    part_ref,
    bf2_ref,
    middle_ref,
    cot_ref,
    mod_ref,
    place_ref,
    present_ref,
    hid_ref,
    slope_ref,
    g_branch_ref,
    out_ref,
    sums_ref,
    acc_ref,
):
    t = pl.program_id(0)
    total = mlp_half(normed_two_ref, b_ref, c0_ref, c1_ref, bf1_ref, hid_ref, slope_ref)

    @pl.when(t == 0)
    def _():
        acc_ref[...] = part_ref[...] + total

    @pl.when(t > 0)
    def _():
        acc_ref[...] += total

    @pl.when(t == pl.num_programs(0) - 1)
    def _():
        branch = acc_ref[...] + bf2_ref[...]
        cot = cot_ref[...]
        gate = mod_ref[5:6, :]
        result = middle_ref[...] + gate * branch
        out = jnp.where(present_ref[...] > 0.0, result, 0.0).astype(BF)
        out_ref[...] = mm_tn(place_ref[...], out).astype(BF)
        g_branch = (cot * gate).astype(BF)
        g_branch_ref[...] = g_branch
        sums_ref[0:1, :] = jnp.sum(cot * branch, axis=0, keepdims=True)
        sums_ref[1:2, :] = jnp.sum(g_branch.astype(F32), axis=0, keepdims=True)


def mlp(normed_two, weights, bf1, last=None):
    length, width = normed_two.shape
    half = weights.shape[1] // 2
    tile = 2 * width // 3
    fixed = lambda a: pl.BlockSpec(a.shape, lambda t: (0, 0))
    cols = lambda r: pl.BlockSpec((r, tile), lambda t: (0, t))
    rows = fc2_tiles(width, half, tile)
    whole = lambda r: pl.BlockSpec((r, width), lambda t: (0, 0))
    more = last or ()
    outs = [shape((length, half), BF), shape((length, half), F32)]
    if last:
        outs += [shape((length, width), BF), shape((length, width), BF), shape((8, width), F32)]
    else:
        outs += [shape((length, width), F32)]
    return pl.pallas_call(
        mlp_last_kernel if last else mlp_first_kernel,
        grid=(half // tile,),
        out_shape=tuple(outs),
        in_specs=[fixed(normed_two), cols(width)] + rows + [cols(1)] + [fixed(a) for a in more],
        out_specs=tuple([cols(length), cols(length)] + [whole(o.shape[0]) for o in outs[2:]]),
        scratch_shapes=[pltpu.VMEM((length, width), F32)] if last else [],
        compiler_params=params(),
        cost_estimate=cost(4 * length * width * half, 16e6),
        name="mlp",
    )(normed_two, weights, weights, weights, bf1, *more)


def mlp_back_kernel(
    g_branch_ref,
    b0_ref,
    b1_ref,
    c00_ref,
    c01_ref,
    c10_ref,
    c11_ref,
    slope0_ref,
    slope1_ref,
    middle_ref,
    attended_ref,
    cot_ref,
    mod_ref,
    w_out_ref,
    *rest,
):
    pre0_ref, pre1_ref, bsum_ref, g_middle_ref, g_att_ref, g_mixed_ref, sums_ref, acc_ref = rest[-8:]
    t = pl.program_id(0)
    g_branch = g_branch_ref[...]
    total = None
    for i, (b_ref, c_refs, slope_ref, pre_ref) in enumerate(
        (
            (b0_ref, (c00_ref, c01_ref), slope0_ref, pre0_ref),
            (b1_ref, (c10_ref, c11_ref), slope1_ref, pre1_ref),
        )
    ):
        c = jnp.concatenate([ref[...] for ref in c_refs], axis=0)
        pre = (mm_nt(g_branch, c) * slope_ref[...]).astype(BF)
        pre_ref[...] = pre
        bsum_ref[i : i + 1, :] = jnp.sum(pre.astype(F32), axis=0, keepdims=True)
        part = mm_nt(pre, b_ref[...])
        total = part if total is None else total + part

    @pl.when(t == 0)
    def _():
        acc_ref[...] = total

    @pl.when(t > 0)
    def _():
        acc_ref[...] += total

    @pl.when(t == pl.num_programs(0) - 1)
    def _():
        g_n2 = acc_ref[...]
        n2, inv2 = normal(middle_ref[...])
        sums_ref[0:1, :] = jnp.sum(g_n2, axis=0, keepdims=True)
        sums_ref[1:2, :] = jnp.sum(g_n2 * n2, axis=0, keepdims=True)
        g_middle = cot_ref[...] + normal_back(g_n2 * (1.0 + mod_ref[4:5, :]), n2, inv2)
        g_middle_ref[...] = g_middle
        sums_ref[2:3, :] = jnp.sum(g_middle * attended_ref[...], axis=0, keepdims=True)
        g_att = (g_middle * mod_ref[2:3, :]).astype(BF)
        g_att_ref[...] = g_att
        sums_ref[3:4, :] = jnp.sum(g_att.astype(F32), axis=0, keepdims=True)
        g_mixed_ref[...] = mm_nt(g_att, w_out_ref[...]).astype(BF)


def mlp_back(g_branch, weights, slope0, slope1, middle, attended, cot, mod, w_out, after=()):
    length, width = middle.shape
    half = weights[0].shape[1] // 2
    tile = 2 * width // 3
    fixed = lambda a: pl.BlockSpec(a.shape, lambda t: (0, 0))
    cols = lambda r: pl.BlockSpec((r, tile), lambda t: (0, t))
    rows = fc2_tiles(width, half, tile)
    whole = lambda r: pl.BlockSpec((r, width), lambda t: (0, 0))
    return pl.pallas_call(
        mlp_back_kernel,
        grid=(half // tile,),
        out_shape=(
            shape((length, half), BF),
            shape((length, half), BF),
            shape((2, half), F32),
            shape((length, width), F32),
            shape((length, width), BF),
            shape((length, width), BF),
            shape((8, width), F32),
        ),
        in_specs=[
            fixed(g_branch),
            cols(width),
            cols(width),
            *rows,
            *rows,
            cols(length),
            cols(length),
            fixed(middle),
            fixed(attended),
            fixed(cot),
            fixed(mod),
            fixed(w_out),
        ]
        + [HBM] * len(after),
        out_specs=(
            cols(length),
            cols(length),
            cols(2),
            whole(length),
            whole(length),
            whole(length),
            whole(8),
        ),
        scratch_shapes=[pltpu.VMEM((length, width), F32)],
        compiler_params=params(),
        cost_estimate=cost(8 * length * width * half, 32e6),
        name="mlp_back",
    )(
        g_branch,
        *weights,
        weights[0],
        weights[0],
        weights[1],
        weights[1],
        slope0,
        slope1,
        middle,
        attended,
        cot,
        mod,
        w_out,
        *after,
    )


def heads_back(q_ref, k_ref, v_ref, strip_ref, keep, gm_ref, dq_ref, dk_ref, dv_ref, sums_ref, start):
    scale = q_ref.shape[2] ** -0.5
    length = q_ref.shape[1]

    def head(i, carry):
        h = start + i
        q, k, v, gm = q_ref[h], k_ref[h], v_ref[h], gm_ref[i]
        sc = mm_nt(q, k) * scale + bias_of(strip_ref[h])
        sc = jnp.where(keep, sc, -1e30)
        ex = jnp.exp(sc - jnp.max(sc, axis=-1, keepdims=True))
        soft = ex / jnp.sum(ex, axis=-1, keepdims=True)
        dv_ref[i] = mm_tn(soft.astype(BF), gm).astype(BF)
        dp = mm_nt(gm, v)
        ds = (soft * (dp - jnp.sum(dp * soft, axis=-1, keepdims=True))).astype(BF)
        dq_ref[i] = (mm(ds, k) * scale).astype(BF)
        dk_ref[i] = (mm_tn(ds, q) * scale).astype(BF)
        dsf = ds.astype(F32)
        total = jnp.zeros((GRID, sums_ref.shape[2]), F32)
        blank = jnp.zeros((GRID, sums_ref.shape[2] - length), F32)
        for y in range(GRID):
            rows = jnp.concatenate([dsf[y * GRID : (y + 1) * GRID, :], blank], axis=1)
            by = (GRID - 1 - y) * GRID
            total = total + (pltpu.roll(rows, by, 1) if by else rows)
        sums_ref[i] = total
        return carry

    lax.fori_loop(0, dq_ref.shape[0], head, 0, unroll=2)


def first_heads_kernel(qh_ref, kh_ref, vh_ref, strip_ref, keep_ref, g_mixed_ref, *rest):
    dq_ref, dk_ref, dv_ref, sums_ref, gm_ref = rest[-5:]
    hd = qh_ref.shape[2]
    for i in range(HEADS // 2):
        gm_ref[i] = g_mixed_ref[:, i * hd : (i + 1) * hd]
    heads_back(
        qh_ref, kh_ref, vh_ref, strip_ref, keep_ref[...] > 0.0, gm_ref, dq_ref, dk_ref, dv_ref, sums_ref, 0
    )


def first_heads(qh, kh, vh, strip, keep, g_mixed, after=()):
    heads, length, hd = qh.shape
    some = shape((heads // 2, length, hd), BF)
    return pl.pallas_call(
        first_heads_kernel,
        out_shape=(some, some, some, shape((heads // 2,) + strip.shape[1:], F32)),
        in_specs=[WHOLE] * 6 + [HBM] * len(after),
        out_specs=(WHOLE,) * 4,
        scratch_shapes=[pltpu.VMEM((heads // 2, length, hd), BF)],
        compiler_params=params(),
        cost_estimate=cost(5 * length * length * heads * hd, 16e6),
        name="first_heads",
    )(qh, kh, vh, strip, keep, g_mixed, *after)


def last_heads_kernel(
    side_ref,
    qh_ref,
    kh_ref,
    vh_ref,
    strip_ref,
    keep_ref,
    g_mixed_ref,
    g_att_ref,
    fq_ref,
    fk_ref,
    fv_ref,
    fsum_ref,
    *rest,
):
    mine_ref, top_ref, low_ref, lo_ref, hi_ref, sums_ref, both_ref, gm_ref, dq_ref, dk_ref, dv_ref, strips_ref = rest[-12:]
    theirs_ref = both_ref
    width = g_mixed_ref.shape[1]
    hd = qh_ref.shape[2]
    half = HEADS // 2
    for i in range(half):
        gm_ref[i] = g_mixed_ref[:, (half + i) * hd : (half + i + 1) * hd]
    heads_back(
        qh_ref, kh_ref, vh_ref, strip_ref, keep_ref[...] > 0.0, gm_ref, dq_ref, dk_ref, dv_ref, strips_ref, half
    )
    for s, (qk_at, v_at) in enumerate(((mine_ref, theirs_ref), (theirs_ref, mine_ref))):

        @pl.when(side_ref[0] == s)
        def _():
            for h in range(HEADS):
                q, k, v = (fq_ref, fk_ref, fv_ref) if h < half else (dq_ref, dk_ref, dv_ref)
                i = h % half
                qk_at[:, h * hd : (h + 1) * hd] = q[i]
                qk_at[:, width + h * hd : width + (h + 1) * hd] = k[i]
                v_at[:, h * hd : (h + 1) * hd] = v[i]
            v_at[:, width:] = g_att_ref[...]
            sums_ref[0:1, :] = jnp.sum(qk_at[:, 0:width].astype(F32), axis=0, keepdims=True)
            sums_ref[1:2, :] = jnp.sum(v_at[:, 0:width].astype(F32), axis=0, keepdims=True)

    length = both_ref.shape[0]
    top_ref[...] = both_ref[0 : length // 2, :]
    low_ref[...] = both_ref[length // 2 :, :]
    lanes = lo_ref.shape[1]
    for part, ref in enumerate((fsum_ref, strips_ref)):
        lo = jnp.zeros((half, lanes), F32)
        hi = jnp.zeros((half, lanes), F32)
        j = lax.broadcasted_iota(jnp.int32, lo.shape, 1) % GRID
        for i in range(GRID):
            k = GRID - 1 - i
            row = ref[:, i, :]
            a = jnp.where(j < GRID - k, row, 0.0)
            lo = lo + (pltpu.roll(a, k, 1) if k else a)
            if k:
                hi = hi + pltpu.roll(jnp.where(j < GRID - k, 0.0, row), lanes - (GRID - k), 1)
        lo_ref[part * half : (part + 1) * half, :] = lo
        hi_ref[part * half : (part + 1) * half, :] = hi


def last_heads(side, qh, kh, vh, strip, keep, g_mixed, g_att, firsts, after=()):
    length, width = g_mixed.shape
    heads, _, hd = qh.shape
    per_head = pltpu.VMEM((heads // 2, length, hd), BF)
    window = shape((heads, strip.shape[2]), F32)
    return pl.pallas_call(
        last_heads_kernel,
        out_shape=(
            shape((length, 2 * width), BF),
            shape((length // 2, 2 * width), BF),
            shape((length // 2, 2 * width), BF),
            window,
            window,
            shape((8, width), F32),
        ),
        in_specs=[SCALAR] + [WHOLE] * 11 + [HBM] * len(after),
        out_specs=(WHOLE,) * 6,
        scratch_shapes=[pltpu.VMEM((length, 2 * width), BF)]
        + [per_head] * 4 + [pltpu.VMEM((heads // 2,) + strip.shape[1:], F32)],
        compiler_params=params(),
        cost_estimate=cost(5 * length * length * width, 16e6),
        name="last_heads",
    )(side, qh, kh, vh, strip, keep, g_mixed, g_att, *firsts, *after)


def tokens_back_kernel(
    side_ref,
    own_ref,
    other_ref,
    mine_ref,
    top_ref,
    low_ref,
    x_ref,
    g_middle_ref,
    mod_ref,
    place_ref,
    *rest,
):
    out_ref, sums_ref, w_ref, acc_ref, qk_ref, v_ref, sem = rest[-7:]
    length, width = x_ref.shape
    wait = fetch_halves(side_ref, own_ref, other_ref, w_ref, sem)
    half = length // 2

    @pl.when(side_ref[0] == 0)
    def _():
        qk_ref[...] = mine_ref[...]
        v_ref[0:half, :] = top_ref[:, 0:width]
        v_ref[half:, :] = low_ref[:, 0:width]

    @pl.when(side_ref[0] == 1)
    def _():
        qk_ref[0:half, :] = top_ref[...]
        qk_ref[half:, :] = low_ref[...]
        v_ref[...] = mine_ref[:, 0:width]

    wait(0)
    acc_ref[...] = mm_nt(qk_ref[...], w_ref[0])
    wait(1)
    g_n1 = acc_ref[...] + mm_nt(v_ref[...], w_ref[1, :, 0:width])
    n1, inv1 = normal(x_ref[...])
    sums_ref[0:1, :] = jnp.sum(g_n1, axis=0, keepdims=True)
    sums_ref[1:2, :] = jnp.sum(g_n1 * n1, axis=0, keepdims=True)
    g_x = g_middle_ref[...] + normal_back(g_n1 * (1.0 + mod_ref[1:2, :]), n1, inv1)
    out_ref[...] = mm_tn(place_ref[...], g_x.astype(BF)).astype(BF)


def tokens_back(side, own, other, mine, theirs, x, g_middle, mod, place, after=()):
    length, width = x.shape
    return pl.pallas_call(
        tokens_back_kernel,
        out_shape=(shape((length, width), BF), shape((8, width), F32)),
        in_specs=[SCALAR, HBM, HBM] + [WHOLE] * 7 + [HBM] * len(after),
        out_specs=(WHOLE,) * 2,
        scratch_shapes=[
            pltpu.VMEM((2, width, 2 * width), BF),
            pltpu.VMEM((length, width), F32),
            pltpu.VMEM((length, 2 * width), BF),
            pltpu.VMEM((length, width), BF),
            pltpu.SemaphoreType.DMA((2,)),
        ],
        compiler_params=params(),
        cost_estimate=cost(6 * length * width * width, 16e6),
        name="tokens_back",
    )(side, own, other, mine, *theirs, x, g_middle, mod, place, *after)


def local(
    n,
    tokens,
    condition,
    kept_index,
    kept_count,
    cotangent,
    w_ada,
    w_qkv,
    w_proj,
    w_fc1,
    w_fc2,
    b_ada,
    b_qv,
    b_proj,
    b_fc1,
    b_fc2,
    rel_table,
):
    side = lax.axis_index("stream")
    chip = lax.axis_index("dp")
    length, width = tokens.shape[2], tokens.shape[3]
    ff = w_fc1.shape[1]
    rows = width // n
    cut = ff // (2 * n)
    first = side == 0
    side_word = side.astype(jnp.int32).reshape(1)
    chip_word = chip.astype(jnp.int32).reshape(1)

    order_first, order_parts = orders_out(n)
    firsts = tuple(part[-1] for part in order_parts)

    ordinal = jnp.arange(length, dtype=jnp.int32)
    count = jnp.where(first, length, kept_count[0])
    position = jnp.where(first, ordinal, kept_index[0])
    place = ((position[None, :] == ordinal[:, None]) & (ordinal[None, :] < count)).astype(BF)
    present = jnp.sum(place.astype(F32), axis=1)
    keep = present.reshape(1, length)
    present = present.reshape(length, 1)
    x = mm(place, tokens[0, 0])
    cot = mm(place, cotangent[0, 0])
    bias = bias_strip(rel_table)

    cond = condition[0, 0]
    sig = jax.nn.sigmoid(cond)
    cond_act = (cond * sig).astype(BF)
    shard_a = attn_shard(side_word, w_qkv, w_proj)
    all_a = Gathering(chip_word, shard_a, n)
    acts = trade(hold(jnp.broadcast_to(cond_act[None], (n, width)), shard_a))
    acts_part = lax.dynamic_slice_in_dim(acts, chip * rows, rows, axis=1)
    shard_bc = mlp_shard(n, side_word, w_fc1, w_fc2, after=(shard_a,))
    last = all_a.step(shard_bc, bias, x, cot, acts_part)
    all_bc = Gathering(chip_word, hold(shard_bc, *last), n)
    for _ in range(len(order_parts[0]) - 2 + len(order_first) - 1):
        last = all_a.step(*last)
    while all_bc.turn < all_bc.cut_at:
        last = all_bc.step(*last)
    acts_twin = swap_stream(acts_part)
    if {p[-1] for p in order_parts} == {p[0] for p in order_parts}:
        last, result_a, on_bc = merge_steps(all_a, all_bc, acts_twin)
        last = on_bc()
    else:
        last = all_a.step(*last, acts_twin)
        result_a = all_a.result
        last = all_bc.step(*last)
    a_own = result_a(*last)
    a_other = swap_stream(a_own)
    mod_part = trade(hold(mm(acts_part, w_ada), a_own))
    last = (mod_part,)
    while not all_bc.done():
        last = all_bc.step(*last)
    modulation = jnp.sum(mod_part, axis=0) + b_ada
    mod = modulation.reshape(6, width)
    n1, _ = normal(x)
    normed = (n1 * (1.0 + mod[1]) + mod[0]).astype(BF)
    qh, kh, vh, lhs_mine, lhs_theirs, attended, middle, normed_two, w_out = attention(
        side_word,
        a_own,
        a_other,
        normed,
        b_qv.reshape(1, -1),
        bias,
        keep,
        x,
        mod,
        b_proj.reshape(1, -1),
    )

    bf1 = jnp.transpose(b_fc1.reshape(n, 2, 2, cut // 2), (1, 2, 0, 3)).reshape(2, 1, ff // 2)
    bf1_own, bf1_other = jnp.where(first, bf1[0], bf1[1]), jnp.where(first, bf1[1], bf1[0])
    bf2 = b_fc2.reshape(1, -1)
    bc_own = all_bc.result(normed_two, bf1_own, bf1_other, bf2, present, place)
    bc_other = swap_stream(bc_own)
    lhs_twin = swap_stream(lhs_theirs)
    n2_twin = swap_stream(normed_two)
    hid0, slope0, part = mlp(normed_two, bc_own, bf1_own)
    hid1, slope1, g_branch, out_tokens, sums_a = mlp(
        normed_two,
        bc_other,
        bf1_other,
        (part, bf2, middle, cot, mod, place, present),
    )

    parts_c = product(
        chip_word, hid0, swap_stream(hid1), g_branch, swap_stream(g_branch), width, n, firsts
    )
    sum_c = Reduction(chip_word, parts_c, n)
    pre0, pre1, pre_sum, g_middle, g_att, g_mixed, sums_b = mlp_back(
        g_branch,
        (bc_own, bc_other),
        slope0,
        slope1,
        middle,
        attended,
        cot,
        mod,
        w_out,
        after=(parts_c[0][0], lhs_twin, n2_twin),
    )
    kept = step([sum_c], g_mixed)
    pre_twin = swap_stream(pre1)
    one = first_heads(qh, kh, vh, bias, keep, g_mixed, after=kept + (pre_twin,))
    kept = step([sum_c], one[0])
    kept = step([sum_c], *kept)
    parts_b = product(
        chip_word,
        normed_two,
        n2_twin,
        pre0,
        pre_twin,
        width,
        n,
        firsts,
        after=kept,
    )
    sum_b = Reduction(chip_word, parts_b, n)
    g_mine, top, low, lo, hi, sums_c = last_heads(
        side_word, qh, kh, vh, bias, keep, g_mixed, g_att, one, after=(parts_b[0][0],)
    )
    g_theirs = (top, low)
    g_twin = (swap_stream(top), swap_stream(low))
    while not sum_c.done():
        step([sum_c])
    d_c = sum_c.result(g_mine)
    kept = step([sum_b], g_mine) + g_twin
    grad_tokens, sums_d = tokens_back(
        side_word, a_own, a_other, g_mine, g_theirs, x, g_middle, mod, place, after=kept
    )
    sums_a, sums_b, sums_c, lo, hi, pre_sum = hold((sums_a, sums_b, sums_c, lo, hi, pre_sum), sums_d)
    g_mod = jnp.concatenate([sums_d[0], sums_d[1], sums_b[2], sums_b[0], sums_b[1], sums_a[0]])
    g_mod = g_mod.astype(BF).astype(F32).reshape(-1, 128)
    pre_sum = jnp.where(first, pre_sum, jnp.concatenate([pre_sum[1:], pre_sum[:1]]))
    pre_sum = jnp.transpose(pre_sum.reshape(2, 2, n, cut // 2), (2, 0, 1, 3))
    smalls = [
        sums_c[0],
        sums_c[1],
        sums_b[3],
        pre_sum.reshape(-1),
        sums_a[1],
        table_of(lo, hi).reshape(-1),
    ]
    sizes = [t.shape[0] for t in smalls]
    packed = jnp.concatenate(smalls)
    packed = jnp.pad(packed, (0, 128 * SUM_ROWS - packed.shape[0])).reshape(-1, 128)
    mod_rows = g_mod.shape[0]
    pad = -mod_rows % 8
    told = jnp.concatenate([packed, jnp.pad(g_mod, ((0, pad), (0, 0)))], axis=0)
    group = told.shape[0] - SUM_ROWS
    bits = all_bits(n)[::-1]
    kept = (d_c,)
    for b in bits[:2]:
        came = swap(told, b, n)
        if not sum_b.done():
            kept = step([sum_b], told, *kept)
        told = meet(chip_word, told, came, b, group, after=kept)
    while not sum_b.done():
        kept = step([sum_b], *kept)
    came = swap(told, bits[2], n)
    parts_a = product(
        chip_word, lhs_mine, lhs_twin, g_mine, g_twin, width, n, firsts, after=(told,) + kept
    )
    sum_a = Reduction(chip_word, parts_a, n)
    told = meet(chip_word, told, came, bits[2], group, after=(parts_a[0][0],))
    grad_w_fc2 = fc2_rows(side_word, d_c, swap_stream(d_c))
    d_b = sum_b.result(parts_a[0][0])
    grad_w_fc1 = fc1_rows(n, side_word, d_b, swap_stream(d_b))
    for b in bits[3:]:
        told = meet(chip_word, told, swap(told, b, n), b, group)
    kept = step([sum_a], told, grad_w_fc2, grad_w_fc1)
    twin = swap_stream(told)

    def mods_of(t):
        return t[SUM_ROWS:].reshape(n, -1, 128)[:, :mod_rows].reshape(n, -1)

    g_own, g_twin = mods_of(told), mods_of(twin)
    grad_w_ada = mm_tn(acts_part, g_own.astype(BF)) + mm_tn(acts_twin, g_twin.astype(BF))
    grad_b_ada = jnp.sum(g_own, axis=0) + jnp.sum(g_twin, axis=0)
    kept = step([sum_a], *kept, grad_w_ada, grad_b_ada)
    while not sum_a.done():
        kept = step([sum_a], *kept)
    g_acts = trade(hold(mm_nt(g_own.astype(BF), w_ada), *kept)).reshape(width)
    grad_condition = g_acts * sig * (1.0 + cond * (1.0 - sig))
    packed = (told[:SUM_ROWS] + twin[:SUM_ROWS]).reshape(-1)
    parts, at = [], 0
    for size in sizes:
        parts.append(packed[at : at + size])
        at += size

    d_a = sum_a.result(g_acts, *parts)
    grad_w_qkv, grad_w_proj = attn_rows(side_word, d_a, swap_stream(d_a))
    return (
        out_tokens[None, None],
        grad_tokens[None, None],
        grad_condition[None, None],
        grad_w_ada,
        grad_w_qkv,
        grad_w_proj,
        grad_w_fc1,
        grad_w_fc2,
        grad_b_ada,
        jnp.concatenate(parts[:2]),
        parts[2],
        parts[3],
        parts[4],
        parts[5].reshape(rel_table.shape),
    )


def solution(mesh):
    n = mesh.shape["dp"]

    def body(*args):
        return local(n, *args)

    return jax.shard_map(
        body,
        mesh=mesh,
        in_specs=(
            P("stream", "dp", None, None),
            P("stream", "dp", None),
            P("dp", None),
            P("dp"),
            P("stream", "dp", None, None),
            P("dp", None),
            P("dp", None),
            P("dp", None),
            P("dp", None),
            P("dp", None),
            P(),
            P(),
            P(),
            P(),
            P(),
            P(),
        ),
        out_specs=(
            P("stream", "dp", None, None),
            P("stream", "dp", None, None),
            P("stream", "dp", None),
            P("dp", None),
            P("dp", None),
            P("dp", None),
            P("dp", None),
            P("dp", None),
            P(),
            P(),
            P(),
            P(),
            P(),
            P(),
        ),
        check_vma=False,
    )
```

profile of v0, /device:TPU:0, one launch (start us, length us, event | category | flops | bytes accessed | tf_op | source)
XLA Modules:
  0.0 497.4 jit_solution(8329709987721953294)
XLA Ops:
  0.7 1.9 attn_shard.1.rest_0_.refs_1_.refs_0_
  2.6 4.0 collective-permute-start
  10.7 4.8 all-to-all-start
  21.6 2.5 mlp_shard.1.refs_2_.refs_0_
  24.1 2.0 bias_strip.1.refs_3_.strip_ref
  27.6 1.9 join.3
  29.6 1.9 collective-permute-start.1
  34.4 2.4 collective-permute-start.7
  39.8 2.5 join.4
  42.4 1.8 collective-permute-start.4
  44.6 2.7 collective-permute-start.6
  48.5 16.3 %collective-permute-done.7.refs_7_ = bf16[1,72,4608]{2,1,0:T(8,128)(2,1)S(1)} collective-permute-done((bf16[1,72,4608]{2,1,0:T(8,128)(2,1)}, bf16[1,72,4608]{2,1,0:T(8,128)(2,1)S(1)}, u32[]{:S(2)}, u32[]{:S(2)}) %collective-permute-start.7) | collective-permute-done | bytes 663584 | tf_op jit(solution)/shard_map/ppermute | solution.py:18
  66.9 4.3 merge.1
  73.0 27.8 %collective-permute-done.10.refs_5_.refs_3_ = bf16[12,72,768]{2,1,0:T(8,128)(2,1)S(1)} collective-permute-done((bf16[12,72,768]{2,1,0:T(8,128)(2,1)}, bf16[12,72,768]{2,1,0:T(8,128)(2,1)S(1)}, u32[]{:S(2)}, u32[]{:S(2)}) %collective-permute-start.10) | collective-permute-done | bytes 1327136 | tf_op jit(solution)/shard_map/ppermute | solution.py:18
  103.4 4.9 cross.1
  108.3 6.2 %assemble.2 = bf16[16,72,2304]{2,1,0:T(8,128)(2,1)} custom-call(s32[1]{0:T(128)} %bitcast.1.chip_ref, bf16[12,72,768]{2,1,0:T(8,128)(2,1)} %get-tuple-element.139.refs_2_.refs_0_, bf16[12,72,768]{2,1,0:T(8,128)(2,1)} %copy-done.4, bf16[12,72,768]{2,1,0:T(8,128)(2,1)} %get-tuple-element.140.refs_4_.refs_2_, bf16[12,72,768]{2,1,0:T(8,128)(2,1)} %copy-done.2, ...), custom_call_target="tpu_custom_call" | custom-call | tf_op jit(solution)/shard_map/assemble/pallas_call | solution.py:297
  117.8 2.3 copy.71
  120.1 5.6 %all-to-all-start.1 = ((f32[16,1,6912]{2,1,0:T(1,128)}), f32[16,1,6912]{2,1,0:T(1,128)S(1)}, u32[]{:S(2)}, u32[]{:S(2)}) async-start(f32[16,1,6912]{2,1,0:T(1,128)} %copy.71), calls=%async_computation.1 | async-start | bytes 884736 | tf_op jit(solution)/shard_map/all_to_all | solution.py:45
  130.0 15.8 %all-to-all-done.1 = f32[16,1,6912]{2,1,0:T(1,128)S(1)} async-done(((f32[16,1,6912]{2,1,0:T(1,128)}), f32[16,1,6912]{2,1,0:T(1,128)S(1)}, u32[]{:S(2)}, u32[]{:S(2)}) %all-to-all-start.1) | async-done | bytes 442400 | tf_op jit(solution)/shard_map/all_to_all | solution.py:45
  146.6 5.2 %join.5 = (bf16[8,72,1536]{2,1,0:T(8,128)(2,1)}, bf16[8,72,1536]{2,1,0:T(8,128)(2,1)}, bf16[8,72,1536]{2,1,0:T(8,128)(2,1)}) custom-call(s32[1]{0:T(128)} %bitcast.1.chip_ref, bf16[4,72,1536]{2,1,0:T(8,128)(2,1)} %get-tuple-element.142.refs_6_.refs_0_, bf16[4,72,1536]{2,1,0:T(8,128)(2,1)} %collective-permute-done.13.refs_1_, ...), custom_call_target="tpu_custom_call" | custom-call | tf_op jit(solution)/shard_map/join/pallas_call | solution.py:264
  157.9 27.5 %attention.1 = (bf16[16,256,72]{2,1,0:T(8,128)(2,1)}, bf16[16,256,72]{2,1,0:T(8,128)(2,1)}, bf16[16,256,72]{2,1,0:T(8,128)(2,1)}, bf16[256,2304]{1,0:T(8,128)(2,...) custom-call(s32[1]{0:T(128)} %bitcast.side_ref, ...), custom_call_target="tpu_custom_call" | custom-call | flops 3019898880 | bytes 24000000 | tf_op jit(solution)/shard_map/attention/pallas_call | solution.py:760
  185.5 6.3 %collective-permute-done.16.refs_1_ = bf16[8,72,1536]{2,1,0:T(8,128)(2,1)} collective-permute-done((bf16[8,72,1536]{2,1,0:T(8,128)(2,1)}, bf16[8,72,1536]{2,1,0:T(8,128)(2,1)}, u32[]{:S(2)}, u32[]{:S(2)}) %collective-permute-start.16) | collective-permute-done | bytes 1769504 | tf_op jit(solution)/shard_map/ppermute | solution.py:18
  192.8 8.7 %assemble.3 = bf16[16,72,4608]{2,1,0:T(8,128)(2,1)} custom-call(s32[1]{0:T(128)} %bitcast.1.chip_ref, bf16[8,72,1536]{2,1,0:T(8,128)(2,1)} %get-tuple-element.146.refs_0_, bf16[8,72,1536]{2,1,0:T(8,128)(2,1)} %collective-permute-done.16.refs_1_, bf16[8,72,1536]{2,1,0:T(8,128)(2,1)} %get-tuple-element.147.refs_2_, ...), custom_call_target="tpu_custom_call" | custom-call | tf_op jit(solution)/shard_map/assemble/pallas_call | solution.py:297
  201.6 9.9 %mlp.2 = (bf16[256,2304]{1,0:T(8,128)(2,1)}, f32[256,2304]{1,0:T(8,128)}, f32[256,1152]{1,0:T(8,128)}) custom-call(bf16[256,1152]{1,0:T(8,128)(2,1)} %get-tuple-element.145.refs_6_.normed_two_ref.l0_ref, bf16[1152,4608]{1,0:T(8,128)(2,1)} %bitcast.93, bf16[1152,4608]{1,0:T(8,128)(2,1)} %bitcast.94, bf16[1152,4608]{1,0:T(8,128)(2,1)} %bitcast.95, ...), custom_call_target="tpu_custom_call" | custom-call | flops 2717908992 | bytes 16000000 | tf_op jit(solution)/shard_map/mlp/pallas_call | solution.py:873
  211.5 6.7 %collective-permute-done.19.b_ref.c0_ref.c1_ref.b1_ref.c10_ref.c11_ref = bf16[1152,4608]{1,0:T(8,128)(2,1)} collective-permute-done((bf16[1152,4608]{1,0:T(8,128)(2,1)}, bf16[1152,4608]{1,0:T(8,128)(2,1)}, u32[]{:S(2)}, u32[]{:S(2)}) %collective-permute-start.19) | collective-permute-done | bytes 10616864 | tf_op jit(solution)/shard_map/ppermute | solution.py:22
  218.2 11.7 %mlp.3 = (bf16[256,2304]{1,0:T(8,128)(2,1)}, f32[256,2304]{1,0:T(8,128)}, bf16[256,1152]{1,0:T(8,128)(2,1)}, bf16[256,1152]{1,0:T(8,128)(2,1)}, f32[8,1152]{1,0:T(8,128)}) custom-call(bf16[256,1152]{1,0:T(8,128)(2,1)} %get-tuple-element.145.refs_6_.normed_two_ref.l0_ref, ...), custom_call_target="tpu_custom_call" | custom-call | flops 2717908992 | bytes 16000000 | tf_op jit(solution)/shard_map/mlp/pallas_call | solution.py:873
  231.1 5.4 %collective-permute-done.21.rest_1_ = bf16[256,1152]{1,0:T(8,128)(2,1)S(1)} collective-permute-done((bf16[256,1152]{1,0:T(8,128)(2,1)}, bf16[256,1152]{1,0:T(8,128)(2,1)S(1)}, u32[]{:S(2)}, u32[]{:S(2)}) %collective-permute-start.21) | collective-permute-done | bytes 589856 | tf_op jit(solution)/shard_map/ppermute | solution.py:22
  237.7 10.5 %product.3 = (bf16[8,72,768]{2,1,0:T(8,128)(2,1)}, bf16[8,72,768]{2,1,0:T(8,128)(2,1)}, bf16[8,72,768]{2,1,0:T(8,128)(2,1)}, bf16[8,72,768]{2,1,0:T(8,128)(2,1)}...) custom-call(s32[1]{0:T(128)} %bitcast.1.chip_ref, bf16[256,2304]{1,0:T(8,128)(2,1)} %get-tuple-element.160.l0_ref, ...), custom_call_target="tpu_custom_call" | custom-call | flops 2717908992 | bytes 12000000 | tf_op jit(solution)/shard_map/product/pallas_call | solution.py:465
  252.1 19.5 %mlp_back.1 = (bf16[256,2304]{1,0:T(8,128)(2,1)}, bf16[256,2304]{1,0:T(8,128)(2,1)}, f32[2,2304]{1,0:T(2,128)}, f32[256,1152]{1,0:T(8,128)}, bf16[256,1152]{1,0:...) custom-call(bf16[256,1152]{1,0:T(8,128)(2,1)} %get-tuple-element.155.rest_0_.g_branch_ref, ...), custom_call_target="tpu_custom_call" | custom-call | flops 5435817984 | bytes 32000000 | tf_op jit(solution)/shard_map/mlp_back/pallas_call | solution.py:951
  273.2 4.5 split.9
  282.1 9.8 %first_heads.1 = (bf16[8,256,72]{2,1,0:T(8,128)(2,1)}, bf16[8,256,72]{2,1,0:T(8,128)(2,1)}, bf16[8,256,72]{2,1,0:T(8,128)(2,1)}, f32[8,16,512]{2,1,0:T(8,128)}) custom-call(bf16[16,256,72]{2,1,0:T(8,128)(2,1)} %get-tuple-element.152.qh_ref, bf16[16,256,72]{2,1,0:T(8,128)(2,1)} %get-tuple-element.153.kh_ref, bf16[16,256,72]{2,1,0:T(8,128)(2,1)} %get-tuple-element.154.vh_ref, ...), custom_call_target="tpu_custom_call" | custom-call | flops 377487360 | bytes 16000000 | tf_op jit(solution)/shard_map/first_heads/pallas_call | solution.py:1051
  293.0 3.0 split.10
  298.7 4.5 collective-permute-done.31.refs_1_
  304.7 2.4 split.11
  307.0 2.4 collective-permute-start.43
  309.4 9.9 %product.4 = (bf16[8,72,768]{2,1,0:T(8,128)(2,1)}, bf16[8,72,768]{2,1,0:T(8,128)(2,1)}, bf16[8,72,768]{2,1,0:T(8,128)(2,1)}, bf16[8,72,768]{2,1,0:T(8,128)(2,1)}...) custom-call(s32[1]{0:T(128)} %bitcast.1.chip_ref, ...), custom_call_target="tpu_custom_call" | custom-call | flops 2717908992 | bytes 12000000 | tf_op jit(solution)/shard_map/product/pallas_call | solution.py:465
  322.1 12.7 %last_heads.1 = (bf16[256,2304]{1,0:T(8,128)(2,1)}, bf16[128,2304]{1,0:T(8,128)(2,1)}, bf16[128,2304]{1,0:T(8,128)(2,1)}, f32[16,512]{1,0:T(8,128)}, f32[16,512]{1,0:T(8,128)}, /*index=5*/f32[8,1152]{1,0:T(8,128)}) custom-call(s32[1]{0:T(128)} %bitcast.side_ref, bf16[16,256,72]{2,1,0:T(8,128)(2,1)} %get-tuple-element.152.qh_ref, ...), custom_call_target="tpu_custom_call" | custom-call | flops 377487360 | bytes 16000000 | tf_op jit(solution)/shard_map/last_heads/pallas_call | solution.py:1126
  335.5 2.0 finish.3.refs_7_.own_ref
  340.1 2.2 collective-permute-done.36.refs_5_
  342.3 4.5 split.12
  346.8 9.6 %tokens_back.1 = (bf16[256,1152]{1,0:T(8,128)(2,1)}, f32[8,1152]{1,0:T(8,128)}) custom-call(s32[1]{0:T(128)} %bitcast.side_ref, bf16[1152,2304]{1,0:T(8,128)(2,1)} %bitcast.102, bf16[1152,2304]{1,0:T(8,128)(2,1)} %collective-permute-done.12.other_ref, bf16[256,2304]{1,0:T(8,128)(2,1)} %get-tuple-element.191.refs_6_.mine_ref.rest_0_, ...), custom_call_target="tpu_custom_call" | custom-call | flops 2038431744 | bytes 16000000 | tf_op jit(solution)/shard_map/tokens_back/pallas_call | solution.py:1189
  366.2 3.0 collective-permute-start.39
  369.2 5.5 %collective-permute-done.40.refs_1_ = bf16[4,72,768]{2,1,0:T(8,128)(2,1)S(1)} collective-permute-done((bf16[4,72,768]{2,1,0:T(8,128)(2,1)}, bf16[4,72,768]{2,1,0:T(8,128)(2,1)S(1)}, u32[]{:S(2)}, u32[]{:S(2)}) %collective-permute-start.40) | collective-permute-done | bytes 442400 | tf_op jit(solution)/shard_map/ppermute | solution.py:18
  374.7 3.6 collective-permute-done.41.refs_3_
  379.8 3.0 split.13
  387.8 2.0 collective-permute-start.44
  391.2 2.4 split.14
  397.4 4.2 collective-permute-start.54
  401.7 11.2 %product.5 = (bf16[8,72,768]{2,1,0:T(8,128)(2,1)}, bf16[8,72,768]{2,1,0:T(8,128)(2,1)}, bf16[8,72,768]{2,1,0:T(8,128)(2,1)}, bf16[8,72,768]{2,1,0:T(8,128)(2,1)}...) custom-call(s32[1]{0:T(128)} %bitcast.1.chip_ref, bf16[256,2304]{1,0:T(8,128)(2,1)} %get-tuple-element.228.l0_ref, ...), custom_call_target="tpu_custom_call" | custom-call | flops 2717908992 | bytes 12000000 | tf_op jit(solution)/shard_map/product/pallas_call | solution.py:465
  413.6 1.8 meet.6.v_ref
  418.8 2.4 fc2_rows.1.refs_7_
  421.9 2.0 finish.4.own_ref
  423.9 2.4 collective-permute-done.49.r_ref
  427.1 1.9 meet.7.refs_6_
  432.4 3.5 fc1_rows.1.refs_8_
  435.9 6.2 %collective-permute-done.50.refs_1_ = bf16[8,72,768]{2,1,0:T(8,128)(2,1)S(1)} collective-permute-done((bf16[8,72,768]{2,1,0:T(8,128)(2,1)}, bf16[8,72,768]{2,1,0:T(8,128)(2,1)S(1)}, u32[]{:S(2)}, u32[]{:S(2)}) %collective-permute-start.50) | collective-permute-done | bytes 884768 | tf_op jit(solution)/shard_map/ppermute | solution.py:18
  443.6 4.6 split.15
  453.0 4.3 collective-permute-done.56.refs_1_
  458.6 3.0 split.16
  471.4 2.4 split.17
  475.0 4.6 all-to-all-start.2
  480.9 6.0 %all-to-all-done.2 = f32[16,1,72]{2,1,0:T(1,128)S(1)} async-done(((f32[16,1,72]{2,1,0:T(1,128)}), f32[16,1,72]{2,1,0:T(1,128)S(1)}, u32[]{:S(2)}, u32[]{:S(2)}) %all-to-all-start.2) | async-done | bytes 4640 | tf_op jit(solution)/shard_map/all_to_all | solution.py:45
  488.2 2.0 finish.5.own_ref
  494.7 2.4 attn_rows.1
  (367 shorter events, 120.0 us)
Async XLA Ops:
  2.6 24.3 %collective-permute-start = (bf16[1,72,2304]{2,1,0:T(8,128)(2,1)}, bf16[1,72,2304]{2,1,0:T(8,128)(2,1)S(1)}, u32[]{:S(2)}, u32[]{:S(2)}) collective-permute-start(bf16[1,72,2304]{2,1,0:T(8,128)(2,1)} %attn_shard.1.rest_0_.refs_1_.refs_0_), channel_id=1, source_target_pairs={{0,8},{1,9},{2,10},{3,11},{4,12},{5,13},{6,14},{7,15},{8,0},{9,1},... | collective-permute-start | bytes 995336 | tf_op jit(solution)/shard_map/ppermute | solution.py:18
  10.7 15.4 %all-to-all-start = ((bf16[16,2,576]{2,1,0:T(2,128)(2,1)}), bf16[16,2,576]{2,1,0:T(2,128)(2,1)S(1)}, u32[]{:S(2)}, u32[]{:S(2)}) async-start(bf16[16,2,576]{2,1,0:T(2,128)(2,1)} %reshape.270), calls=%async_computation | async-start | bytes 81920 | tf_op jit(solution)/shard_map/all_to_all | solution.py:45
  29.6 7.2 %collective-permute-start.1 = (bf16[2,72,768]{2,1,0:T(8,128)(2,1)}, bf16[2,72,768]{2,1,0:T(8,128)(2,1)S(1)}, u32[]{:S(2)}, u32[]{:S(2)}) collective-permute-start(bf16[2,72,768]{2,1,0:T(8,128)(2,1)} %get-tuple-element.133.refs_0_.refs_6_.refs_1_), channel_id=1, source_target_pairs={{0,4},{1,5},{2,6},{3,7},{4,0},{5,1},{6,2},{7,3},{8,12},{9,13},{10,... | collective-permute-start | bytes 663560 | tf_op jit(solution)/shard_map/ppermute | solution.py:18
  31.5 6.3 %collective-permute-start.2 = (bf16[2,72,768]{2,1,0:T(8,128)(2,1)}, bf16[2,72,768]{2,1,0:T(8,128)(2,1)S(1)}, u32[]{:S(2)}, u32[]{:S(2)}) collective-permute-start(bf16[2,72,768]{2,1,0:T(8,128)(2,1)} %get-tuple-element.134.refs_2_.refs_7_), channel_id=1, source_target_pairs={{0,1},{1,0},{2,3},{3,2},{4,5},{5,4},{6,7},{7,6},{8,9},{9,8},{10,11... | collective-permute-start | bytes 663560 | tf_op jit(solution)/shard_map/ppermute | solution.py:18
  33.0 6.1 %collective-permute-start.3 = (bf16[2,72,768]{2,1,0:T(8,128)(2,1)}, bf16[2,72,768]{2,1,0:T(8,128)(2,1)S(1)}, u32[]{:S(2)}, u32[]{:S(2)}) collective-permute-start(bf16[2,72,768]{2,1,0:T(8,128)(2,1)} %get-tuple-element.135.refs_4_.refs_8_.refs_3_), channel_id=1, source_target_pairs={{0,2},{1,3},{2,0},{3,1},{4,6},{5,7},{6,4},{7,5},{8,10},{9,11},{10,... | collective-permute-start | bytes 663560 | tf_op jit(solution)/shard_map/ppermute | solution.py:18
  34.4 30.4 %collective-permute-start.7 = (bf16[1,72,4608]{2,1,0:T(8,128)(2,1)}, bf16[1,72,4608]{2,1,0:T(8,128)(2,1)S(1)}, u32[]{:S(2)}, u32[]{:S(2)}) collective-permute-start(bf16[1,72,4608]{2,1,0:T(8,128)(2,1)} %hold.6.refs_6_), channel_id=1, source_target_pairs={{0,8},{1,9},{2,10},{3,11},{4,12},{5,13},{6,14},{7,15},{8,0},{9,1},... | collective-permute-start | bytes 1990664 | tf_op jit(solution)/shard_map/ppermute | solution.py:18
  42.4 22.5 %collective-permute-start.4 = (bf16[4,72,768]{2,1,0:T(8,128)(2,1)}, bf16[4,72,768]{2,1,0:T(8,128)(2,1)S(1)}, u32[]{:S(2)}, u32[]{:S(2)}) collective-permute-start(bf16[4,72,768]{2,1,0:T(8,128)(2,1)} %get-tuple-element.136.refs_0_), channel_id=1, source_target_pairs={{0,2},{1,3},{2,0},{3,1},{4,6},{5,7},{6,4},{7,5},{8,10},{9,11},{10,... | collective-permute-start | bytes 1327112 | tf_op jit(solution)/shard_map/ppermute | solution.py:18
  44.1 21.3 %collective-permute-start.5 = (bf16[4,72,768]{2,1,0:T(8,128)(2,1)}, bf16[4,72,768]{2,1,0:T(8,128)(2,1)S(1)}, u32[]{:S(2)}, u32[]{:S(2)}) collective-permute-start(bf16[4,72,768]{2,1,0:T(8,128)(2,1)} %get-tuple-element.137.refs_2_), channel_id=1, source_target_pairs={{0,4},{1,5},{2,6},{3,7},{4,0},{5,1},{6,2},{7,3},{8,12},{9,13},{10,... | collective-permute-start | bytes 1327112 | tf_op jit(solution)/shard_map/ppermute | solution.py:18
  44.6 20.8 %collective-permute-start.6 = (bf16[4,72,768]{2,1,0:T(8,128)(2,1)}, bf16[4,72,768]{2,1,0:T(8,128)(2,1)S(1)}, u32[]{:S(2)}, u32[]{:S(2)}) collective-permute-start(bf16[4,72,768]{2,1,0:T(8,128)(2,1)} %get-tuple-element.138.refs_4_), channel_id=1, source_target_pairs={{0,1},{1,0},{2,3},{3,2},{4,5},{5,4},{6,7},{7,6},{8,9},{9,8},{10,11... | collective-permute-start | bytes 1327112 | tf_op jit(solution)/shard_map/ppermute | solution.py:18
  71.2 29.5 %collective-permute-start.10 = (bf16[12,72,768]{2,1,0:T(8,128)(2,1)}, bf16[12,72,768]{2,1,0:T(8,128)(2,1)S(1)}, u32[]{:S(2)}, u32[]{:S(2)}) collective-permute-start(bf16[12,72,768]{2,1,0:T(8,128)(2,1)} %get-tuple-element.140.refs_4_.refs_2_), channel_id=1, source_target_pairs={{0,2},{1,3},{2,0},{3,1},{4,6},{5,7},{6,4},{7,5},{8,10},{9,11},{10,... | collective-permute-start | bytes 3981320 | tf_op jit(solution)/shard_map/ppermute | solution.py:18
  71.4 29.3 %collective-permute-start.11 = (bf16[12,72,768]{2,1,0:T(8,128)(2,1)}, bf16[12,72,768]{2,1,0:T(8,128)(2,1)S(1)}, u32[]{:S(2)}, u32[]{:S(2)}) collective-permute-start(bf16[12,72,768]{2,1,0:T(8,128)(2,1)} %get-tuple-element.141.refs_0_.refs_4_), channel_id=1, source_target_pairs={{0,4},{1,5},{2,6},{3,7},{4,0},{5,1},{6,2},{7,3},{8,12},{9,13},{10,... | collective-permute-start | bytes 3981320 | tf_op jit(solution)/shard_map/ppermute | solution.py:18
  71.4 29.4 %collective-permute-start.9 = (bf16[12,72,768]{2,1,0:T(8,128)(2,1)}, bf16[12,72,768]{2,1,0:T(8,128)(2,1)S(1)}, u32[]{:S(2)}, u32[]{:S(2)}) collective-permute-start(bf16[12,72,768]{2,1,0:T(8,128)(2,1)} %get-tuple-element.139.refs_2_.refs_0_), channel_id=1, source_target_pairs={{0,1},{1,0},{2,3},{3,2},{4,5},{5,4},{6,7},{7,6},{8,9},{9,8},{10,11... | collective-permute-start | bytes 3981320 | tf_op jit(solution)/shard_map/ppermute | solution.py:18
  114.5 43.5 %collective-permute-start.12 = (bf16[1152,2304]{1,0:T(8,128)(2,1)}, bf16[1152,2304]{1,0:T(8,128)(2,1)}, u32[]{:S(2)}, u32[]{:S(2)}) collective-permute-start(bf16[1152,2304]{1,0:T(8,128)(2,1)} %bitcast.99), channel_id=1, source_target_pairs={{0,16},{16,0},{1,17},{17,1},{2,18},{18,2},{3,19},{19,3},{4,20},{20... | collective-permute-start | bytes 15925256 | tf_op jit(solution)/shard_map/ppermute | solution.py:22
  114.5 32.1 %collective-permute-start.13 = (bf16[4,72,1536]{2,1,0:T(8,128)(2,1)S(1)}, bf16[4,72,1536]{2,1,0:T(8,128)(2,1)}, u32[]{:S(2)}, u32[]{:S(2)}) collective-permute-start(bf16[4,72,1536]{2,1,0:T(8,128)(2,1)S(1)} %copy-done.6), channel_id=1, source_target_pairs={{0,2},{1,3},{2,0},{3,1},{4,6},{5,7},{6,4},{7,5},{8,10},{9,11},{10,... | collective-permute-start | bytes 2654216 | tf_op jit(solution)/shard_map/ppermute | solution.py:18
  115.9 30.7 %collective-permute-start.14 = (bf16[4,72,1536]{2,1,0:T(8,128)(2,1)S(1)}, bf16[4,72,1536]{2,1,0:T(8,128)(2,1)}, u32[]{:S(2)}, u32[]{:S(2)}) collective-permute-start(bf16[4,72,1536]{2,1,0:T(8,128)(2,1)S(1)} %copy-done.7), channel_id=1, source_target_pairs={{0,4},{1,5},{2,6},{3,7},{4,0},{5,1},{6,2},{7,3},{8,12},{9,13},{10,... | collective-permute-start | bytes 2654216 | tf_op jit(solution)/shard_map/ppermute | solution.py:18
  116.5 30.0 %collective-permute-start.15 = (bf16[4,72,1536]{2,1,0:T(8,128)(2,1)}, bf16[4,72,1536]{2,1,0:T(8,128)(2,1)}, u32[]{:S(2)}, u32[]{:S(2)}) collective-permute-start(bf16[4,72,1536]{2,1,0:T(8,128)(2,1)} %get-tuple-element.144.refs_8_.refs_4_), channel_id=1, source_target_pairs={{0,1},{1,0},{2,3},{3,2},{4,5},{5,4},{6,7},{7,6},{8,9},{9,8},{10,11... | collective-permute-start | bytes 2654216 | tf_op jit(solution)/shard_map/ppermute | solution.py:18
  120.1 25.6 %all-to-all-start.1 = ((f32[16,1,6912]{2,1,0:T(1,128)}), f32[16,1,6912]{2,1,0:T(1,128)S(1)}, u32[]{:S(2)}, u32[]{:S(2)}) async-start(f32[16,1,6912]{2,1,0:T(1,128)} %copy.71), calls=%async_computation.1 | async-start | bytes 884736 | tf_op jit(solution)/shard_map/all_to_all | solution.py:45
  151.8 39.9 %collective-permute-start.16 = (bf16[8,72,1536]{2,1,0:T(8,128)(2,1)}, bf16[8,72,1536]{2,1,0:T(8,128)(2,1)}, u32[]{:S(2)}, u32[]{:S(2)}) collective-permute-start(bf16[8,72,1536]{2,1,0:T(8,128)(2,1)} %get-tuple-element.146.refs_0_), channel_id=1, source_target_pairs={{0,1},{1,0},{2,3},{3,2},{4,5},{5,4},{6,7},{7,6},{8,9},{9,8},{10,11... | collective-permute-start | bytes 5308424 | tf_op jit(solution)/shard_map/ppermute | solution.py:18
  152.1 39.9 %collective-permute-start.17 = (bf16[8,72,1536]{2,1,0:T(8,128)(2,1)}, bf16[8,72,1536]{2,1,0:T(8,128)(2,1)}, u32[]{:S(2)}, u32[]{:S(2)}) collective-permute-start(bf16[8,72,1536]{2,1,0:T(8,128)(2,1)} %get-tuple-element.147.refs_2_), channel_id=1, source_target_pairs={{0,2},{1,3},{2,0},{3,1},{4,6},{5,7},{6,4},{7,5},{8,10},{9,11},{10,... | collective-permute-start | bytes 5308424 | tf_op jit(solution)/shard_map/ppermute | solution.py:18
  153.7 39.2 %collective-permute-start.18 = (bf16[8,72,1536]{2,1,0:T(8,128)(2,1)}, bf16[8,72,1536]{2,1,0:T(8,128)(2,1)}, u32[]{:S(2)}, u32[]{:S(2)}) collective-permute-start(bf16[8,72,1536]{2,1,0:T(8,128)(2,1)} %get-tuple-element.148.refs_4_), channel_id=1, source_target_pairs={{0,4},{1,5},{2,6},{3,7},{4,0},{5,1},{6,2},{7,3},{8,12},{9,13},{10,... | collective-permute-start | bytes 5308424 | tf_op jit(solution)/shard_map/ppermute | solution.py:18
  201.6 16.7 %collective-permute-start.19 = (bf16[1152,4608]{1,0:T(8,128)(2,1)}, bf16[1152,4608]{1,0:T(8,128)(2,1)}, u32[]{:S(2)}, u32[]{:S(2)}) collective-permute-start(bf16[1152,4608]{1,0:T(8,128)(2,1)} %bitcast.92), channel_id=1, source_target_pairs={{0,16},{16,0},{1,17},{17,1},{2,18},{18,2},{3,19},{19,3},{4,20},{20... | collective-permute-start | bytes 31850504 | tf_op jit(solution)/shard_map/ppermute | solution.py:22
  230.0 6.5 %collective-permute-start.20 = (bf16[256,2304]{1,0:T(8,128)(2,1)}, bf16[256,2304]{1,0:T(8,128)(2,1)S(1)}, u32[]{:S(2)}, u32[]{:S(2)}) collective-permute-start(bf16[256,2304]{1,0:T(8,128)(2,1)} %get-tuple-element.161), channel_id=1, source_target_pairs={{0,16},{16,0},{1,17},{17,1},{2,18},{18,2},{3,19},{19,3},{4,20},{20... | collective-permute-start | bytes 3538952 | tf_op jit(solution)/shard_map/ppermute | solution.py:22
  230.2 20.7 %collective-permute-start.22 = (bf16[256,2304]{1,0:T(8,128)(2,1)}, bf16[256,2304]{1,0:T(8,128)(2,1)S(1)}, u32[]{:S(2)}, u32[]{:S(2)}) collective-permute-start(bf16[256,2304]{1,0:T(8,128)(2,1)} %get-tuple-element.163), channel_id=1, source_target_pairs={{0,16},{16,0},{1,17},{17,1},{2,18},{18,2},{3,19},{19,3},{4,20},{20... | collective-permute-start | bytes 3538952 | tf_op jit(solution)/shard_map/ppermute | solution.py:22
  230.7 20.2 %collective-permute-start.23 = (bf16[256,1152]{1,0:T(8,128)(2,1)S(1)}, bf16[256,1152]{1,0:T(8,128)(2,1)S(1)}, u32[]{:S(2)}, u32[]{:S(2)}) collective-permute-start(bf16[256,1152]{1,0:T(8,128)(2,1)S(1)} %copy-done.5), channel_id=1, source_target_pairs={{0,16},{16,0},{1,17},{17,1},{2,18},{18,2},{3,19},{19,3},{4,20},{20... | collective-permute-start | bytes 1769480 | tf_op jit(solution)/shard_map/ppermute | solution.py:22
  248.3 23.5 %collective-permute-start.24 = (bf16[8,72,768]{2,1,0:T(8,128)(2,1)}, bf16[8,72,768]{2,1,0:T(8,128)(2,1)S(1)}, u32[]{:S(2)}, u32[]{:S(2)}) collective-permute-start(bf16[8,72,768]{2,1,0:T(8,128)(2,1)} %get-tuple-element.166), channel_id=1, source_target_pairs={{0,1},{1,0},{2,3},{3,2},{4,5},{5,4},{6,7},{7,6},{8,9},{9,8},{10,11... | collective-permute-start | bytes 2654216 | tf_op jit(solution)/shard_map/ppermute | solution.py:18
  248.9 22.8 %collective-permute-start.25 = (bf16[8,72,768]{2,1,0:T(8,128)(2,1)}, bf16[8,72,768]{2,1,0:T(8,128)(2,1)S(1)}, u32[]{:S(2)}, u32[]{:S(2)}) collective-permute-start(bf16[8,72,768]{2,1,0:T(8,128)(2,1)} %get-tuple-element.168), channel_id=1, source_target_pairs={{0,2},{1,3},{2,0},{3,1},{4,6},{5,7},{6,4},{7,5},{8,10},{9,11},{10,... | collective-permute-start | bytes 2654216 | tf_op jit(solution)/shard_map/ppermute | solution.py:18
  250.7 21.4 %collective-permute-start.26 = (bf16[8,72,768]{2,1,0:T(8,128)(2,1)}, bf16[8,72,768]{2,1,0:T(8,128)(2,1)S(1)}, u32[]{:S(2)}, u32[]{:S(2)}) collective-permute-start(bf16[8,72,768]{2,1,0:T(8,128)(2,1)} %get-tuple-element.170), channel_id=1, source_target_pairs={{0,4},{1,5},{2,6},{3,7},{4,0},{5,1},{6,2},{7,3},{8,12},{9,13},{10,... | collective-permute-start | bytes 2654216 | tf_op jit(solution)/shard_map/ppermute | solution.py:18
  271.6 9.5 %collective-permute-start.27 = (bf16[256,2304]{1,0:T(8,128)(2,1)}, bf16[256,2304]{1,0:T(8,128)(2,1)S(1)}, u32[]{:S(2)}, u32[]{:S(2)}) collective-permute-start(bf16[256,2304]{1,0:T(8,128)(2,1)} %get-tuple-element.174), channel_id=1, source_target_pairs={{0,16},{16,0},{1,17},{17,1},{2,18},{18,2},{3,19},{19,3},{4,20},{20... | collective-permute-start | bytes 3538952 | tf_op jit(solution)/shard_map/ppermute | solution.py:22
  277.7 14.3 %collective-permute-start.28 = (bf16[4,72,768]{2,1,0:T(8,128)(2,1)}, bf16[4,72,768]{2,1,0:T(8,128)(2,1)S(1)}, u32[]{:S(2)}, u32[]{:S(2)}) collective-permute-start(bf16[4,72,768]{2,1,0:T(8,128)(2,1)} %get-tuple-element.180), channel_id=1, source_target_pairs={{0,2},{1,3},{2,0},{3,1},{4,6},{5,7},{6,4},{7,5},{8,10},{9,11},{10,... | collective-permute-start | bytes 1327112 | tf_op jit(solution)/shard_map/ppermute | solution.py:18
  278.2 13.8 %collective-permute-start.29 = (bf16[4,72,768]{2,1,0:T(8,128)(2,1)}, bf16[4,72,768]{2,1,0:T(8,128)(2,1)S(1)}, u32[]{:S(2)}, u32[]{:S(2)}) collective-permute-start(bf16[4,72,768]{2,1,0:T(8,128)(2,1)} %get-tuple-element.181), channel_id=1, source_target_pairs={{0,4},{1,5},{2,6},{3,7},{4,0},{5,1},{6,2},{7,3},{8,12},{9,13},{10,... | collective-permute-start | bytes 1327112 | tf_op jit(solution)/shard_map/ppermute | solution.py:18
  279.7 12.3 %collective-permute-start.30 = (bf16[4,72,768]{2,1,0:T(8,128)(2,1)}, bf16[4,72,768]{2,1,0:T(8,128)(2,1)S(1)}, u32[]{:S(2)}, u32[]{:S(2)}) collective-permute-start(bf16[4,72,768]{2,1,0:T(8,128)(2,1)} %get-tuple-element.182), channel_id=1, source_target_pairs={{0,1},{1,0},{2,3},{3,2},{4,5},{5,4},{6,7},{7,6},{8,9},{9,8},{10,11... | collective-permute-start | bytes 1327112 | tf_op jit(solution)/shard_map/ppermute | solution.py:18
  296.0 7.2 %collective-permute-start.31 = (bf16[2,72,768]{2,1,0:T(8,128)(2,1)}, bf16[2,72,768]{2,1,0:T(8,128)(2,1)S(1)}, u32[]{:S(2)}, u32[]{:S(2)}) collective-permute-start(bf16[2,72,768]{2,1,0:T(8,128)(2,1)} %get-tuple-element.184), channel_id=1, source_target_pairs={{0,4},{1,5},{2,6},{3,7},{4,0},{5,1},{6,2},{7,3},{8,12},{9,13},{10,... | collective-permute-start | bytes 663560 | tf_op jit(solution)/shard_map/ppermute | solution.py:18
  296.8 6.9 %collective-permute-start.32 = (bf16[2,72,768]{2,1,0:T(8,128)(2,1)}, bf16[2,72,768]{2,1,0:T(8,128)(2,1)S(1)}, u32[]{:S(2)}, u32[]{:S(2)}) collective-permute-start(bf16[2,72,768]{2,1,0:T(8,128)(2,1)} %get-tuple-element.186), channel_id=1, source_target_pairs={{0,1},{1,0},{2,3},{3,2},{4,5},{5,4},{6,7},{7,6},{8,9},{9,8},{10,11... | collective-permute-start | bytes 663560 | tf_op jit(solution)/shard_map/ppermute | solution.py:18
  297.9 6.1 %collective-permute-start.33 = (bf16[2,72,768]{2,1,0:T(8,128)(2,1)}, bf16[2,72,768]{2,1,0:T(8,128)(2,1)S(1)}, u32[]{:S(2)}, u32[]{:S(2)}) collective-permute-start(bf16[2,72,768]{2,1,0:T(8,128)(2,1)} %get-tuple-element.188), channel_id=1, source_target_pairs={{0,2},{1,3},{2,0},{3,1},{4,6},{5,7},{6,4},{7,5},{8,10},{9,11},{10,... | collective-permute-start | bytes 663560 | tf_op jit(solution)/shard_map/ppermute | solution.py:18
  307.0 27.8 %collective-permute-start.43 = (bf16[1,72,2304]{2,1,0:T(8,128)(2,1)}, bf16[1,72,2304]{2,1,0:T(8,128)(2,1)S(1)}, u32[]{:S(2)}, u32[]{:S(2)}) collective-permute-start(bf16[1,72,2304]{2,1,0:T(8,128)(2,1)} %get-tuple-element.220), channel_id=1, source_target_pairs={{0,8},{1,9},{2,10},{3,11},{4,12},{5,13},{6,14},{7,15},{8,0},{9,1},... | collective-permute-start | bytes 995336 | tf_op jit(solution)/shard_map/ppermute | solution.py:18
  319.3 19.7 %collective-permute-start.34 = (bf16[8,72,768]{2,1,0:T(8,128)(2,1)}, bf16[8,72,768]{2,1,0:T(8,128)(2,1)S(1)}, u32[]{:S(2)}, u32[]{:S(2)}) collective-permute-start(bf16[8,72,768]{2,1,0:T(8,128)(2,1)} %get-tuple-element.195), channel_id=1, source_target_pairs={{0,1},{1,0},{2,3},{3,2},{4,5},{5,4},{6,7},{7,6},{8,9},{9,8},{10,11... | collective-permute-start | bytes 2654216 | tf_op jit(solution)/shard_map/ppermute | solution.py:18
  320.7 19.4 %collective-permute-start.35 = (bf16[8,72,768]{2,1,0:T(8,128)(2,1)}, bf16[8,72,768]{2,1,0:T(8,128)(2,1)S(1)}, u32[]{:S(2)}, u32[]{:S(2)}) collective-permute-start(bf16[8,72,768]{2,1,0:T(8,128)(2,1)} %get-tuple-element.197), channel_id=1, source_target_pairs={{0,2},{1,3},{2,0},{3,1},{4,6},{5,7},{6,4},{7,5},{8,10},{9,11},{10,... | collective-permute-start | bytes 2654216 | tf_op jit(solution)/shard_map/ppermute | solution.py:18
  321.0 21.2 %collective-permute-start.36 = (bf16[8,72,768]{2,1,0:T(8,128)(2,1)}, bf16[8,72,768]{2,1,0:T(8,128)(2,1)}, u32[]{:S(2)}, u32[]{:S(2)}) collective-permute-start(bf16[8,72,768]{2,1,0:T(8,128)(2,1)} %get-tuple-element.199), channel_id=1, source_target_pairs={{0,4},{1,5},{2,6},{3,7},{4,0},{5,1},{6,2},{7,3},{8,12},{9,13},{10,... | collective-permute-start | bytes 2654216 | tf_op jit(solution)/shard_map/ppermute | solution.py:18
  334.8 12.0 %collective-permute-start.37 = (bf16[128,2304]{1,0:T(8,128)(2,1)}, bf16[128,2304]{1,0:T(8,128)(2,1)}, u32[]{:S(2)}, u32[]{:S(2)}) collective-permute-start(bf16[128,2304]{1,0:T(8,128)(2,1)} %get-tuple-element.192.top_ref), channel_id=1, source_target_pairs={{0,16},{16,0},{1,17},{17,1},{2,18},{18,2},{3,19},{19,3},{4,20},{20... | collective-permute-start | bytes 1769480 | tf_op jit(solution)/shard_map/ppermute | solution.py:22
  334.8 12.0 %collective-permute-start.38 = (bf16[128,2304]{1,0:T(8,128)(2,1)}, bf16[128,2304]{1,0:T(8,128)(2,1)}, u32[]{:S(2)}, u32[]{:S(2)}) collective-permute-start(bf16[128,2304]{1,0:T(8,128)(2,1)} %get-tuple-element.193.low_ref), channel_id=1, source_target_pairs={{0,16},{16,0},{1,17},{17,1},{2,18},{18,2},{3,19},{19,3},{4,20},{20... | collective-permute-start | bytes 1769480 | tf_op jit(solution)/shard_map/ppermute | solution.py:22
  339.0 78.9 %collective-permute-start.53 = (f32[72,2304]{1,0:T(8,128)}, f32[72,2304]{1,0:T(8,128)S(1)}, u32[]{:S(2)}, u32[]{:S(2)}) collective-permute-start(f32[72,2304]{1,0:T(8,128)} %finish.3.refs_7_.own_ref), channel_id=1, source_target_pairs={{0,16},{16,0},{1,17},{17,1},{2,18},{18,2},{3,19},{19,3},{4,20},{20... | collective-permute-start | bytes 1990664 | tf_op jit(solution)/shard_map/ppermute | solution.py:22
  362.3 12.4 %collective-permute-start.40 = (bf16[4,72,768]{2,1,0:T(8,128)(2,1)}, bf16[4,72,768]{2,1,0:T(8,128)(2,1)S(1)}, u32[]{:S(2)}, u32[]{:S(2)}) collective-permute-start(bf16[4,72,768]{2,1,0:T(8,128)(2,1)} %get-tuple-element.217), channel_id=1, source_target_pairs={{0,2},{1,3},{2,0},{3,1},{4,6},{5,7},{6,4},{7,5},{8,10},{9,11},{10,... | collective-permute-start | bytes 1327112 | tf_op jit(solution)/shard_map/ppermute | solution.py:18
  363.7 14.5 %collective-permute-start.41 = (bf16[4,72,768]{2,1,0:T(8,128)(2,1)}, bf16[4,72,768]{2,1,0:T(8,128)(2,1)S(1)}, u32[]{:S(2)}, u32[]{:S(2)}) collective-permute-start(bf16[4,72,768]{2,1,0:T(8,128)(2,1)} %get-tuple-element.218), channel_id=1, source_target_pairs={{0,4},{1,5},{2,6},{3,7},{4,0},{5,1},{6,2},{7,3},{8,12},{9,13},{10,... | collective-permute-start | bytes 1327112 | tf_op jit(solution)/shard_map/ppermute | solution.py:18
  363.8 14.5 %collective-permute-start.42 = (bf16[4,72,768]{2,1,0:T(8,128)(2,1)}, bf16[4,72,768]{2,1,0:T(8,128)(2,1)S(1)}, u32[]{:S(2)}, u32[]{:S(2)}) collective-permute-start(bf16[4,72,768]{2,1,0:T(8,128)(2,1)} %get-tuple-element.219), channel_id=1, source_target_pairs={{0,1},{1,0},{2,3},{3,2},{4,5},{5,4},{6,7},{7,6},{8,9},{9,8},{10,11... | collective-permute-start | bytes 1327112 | tf_op jit(solution)/shard_map/ppermute | solution.py:18
  366.2 19.3 %collective-permute-start.39 = (f32[256,128]{1,0:T(8,128)S(1)}, f32[256,128]{1,0:T(8,128)S(1)}, u32[]{:S(2)}, u32[]{:S(2)}) collective-permute-start(f32[256,128]{1,0:T(8,128)S(1)} %pad_maximum_fusion.1.refs_6_.v_ref), channel_id=1, source_target_pairs={{0,8},{1,9},{2,10},{3,11},{4,12},{5,13},{6,14},{7,15},{8,0},{9,1},... | collective-permute-start | bytes 393224 | tf_op jit(solution)/shard_map/ppermute | solution.py:18
  382.8 7.0 %collective-permute-start.45 = (bf16[2,72,768]{2,1,0:T(8,128)(2,1)}, bf16[2,72,768]{2,1,0:T(8,128)(2,1)S(1)}, u32[]{:S(2)}, u32[]{:S(2)}) collective-permute-start(bf16[2,72,768]{2,1,0:T(8,128)(2,1)} %get-tuple-element.224), channel_id=1, source_target_pairs={{0,4},{1,5},{2,6},{3,7},{4,0},{5,1},{6,2},{7,3},{8,12},{9,13},{10,... | collective-permute-start | bytes 663560 | tf_op jit(solution)/shard_map/ppermute | solution.py:18
  382.8 7.0 %collective-permute-start.46 = (bf16[2,72,768]{2,1,0:T(8,128)(2,1)}, bf16[2,72,768]{2,1,0:T(8,128)(2,1)S(1)}, u32[]{:S(2)}, u32[]{:S(2)}) collective-permute-start(bf16[2,72,768]{2,1,0:T(8,128)(2,1)} %get-tuple-element.225), channel_id=1, source_target_pairs={{0,1},{1,0},{2,3},{3,2},{4,5},{5,4},{6,7},{7,6},{8,9},{9,8},{10,11... | collective-permute-start | bytes 663560 | tf_op jit(solution)/shard_map/ppermute | solution.py:18
  384.0 6.2 %collective-permute-start.47 = (bf16[2,72,768]{2,1,0:T(8,128)(2,1)}, bf16[2,72,768]{2,1,0:T(8,128)(2,1)S(1)}, u32[]{:S(2)}, u32[]{:S(2)}) collective-permute-start(bf16[2,72,768]{2,1,0:T(8,128)(2,1)} %get-tuple-element.226), channel_id=1, source_target_pairs={{0,2},{1,3},{2,0},{3,1},{4,6},{5,7},{6,4},{7,5},{8,10},{9,11},{10,... | collective-permute-start | bytes 663560 | tf_op jit(solution)/shard_map/ppermute | solution.py:18
  396.0 16.9 %collective-permute-start.48 = (f32[424,128]{1,0:T(8,128)}, f32[424,128]{1,0:T(8,128)S(1)}, u32[]{:S(2)}, u32[]{:S(2)}) collective-permute-start(f32[424,128]{1,0:T(8,128)} %meet.5.rest_3_.v_ref), channel_id=1, source_target_pairs={{0,2},{1,3},{2,0},{3,1},{4,6},{5,7},{6,4},{7,5},{8,10},{9,11},{10,... | collective-permute-start | bytes 651272 | tf_op jit(solution)/shard_map/ppermute | solution.py:18
  397.4 23.8 %collective-permute-start.54 = (bf16[1,72,2304]{2,1,0:T(8,128)(2,1)}, bf16[1,72,2304]{2,1,0:T(8,128)(2,1)S(1)}, u32[]{:S(2)}, u32[]{:S(2)}) collective-permute-start(bf16[1,72,2304]{2,1,0:T(8,128)(2,1)} %get-tuple-element.235), channel_id=1, source_target_pairs={{0,8},{1,9},{2,10},{3,11},{4,12},{5,13},{6,14},{7,15},{8,0},{9,1},... | collective-permute-start | bytes 995336 | tf_op jit(solution)/shard_map/ppermute | solution.py:18
  415.4 10.9 %collective-permute-start.49 = (f32[648,128]{1,0:T(8,128)}, f32[648,128]{1,0:T(8,128)S(1)}, u32[]{:S(2)}, u32[]{:S(2)}) collective-permute-start(f32[648,128]{1,0:T(8,128)} %meet.6.v_ref), channel_id=1, source_target_pairs={{0,1},{1,0},{2,3},{3,2},{4,5},{5,4},{6,7},{7,6},{8,9},{9,8},{10,11... | collective-permute-start | bytes 995336 | tf_op jit(solution)/shard_map/ppermute | solution.py:18
  416.3 25.7 %collective-permute-start.50 = (bf16[8,72,768]{2,1,0:T(8,128)(2,1)}, bf16[8,72,768]{2,1,0:T(8,128)(2,1)S(1)}, u32[]{:S(2)}, u32[]{:S(2)}) collective-permute-start(bf16[8,72,768]{2,1,0:T(8,128)(2,1)} %get-tuple-element.230), channel_id=1, source_target_pairs={{0,1},{1,0},{2,3},{3,2},{4,5},{5,4},{6,7},{7,6},{8,9},{9,8},{10,11... | collective-permute-start | bytes 2654216 | tf_op jit(solution)/shard_map/ppermute | solution.py:18
  417.4 24.7 %collective-permute-start.51 = (bf16[8,72,768]{2,1,0:T(8,128)(2,1)}, bf16[8,72,768]{2,1,0:T(8,128)(2,1)S(1)}, u32[]{:S(2)}, u32[]{:S(2)}) collective-permute-start(bf16[8,72,768]{2,1,0:T(8,128)(2,1)} %get-tuple-element.232), channel_id=1, source_target_pairs={{0,2},{1,3},{2,0},{3,1},{4,6},{5,7},{6,4},{7,5},{8,10},{9,11},{10,... | collective-permute-start | bytes 2654216 | tf_op jit(solution)/shard_map/ppermute | solution.py:18
  417.9 24.2 %collective-permute-start.52 = (bf16[8,72,768]{2,1,0:T(8,128)(2,1)}, bf16[8,72,768]{2,1,0:T(8,128)(2,1)S(1)}, u32[]{:S(2)}, u32[]{:S(2)}) collective-permute-start(bf16[8,72,768]{2,1,0:T(8,128)(2,1)} %get-tuple-element.234), channel_id=1, source_target_pairs={{0,4},{1,5},{2,6},{3,7},{4,0},{5,1},{6,2},{7,3},{8,12},{9,13},{10,... | collective-permute-start | bytes 2654216 | tf_op jit(solution)/shard_map/ppermute | solution.py:18
  423.9 7.6 %collective-permute-start.55 = (f32[72,2304]{1,0:T(8,128)}, f32[72,2304]{1,0:T(8,128)S(1)}, u32[]{:S(2)}, u32[]{:S(2)}) collective-permute-start(f32[72,2304]{1,0:T(8,128)} %finish.4.own_ref), channel_id=1, source_target_pairs={{0,16},{16,0},{1,17},{17,1},{2,18},{18,2},{3,19},{19,3},{4,20},{20... | collective-permute-start | bytes 1990664 | tf_op jit(solution)/shard_map/ppermute | solution.py:22
  429.0 21.6 %collective-permute-start.59 = (f32[1096,128]{1,0:T(8,128)}, f32[1096,128]{1,0:T(8,128)S(1)}, u32[]{:S(2)}, u32[]{:S(2)}) collective-permute-start(f32[1096,128]{1,0:T(8,128)} %meet.7.refs_6_), channel_id=1, source_target_pairs={{0,16},{16,0},{1,17},{17,1},{2,18},{18,2},{3,19},{19,3},{4,20},{20... | collective-permute-start | bytes 1683464 | tf_op jit(solution)/shard_map/ppermute | solution.py:22
  448.2 9.2 %collective-permute-start.56 = (bf16[4,72,768]{2,1,0:T(8,128)(2,1)}, bf16[4,72,768]{2,1,0:T(8,128)(2,1)S(1)}, u32[]{:S(2)}, u32[]{:S(2)}) collective-permute-start(bf16[4,72,768]{2,1,0:T(8,128)(2,1)} %get-tuple-element.237), channel_id=1, source_target_pairs={{0,2},{1,3},{2,0},{3,1},{4,6},{5,7},{6,4},{7,5},{8,10},{9,11},{10,... | collective-permute-start | bytes 1327112 | tf_op jit(solution)/shard_map/ppermute | solution.py:18
  448.7 8.9 %collective-permute-start.57 = (bf16[4,72,768]{2,1,0:T(8,128)(2,1)}, bf16[4,72,768]{2,1,0:T(8,128)(2,1)S(1)}, u32[]{:S(2)}, u32[]{:S(2)}) collective-permute-start(bf16[4,72,768]{2,1,0:T(8,128)(2,1)} %get-tuple-element.239), channel_id=1, source_target_pairs={{0,4},{1,5},{2,6},{3,7},{4,0},{5,1},{6,2},{7,3},{8,12},{9,13},{10,... | collective-permute-start | bytes 1327112 | tf_op jit(solution)/shard_map/ppermute | solution.py:18
  449.3 8.6 %collective-permute-start.58 = (bf16[4,72,768]{2,1,0:T(8,128)(2,1)}, bf16[4,72,768]{2,1,0:T(8,128)(2,1)S(1)}, u32[]{:S(2)}, u32[]{:S(2)}) collective-permute-start(bf16[4,72,768]{2,1,0:T(8,128)(2,1)} %get-tuple-element.241), channel_id=1, source_target_pairs={{0,1},{1,0},{2,3},{3,2},{4,5},{5,4},{6,7},{7,6},{8,9},{9,8},{10,11... | collective-permute-start | bytes 1327112 | tf_op jit(solution)/shard_map/ppermute | solution.py:18
  461.6 6.1 %collective-permute-start.60 = (bf16[2,72,768]{2,1,0:T(8,128)(2,1)}, bf16[2,72,768]{2,1,0:T(8,128)(2,1)S(1)}, u32[]{:S(2)}, u32[]{:S(2)}) collective-permute-start(bf16[2,72,768]{2,1,0:T(8,128)(2,1)} %get-tuple-element.243), channel_id=1, source_target_pairs={{0,4},{1,5},{2,6},{3,7},{4,0},{5,1},{6,2},{7,3},{8,12},{9,13},{10,... | collective-permute-start | bytes 663560 | tf_op jit(solution)/shard_map/ppermute | solution.py:18
  463.0 6.1 %collective-permute-start.61 = (bf16[2,72,768]{2,1,0:T(8,128)(2,1)}, bf16[2,72,768]{2,1,0:T(8,128)(2,1)S(1)}, u32[]{:S(2)}, u32[]{:S(2)}) collective-permute-start(bf16[2,72,768]{2,1,0:T(8,128)(2,1)} %get-tuple-element.245), channel_id=1, source_target_pairs={{0,1},{1,0},{2,3},{3,2},{4,5},{5,4},{6,7},{7,6},{8,9},{9,8},{10,11... | collective-permute-start | bytes 663560 | tf_op jit(solution)/shard_map/ppermute | solution.py:18
  464.6 6.1 %collective-permute-start.62 = (bf16[2,72,768]{2,1,0:T(8,128)(2,1)}, bf16[2,72,768]{2,1,0:T(8,128)(2,1)S(1)}, u32[]{:S(2)}, u32[]{:S(2)}) collective-permute-start(bf16[2,72,768]{2,1,0:T(8,128)(2,1)} %get-tuple-element.247), channel_id=1, source_target_pairs={{0,2},{1,3},{2,0},{3,1},{4,6},{5,7},{6,4},{7,5},{8,10},{9,11},{10,... | collective-permute-start | bytes 663560 | tf_op jit(solution)/shard_map/ppermute | solution.py:18
  473.8 13.7 %collective-permute-start.63 = (bf16[1,72,2304]{2,1,0:T(8,128)(2,1)}, bf16[1,72,2304]{2,1,0:T(8,128)(2,1)S(1)}, u32[]{:S(2)}, u32[]{:S(2)}) collective-permute-start(bf16[1,72,2304]{2,1,0:T(8,128)(2,1)} %get-tuple-element.249), channel_id=1, source_target_pairs={{0,8},{1,9},{2,10},{3,11},{4,12},{5,13},{6,14},{7,15},{8,0},{9,1},... | collective-permute-start | bytes 995336 | tf_op jit(solution)/shard_map/ppermute | solution.py:18
  475.0 11.8 %all-to-all-start.2 = ((f32[16,1,72]{2,1,0:T(1,128)}), f32[16,1,72]{2,1,0:T(1,128)S(1)}, u32[]{:S(2)}, u32[]{:S(2)}) async-start(f32[16,1,72]{2,1,0:T(1,128)} %bitcast.119), calls=%async_computation.2 | async-start | bytes 16384 | tf_op jit(solution)/shard_map/all_to_all | solution.py:45
  (80 other events, 385.9 us)
where the time goes:
time: 504 us; the launch traced here: 497 us
  Pallas kernels  224 us (44%)
  waiting for transfers between devices  127 us (25%)
  starting transfers between devices  80.3 us (16%)
  local copies, waits for them, and re-layouts  48.4 us (10%)
  other arithmetic  8.99 us (2%)
  matrix products  6.95 us (1%)
    ppermute x51, waiting for transfers between devices, swap(): return lax.ppermute(v, 'dp', [(i, i ^ bit) for i in range(n)])  91.6 us
    ppermute x51, starting transfers between devices, swap(): return lax.ppermute(v, 'dp', [(i, i ^ bit) for i in range(n)])  63.6 us
    pallas_call x3, Pallas kernels, product(): pl.pallas_call(functools.partial(product_kernel, n, firsts, steps, per, l...  31.6 us
    pallas_call x9, Pallas kernels, split(): pl.pallas_call(functools.partial(split_kernel, plan), out_shape=tuple(out...  29.6 us
    pallas_call x1, Pallas kernels, attention(): pl.pallas_call(attention_kernel, out_shape=(per_head, per_head, per_head,...  27.5 us
    unnamed x163, local copies, waits for them, and re-layouts  26.8 us
    all_to_all x3, waiting for transfers between devices, trade(): return lax.all_to_all(v, 'dp', 0, 0, tiled=True)  21.7 us
    pallas_call x2, Pallas kernels, mlp(): pl.pallas_call(mlp_last_kernel if last else mlp_first_kernel, grid=(half...  21.7 us
  transfers between devices with their start and end apart: 68, of which 32 were waited for; matrix products, arithmetic and copies ran while one was open for 8% of the time, Pallas kernels for 34%

commit v1 on v0

--- a/solution.py
+++ b/solution.py
@@ -145,13 +145,13 @@
         def _():
             for half, ref in ((s, own_ref), (1 - s, other_ref)):
                 for src, dst, w in pieces(n, rows, cut, half):
-                    out_ref[:, src : src + w] = ref[:, dst : dst + w]
+                    out_ref[:, src : src + w] = ref[:, ff // 2 + dst : ff // 2 + dst + w]
 
 
 def fc1_rows(n, side, own, other):
     return pl.pallas_call(
         functools.partial(fc1_rows_kernel, n),
-        out_shape=shape((own.shape[0], 2 * own.shape[1]), F32),
+        out_shape=shape(own.shape, F32),
         in_specs=[SCALAR, WHOLE, WHOLE],
         out_specs=WHOLE,
         compiler_params=params(),
@@ -529,6 +529,48 @@
     )(v, r, *after)
 
 
+def pack_kernel(side_ref, a_ref, b_ref, c_ref, d_ref, lo_ref, hi_ref, pre_ref, *rest):
+    out_ref = rest[-1]
+    lanes = out_ref.shape[1]
+    per = a_ref.shape[1] // lanes
+
+    def row(at, ref, i, rounded=False):
+        for k in range(ref.shape[1] // lanes):
+            value = ref[i : i + 1, k * lanes : (k + 1) * lanes]
+            out_ref[at + k : at + k + 1, :] = value.astype(BF).astype(F32) if rounded else value
+
+    for k, (ref, i) in enumerate(((c_ref, 0), (c_ref, 1), (b_ref, 3), (a_ref, 1))):
+        row(k * per, ref, i)
+    many = pre_ref.shape[1] // lanes
+    for s in range(2):
+
+        @pl.when(side_ref[0] == s)
+        def _():
+            for i in range(2):
+                row(4 * per + (s ^ i) * many, pre_ref, i)
+
+    at = 4 * per + 2 * many
+    for ref in (lo_ref, hi_ref):
+        for k in range(ref.shape[1] // lanes):
+            out_ref[at : at + HEADS, :] = ref[:, k * lanes : (k + 1) * lanes]
+            at += HEADS
+    out_ref[at:, :] = jnp.zeros((out_ref.shape[0] - at, lanes), F32)
+    parts = ((d_ref, 0), (d_ref, 1), (b_ref, 2), (b_ref, 0), (b_ref, 1), (a_ref, 0))
+    for k, (ref, i) in enumerate(parts):
+        row(at + k * per, ref, i, True)
+
+
+def pack(side, arrays, rows, after=()):
+    return pl.pallas_call(
+        pack_kernel,
+        out_shape=shape((rows, 128), F32),
+        in_specs=[SCALAR] + [WHOLE] * len(arrays) + [HBM] * len(after),
+        out_specs=WHOLE,
+        compiler_params=params(),
+        name="pack",
+    )(side, *arrays, *after)
+
+
 def meet_kernel(bit, rows, chip_ref, v_ref, r_ref, *rest):
     out_ref = rest[-1]
     out_ref[0:SUM_ROWS, :] = v_ref[0:SUM_ROWS, :] + r_ref[0:SUM_ROWS, :]
@@ -569,14 +611,20 @@
 
     def plan(self):
         chains = [[k] for k in range(len(self.pairs))]
-        if len(self.pairs) == 3 and not self.orders[0]:
-            chains = [[0, 1, 2]]
+        if len(self.pairs) > 1 and not self.orders[0]:
+            chains = [list(range(len(self.pairs)))]
             self.orders = [list(self.tail)]
         bits = [self.orders[chain[0]].pop(0) for chain in chains]
         return [
             ([self.pairs[j] for j in chain], bit, list(self.left[chain[0]]))
             for chain, bit in zip(chains, bits)
         ]
+
+    def parted(self):
+        return len(self.pairs) > 1 and not self.orders[0]
+
+    def take(self, other):
+        self.pairs = other.pairs + self.pairs
 
     def go(self, jobs, outs):
         self.pairs = [
@@ -617,7 +665,7 @@
 def fc2_rows(side, own, other):
     return pl.pallas_call(
         fc2_rows_kernel,
-        out_shape=shape((4 * own.shape[0], own.shape[1] // 2), F32),
+        out_shape=shape((4 * own.shape[0], own.shape[1] // 4), F32),
         in_specs=[SCALAR, WHOLE, WHOLE],
         out_specs=WHOLE,
         compiler_params=params(),
@@ -1327,72 +1375,50 @@
     pre_twin = swap_stream(pre1)
     one = first_heads(qh, kh, vh, bias, keep, g_mixed, after=kept + (pre_twin,))
     kept = step([sum_c], one[0])
-    kept = step([sum_c], *kept)
-    parts_b = product(
-        chip_word,
-        normed_two,
-        n2_twin,
-        pre0,
-        pre_twin,
-        width,
-        n,
-        firsts,
-        after=kept,
-    )
+    while not sum_c.parted():
+        kept = step([sum_c], *kept)
+    parts_b = product(chip_word, normed_two, n2_twin, pre0, pre_twin, width, n, firsts, after=kept)
     sum_b = Reduction(chip_word, parts_b, n)
     g_mine, top, low, lo, hi, sums_c = last_heads(
         side_word, qh, kh, vh, bias, keep, g_mixed, g_att, one, after=(parts_b[0][0],)
     )
     g_theirs = (top, low)
     g_twin = (swap_stream(top), swap_stream(low))
-    while not sum_c.done():
-        step([sum_c])
-    d_c = sum_c.result(g_mine)
     kept = step([sum_b], g_mine) + g_twin
     grad_tokens, sums_d = tokens_back(
         side_word, a_own, a_other, g_mine, g_theirs, x, g_middle, mod, place, after=kept
     )
-    sums_a, sums_b, sums_c, lo, hi, pre_sum = hold((sums_a, sums_b, sums_c, lo, hi, pre_sum), sums_d)
-    g_mod = jnp.concatenate([sums_d[0], sums_d[1], sums_b[2], sums_b[0], sums_b[1], sums_a[0]])
-    g_mod = g_mod.astype(BF).astype(F32).reshape(-1, 128)
-    pre_sum = jnp.where(first, pre_sum, jnp.concatenate([pre_sum[1:], pre_sum[:1]]))
-    pre_sum = jnp.transpose(pre_sum.reshape(2, 2, n, cut // 2), (2, 0, 1, 3))
-    smalls = [
-        sums_c[0],
-        sums_c[1],
-        sums_b[3],
-        pre_sum.reshape(-1),
-        sums_a[1],
-        table_of(lo, hi).reshape(-1),
-    ]
-    sizes = [t.shape[0] for t in smalls]
-    packed = jnp.concatenate(smalls)
-    packed = jnp.pad(packed, (0, 128 * SUM_ROWS - packed.shape[0])).reshape(-1, 128)
-    mod_rows = g_mod.shape[0]
-    pad = -mod_rows % 8
-    told = jnp.concatenate([packed, jnp.pad(g_mod, ((0, pad), (0, 0)))], axis=0)
-    group = told.shape[0] - SUM_ROWS
+
+    kept = (sums_d,)
+    while not sum_b.parted():
+        kept = step([sum_b], *kept)
+    mod_rows = 6 * width // 128
+    group = -(-mod_rows // 8) * 8
+    told = pack(
+        side_word, (sums_a, sums_b, sums_c, sums_d, lo, hi, pre_sum), SUM_ROWS + group, after=kept
+    )
     bits = all_bits(n)[::-1]
-    kept = (d_c,)
-    for b in bits[:2]:
-        came = swap(told, b, n)
-        if not sum_b.done():
-            kept = step([sum_b], told, *kept)
-        told = meet(chip_word, told, came, b, group, after=kept)
+    came = swap(told, bits[0], n)
+    sum_b.take(sum_c)
+    kept = (told,)
     while not sum_b.done():
         kept = step([sum_b], *kept)
+    told = meet(chip_word, told, came, bits[0], group, after=kept)
+    told = meet(chip_word, told, swap(told, bits[1], n), bits[1], group)
     came = swap(told, bits[2], n)
     parts_a = product(
         chip_word, lhs_mine, lhs_twin, g_mine, g_twin, width, n, firsts, after=(told,) + kept
     )
+    told = meet(chip_word, told, came, bits[2], group, after=(parts_a[0][0],))
     sum_a = Reduction(chip_word, parts_a, n)
-    told = meet(chip_word, told, came, bits[2], group, after=(parts_a[0][0],))
-    grad_w_fc2 = fc2_rows(side_word, d_c, swap_stream(d_c))
-    d_b = sum_b.result(parts_a[0][0])
-    grad_w_fc1 = fc1_rows(n, side_word, d_b, swap_stream(d_b))
     for b in bits[3:]:
         told = meet(chip_word, told, swap(told, b, n), b, group)
-    kept = step([sum_a], told, grad_w_fc2, grad_w_fc1)
+    d_cb = sum_b.result()
+    kept = step([sum_a], told, d_cb)
+    d_cb_twin = swap_stream(d_cb)
+    grad_w_fc2 = fc2_rows(side_word, d_cb, d_cb_twin)
+    grad_w_fc1 = fc1_rows(n, side_word, d_cb, d_cb_twin)
+    kept = step([sum_a], told, grad_w_fc2)
     twin = swap_stream(told)
 
     def mods_of(t):
@@ -1406,13 +1432,19 @@
         kept = step([sum_a], *kept)
     g_acts = trade(hold(mm_nt(g_own.astype(BF), w_ada), *kept)).reshape(width)
     grad_condition = g_acts * sig * (1.0 + cond * (1.0 - sig))
-    packed = (told[:SUM_ROWS] + twin[:SUM_ROWS]).reshape(-1)
-    parts, at = [], 0
-    for size in sizes:
-        parts.append(packed[at : at + size])
-        at += size
-
-    d_a = sum_a.result(g_acts, *parts)
+    sums = told[:SUM_ROWS] + twin[:SUM_ROWS]
+    per = width // 128
+    at = 4 * per + ff // 128
+    grad_b_fc1 = jnp.transpose(sums[4 * per : at].reshape(2, 2, n, cut // 2), (2, 0, 1, 3)).reshape(-1)
+    windows = jnp.transpose(sums[at:].reshape(2, -1, HEADS, 128), (0, 2, 1, 3)).reshape(2, HEADS, -1)
+    parts = (
+        sums[: 2 * per].reshape(-1),
+        sums[2 * per : 3 * per].reshape(-1),
+        grad_b_fc1,
+        sums[3 * per : 4 * per].reshape(-1),
+        table_of(windows[0], windows[1]),
+    )
+    d_a = sum_a.result(g_acts, grad_w_fc1, *parts)
     grad_w_qkv, grad_w_proj = attn_rows(side_word, d_a, swap_stream(d_a))
     return (
         out_tokens[None, None],
@@ -1424,11 +1456,7 @@
         grad_w_fc1,
         grad_w_fc2,
         grad_b_ada,
-        jnp.concatenate(parts[:2]),
-        parts[2],
-        parts[3],
-        parts[4],
-        parts[5].reshape(rel_table.shape),
+        *parts,
     )
 
 

time: 504 us -> 483 us (0.958)
  waiting for transfers between devices: 127 us -> 113 us
  starting transfers between devices: 80.3 us -> 75.2 us
    ppermute x51 -> x50, waiting for transfers between devices: 91.6 us -> 83.6 us  [swap(): return lax.ppermute(v, 'dp', [(i, i ^ bit) for i in range(n)])]
    ppermute x51 -> x50, starting transfers between devices: 63.6 us -> 58.5 us  [swap(): return lax.ppermute(v, 'dp', [(i, i ^ bit) for i in range(n)])]
    unnamed x163 -> x159, local copies, waits for them, and re-layouts: 26.8 us -> 25.1 us
    pallas_call x9 -> x8, Pallas kernels: 29.6 us -> 28.3 us  [split(): pl.pallas_call(functools.partial(split_kernel, plan), out_shape=tuple(out...]
    ppermute x14 -> x13, waiting for transfers between devices: 13.3 us -> 12.3 us  [swap_stream(): return lax.ppermute(v, 'stream', [(0, 1), (1, 0)])]
  transfers between devices with their start and end apart: 68 -> 66, of which waited for: 32 -> 28; matrix products, arithmetic and copies ran while one was open for 8% -> 9% of each run, Pallas kernels for 34% -> 33%
where the time goes in v1:
time: 483 us; the launch traced here: 476 us
  Pallas kernels  223 us (46%)
  waiting for transfers between devices  113 us (23%)
  starting transfers between devices  75.2 us (16%)
  local copies, waits for them, and re-layouts  47.6 us (10%)
  other arithmetic  8.58 us (2%)
  matrix products  6.91 us (1%)
    ppermute x50, waiting for transfers between devices, swap(): return lax.ppermute(v, 'dp', [(i, i ^ bit) for i in range(n)])  83.6 us
    ppermute x50, starting transfers between devices, swap(): return lax.ppermute(v, 'dp', [(i, i ^ bit) for i in range(n)])  58.5 us
    pallas_call x3, Pallas kernels, product(): pl.pallas_call(functools.partial(product_kernel, n, firsts, steps, per, l...  31.7 us
    pallas_call x8, Pallas kernels, split(): pl.pallas_call(functools.partial(split_kernel, plan), out_shape=tuple(out...  28.3 us
    pallas_call x1, Pallas kernels, attention(): pl.pallas_call(attention_kernel, out_shape=(per_head, per_head, per_head,...  27.1 us
    unnamed x159, local copies, waits for them, and re-layouts  25.1 us
    pallas_call x2, Pallas kernels, mlp(): pl.pallas_call(mlp_last_kernel if last else mlp_first_kernel, grid=(half...  21.8 us
    pallas_call x1, Pallas kernels, mlp_back(): pl.pallas_call(mlp_back_kernel, grid=(half // tile,), out_shape=(shape((l...  19.7 us
  transfers between devices with their start and end apart: 66, of which 28 were waited for; matrix products, arithmetic and copies ran while one was open for 9% of the time, Pallas kernels for 33%

profile of v1, /device:TPU:0, one launch (start us, length us, event | category | flops | bytes accessed | tf_op | source)
XLA Modules:
  0.0 476.4 jit_solution(9067573480553518981)
XLA Ops:
  0.7 1.9 attn_shard.1.rest_0_.refs_1_.refs_0_
  2.6 4.0 collective-permute-start
  10.7 4.8 %all-to-all-start = ((bf16[16,2,576]{2,1,0:T(2,128)(2,1)}), bf16[16,2,576]{2,1,0:T(2,128)(2,1)S(1)}, u32[]{:S(2)}, u32[]{:S(2)}) async-start(bf16[16,2,576]{2,1,0:T(2,128)(2,1)} %reshape.250), calls=%async_computation | async-start | bytes 81920 | tf_op jit(solution)/shard_map/all_to_all | solution.py:45
  21.6 2.5 mlp_shard.1.refs_2_.refs_0_
  24.1 2.0 bias_strip.1.refs_3_.strip_ref
  27.6 1.9 join.3
  29.5 1.9 collective-permute-start.1
  34.4 2.4 collective-permute-start.7
  39.8 2.5 join.4
  42.3 1.8 collective-permute-start.4
  44.6 2.7 collective-permute-start.6
  48.5 16.3 %collective-permute-done.7.refs_7_ = bf16[1,72,4608]{2,1,0:T(8,128)(2,1)S(1)} collective-permute-done((bf16[1,72,4608]{2,1,0:T(8,128)(2,1)}, bf16[1,72,4608]{2,1,0:T(8,128)(2,1)S(1)}, u32[]{:S(2)}, u32[]{:S(2)}) %collective-permute-start.7) | collective-permute-done | bytes 663584 | tf_op jit(solution)/shard_map/ppermute | solution.py:18
  66.9 4.3 merge.1
  72.9 27.9 %collective-permute-done.10.refs_5_.refs_3_ = bf16[12,72,768]{2,1,0:T(8,128)(2,1)S(1)} collective-permute-done((bf16[12,72,768]{2,1,0:T(8,128)(2,1)}, bf16[12,72,768]{2,1,0:T(8,128)(2,1)S(1)}, u32[]{:S(2)}, u32[]{:S(2)}) %collective-permute-start.10) | collective-permute-done | bytes 1327136 | tf_op jit(solution)/shard_map/ppermute | solution.py:18
  103.4 4.9 %cross.1 = (bf16[4,72,1536]{2,1,0:T(8,128)(2,1)}, bf16[4,72,1536]{2,1,0:T(8,128)(2,1)}, bf16[4,72,1536]{2,1,0:T(8,128)(2,1)}) custom-call(s32[1]{0:T(128)} %bitcast.1.chip_ref, bf16[12,72,768]{2,1,0:T(8,128)(2,1)} %get-tuple-element.133.refs_0_.refs_4_, bf16[12,72,768]{2,1,0:T(8,128)(2,1)} %copy-done.3, ...), custom_call_target="tpu_custom_call" | custom-call | tf_op jit(solution)/shard_map/cross/pallas_call | solution.py:398
  108.3 6.1 %assemble.2 = bf16[16,72,2304]{2,1,0:T(8,128)(2,1)} custom-call(s32[1]{0:T(128)} %bitcast.1.chip_ref, bf16[12,72,768]{2,1,0:T(8,128)(2,1)} %get-tuple-element.131.refs_2_.refs_0_, bf16[12,72,768]{2,1,0:T(8,128)(2,1)} %copy-done.4, bf16[12,72,768]{2,1,0:T(8,128)(2,1)} %get-tuple-element.132.refs_4_.refs_2_, bf16[12,72,768]{2,1,0:T(8,128)(2,1)} %copy-done.2, ...), custom_call_target="tpu_custom_call" | custom-call | tf_op jit(solution)/shard_map/assemble/pallas_call | solution.py:297
  117.8 2.3 copy.77
  120.1 5.7 %all-to-all-start.1 = ((f32[16,1,6912]{2,1,0:T(1,128)}), f32[16,1,6912]{2,1,0:T(1,128)S(1)}, u32[]{:S(2)}, u32[]{:S(2)}) async-start(f32[16,1,6912]{2,1,0:T(1,128)} %copy.77), calls=%async_computation.1 | async-start | bytes 884736 | tf_op jit(solution)/shard_map/all_to_all | solution.py:45
  130.1 15.6 %all-to-all-done.1 = f32[16,1,6912]{2,1,0:T(1,128)S(1)} async-done(((f32[16,1,6912]{2,1,0:T(1,128)}), f32[16,1,6912]{2,1,0:T(1,128)S(1)}, u32[]{:S(2)}, u32[]{:S(2)}) %all-to-all-start.1) | async-done | bytes 442400 | tf_op jit(solution)/shard_map/all_to_all | solution.py:45
  146.5 5.2 %join.5 = (bf16[8,72,1536]{2,1,0:T(8,128)(2,1)}, bf16[8,72,1536]{2,1,0:T(8,128)(2,1)}, bf16[8,72,1536]{2,1,0:T(8,128)(2,1)}) custom-call(s32[1]{0:T(128)} %bitcast.1.chip_ref, bf16[4,72,1536]{2,1,0:T(8,128)(2,1)} %get-tuple-element.134.refs_6_.refs_0_, bf16[4,72,1536]{2,1,0:T(8,128)(2,1)} %collective-permute-done.13.refs_1_, ...), custom_call_target="tpu_custom_call" | custom-call | tf_op jit(solution)/shard_map/join/pallas_call | solution.py:264
  157.9 27.1 %attention.1 = (bf16[16,256,72]{2,1,0:T(8,128)(2,1)}, bf16[16,256,72]{2,1,0:T(8,128)(2,1)}, bf16[16,256,72]{2,1,0:T(8,128)(2,1)}, bf16[256,2304]{1,0:T(8,128)(2,...) custom-call(s32[1]{0:T(128)} %bitcast.side_ref, ...), custom_call_target="tpu_custom_call" | custom-call | flops 3019898880 | bytes 24000000 | tf_op jit(solution)/shard_map/attention/pallas_call | solution.py:808
  185.0 6.7 %collective-permute-done.16.refs_1_ = bf16[8,72,1536]{2,1,0:T(8,128)(2,1)} collective-permute-done((bf16[8,72,1536]{2,1,0:T(8,128)(2,1)}, bf16[8,72,1536]{2,1,0:T(8,128)(2,1)}, u32[]{:S(2)}, u32[]{:S(2)}) %collective-permute-start.16) | collective-permute-done | bytes 1769504 | tf_op jit(solution)/shard_map/ppermute | solution.py:18
  192.4 8.7 %assemble.3 = bf16[16,72,4608]{2,1,0:T(8,128)(2,1)} custom-call(s32[1]{0:T(128)} %bitcast.1.chip_ref, bf16[8,72,1536]{2,1,0:T(8,128)(2,1)} %get-tuple-element.138.refs_0_, bf16[8,72,1536]{2,1,0:T(8,128)(2,1)} %collective-permute-done.16.refs_1_, bf16[8,72,1536]{2,1,0:T(8,128)(2,1)} %get-tuple-element.139.refs_2_, ...), custom_call_target="tpu_custom_call" | custom-call | tf_op jit(solution)/shard_map/assemble/pallas_call | solution.py:297
  201.1 10.0 %mlp.2 = (bf16[256,2304]{1,0:T(8,128)(2,1)}, f32[256,2304]{1,0:T(8,128)}, f32[256,1152]{1,0:T(8,128)}) custom-call(bf16[256,1152]{1,0:T(8,128)(2,1)} %get-tuple-element.137.refs_6_.normed_two_ref.l0_ref, bf16[1152,4608]{1,0:T(8,128)(2,1)} %bitcast.86, bf16[1152,4608]{1,0:T(8,128)(2,1)} %bitcast.87, bf16[1152,4608]{1,0:T(8,128)(2,1)} %bitcast.88, ...), custom_call_target="tpu_custom_call" | custom-call | flops 2717908992 | bytes 16000000 | tf_op jit(solution)/shard_map/mlp/pallas_call | solution.py:921
  211.1 6.7 %collective-permute-done.19.b_ref.c0_ref.c1_ref.b1_ref.c10_ref.c11_ref = bf16[1152,4608]{1,0:T(8,128)(2,1)} collective-permute-done((bf16[1152,4608]{1,0:T(8,128)(2,1)}, bf16[1152,4608]{1,0:T(8,128)(2,1)}, u32[]{:S(2)}, u32[]{:S(2)}) %collective-permute-start.19) | collective-permute-done | bytes 10616864 | tf_op jit(solution)/shard_map/ppermute | solution.py:22
  217.8 11.8 %mlp.3 = (bf16[256,2304]{1,0:T(8,128)(2,1)}, f32[256,2304]{1,0:T(8,128)}, bf16[256,1152]{1,0:T(8,128)(2,1)}, bf16[256,1152]{1,0:T(8,128)(2,1)}, f32[8,1152]{1,0:T(8,128)}) custom-call(bf16[256,1152]{1,0:T(8,128)(2,1)} %get-tuple-element.137.refs_6_.normed_two_ref.l0_ref, ...), custom_call_target="tpu_custom_call" | custom-call | flops 2717908992 | bytes 16000000 | tf_op jit(solution)/shard_map/mlp/pallas_call | solution.py:921
  230.7 4.0 collective-permute-done.21.rest_1_
  235.9 10.6 %product.3 = (bf16[8,72,768]{2,1,0:T(8,128)(2,1)}, bf16[8,72,768]{2,1,0:T(8,128)(2,1)}, bf16[8,72,768]{2,1,0:T(8,128)(2,1)}, bf16[8,72,768]{2,1,0:T(8,128)(2,1)}...) custom-call(s32[1]{0:T(128)} %bitcast.1.chip_ref, bf16[256,2304]{1,0:T(8,128)(2,1)} %get-tuple-element.152.l0_ref, ...), custom_call_target="tpu_custom_call" | custom-call | flops 2717908992 | bytes 12000000 | tf_op jit(solution)/shard_map/product/pallas_call | solution.py:465
  247.5 1.8 collective-permute-start.25
  250.8 19.7 %mlp_back.1 = (bf16[256,2304]{1,0:T(8,128)(2,1)}, bf16[256,2304]{1,0:T(8,128)(2,1)}, f32[2,2304]{1,0:T(2,128)}, f32[256,1152]{1,0:T(8,128)}, bf16[256,1152]{1,0:...) custom-call(bf16[256,1152]{1,0:T(8,128)(2,1)} %get-tuple-element.147.rest_0_.g_branch_ref, ...), custom_call_target="tpu_custom_call" | custom-call | flops 5435817984 | bytes 32000000 | tf_op jit(solution)/shard_map/mlp_back/pallas_call | solution.py:999
  272.1 4.5 split.8
  280.7 9.9 %first_heads.1 = (bf16[8,256,72]{2,1,0:T(8,128)(2,1)}, bf16[8,256,72]{2,1,0:T(8,128)(2,1)}, bf16[8,256,72]{2,1,0:T(8,128)(2,1)}, f32[8,16,512]{2,1,0:T(8,128)}) custom-call(bf16[16,256,72]{2,1,0:T(8,128)(2,1)} %get-tuple-element.144.qh_ref, bf16[16,256,72]{2,1,0:T(8,128)(2,1)} %get-tuple-element.145.kh_ref, bf16[16,256,72]{2,1,0:T(8,128)(2,1)} %get-tuple-element.146.vh_ref, ...), custom_call_target="tpu_custom_call" | custom-call | flops 377487360 | bytes 16000000 | tf_op jit(solution)/shard_map/first_heads/pallas_call | solution.py:1099
  291.7 3.0 split.9
  294.7 9.9 %product.4 = (bf16[8,72,768]{2,1,0:T(8,128)(2,1)}, bf16[8,72,768]{2,1,0:T(8,128)(2,1)}, bf16[8,72,768]{2,1,0:T(8,128)(2,1)}, bf16[8,72,768]{2,1,0:T(8,128)(2,1)}...) custom-call(s32[1]{0:T(128)} %bitcast.1.chip_ref, ...), custom_call_target="tpu_custom_call" | custom-call | flops 2717908992 | bytes 12000000 | tf_op jit(solution)/shard_map/product/pallas_call | solution.py:465
  305.5 1.8 collective-permute-start.32
  307.5 12.7 %last_heads.1 = (bf16[256,2304]{1,0:T(8,128)(2,1)}, bf16[128,2304]{1,0:T(8,128)(2,1)}, bf16[128,2304]{1,0:T(8,128)(2,1)}, f32[16,512]{1,0:T(8,128)}, f32[16,512]{1,0:T(8,128)}, /*index=5*/f32[8,1152]{1,0:T(8,128)}) custom-call(s32[1]{0:T(128)} %bitcast.side_ref, bf16[16,256,72]{2,1,0:T(8,128)(2,1)} %get-tuple-element.144.qh_ref, ...), custom_call_target="tpu_custom_call" | custom-call | flops 377487360 | bytes 16000000 | tf_op jit(solution)/shard_map/last_heads/pallas_call | solution.py:1174
  320.7 5.2 %collective-permute-done.31.refs_1_ = bf16[8,72,768]{2,1,0:T(8,128)(2,1)S(1)} collective-permute-done((bf16[8,72,768]{2,1,0:T(8,128)(2,1)}, bf16[8,72,768]{2,1,0:T(8,128)(2,1)S(1)}, u32[]{:S(2)}, u32[]{:S(2)}) %collective-permute-start.31) | collective-permute-done | bytes 884768 | tf_op jit(solution)/shard_map/ppermute | solution.py:18
  329.0 4.7 split.10
  338.5 9.6 %tokens_back.1 = (bf16[256,1152]{1,0:T(8,128)(2,1)}, f32[8,1152]{1,0:T(8,128)}) custom-call(s32[1]{0:T(128)} %bitcast.side_ref, bf16[1152,2304]{1,0:T(8,128)(2,1)} %bitcast.95, bf16[1152,2304]{1,0:T(8,128)(2,1)} %collective-permute-done.12.other_ref, bf16[256,2304]{1,0:T(8,128)(2,1)} %get-tuple-element.179.refs_6_.mine_ref.rest_0_, ...), custom_call_target="tpu_custom_call" | custom-call | flops 2038431744 | bytes 16000000 | tf_op jit(solution)/shard_map/tokens_back/pallas_call | solution.py:1237
  350.6 3.0 split.11
  357.5 2.3 collective-permute-start.39
  362.6 3.3 split.12
  366.5 1.6 meet.4.v_ref
  368.8 2.0 collective-permute-start.52
  370.8 3.9 collective-permute-done.46.r_ref
  375.3 1.7 meet.5.rest_3_.v_ref
  377.0 11.2 %product.5 = (bf16[8,72,768]{2,1,0:T(8,128)(2,1)}, bf16[8,72,768]{2,1,0:T(8,128)(2,1)}, bf16[8,72,768]{2,1,0:T(8,128)(2,1)}, bf16[8,72,768]{2,1,0:T(8,128)(2,1)}...) custom-call(s32[1]{0:T(128)} %bitcast.1.chip_ref, bf16[256,2304]{1,0:T(8,128)(2,1)} %get-tuple-element.212.l0_ref, ...), custom_call_target="tpu_custom_call" | custom-call | flops 2717908992 | bytes 12000000 | tf_op jit(solution)/shard_map/product/pallas_call | solution.py:465
  389.0 1.8 meet.6.v_ref
  392.8 2.0 collective-permute-start.50
  398.5 2.5 finish.2.refs_7_.own_ref
  402.4 2.0 meet.7.refs_6_
  406.9 7.1 %collective-permute-done.49.refs_1_ = bf16[8,72,768]{2,1,0:T(8,128)(2,1)S(1)} collective-permute-done((bf16[8,72,768]{2,1,0:T(8,128)(2,1)}, bf16[8,72,768]{2,1,0:T(8,128)(2,1)S(1)}, u32[]{:S(2)}, u32[]{:S(2)}) %collective-permute-start.49) | collective-permute-done | bytes 884768 | tf_op jit(solution)/shard_map/ppermute | solution.py:18
  414.1 2.4 collective-permute-done.51.refs_5_
  417.5 4.5 split.13
  431.1 1.7 convolution_add_fusion.refs_9_
  432.8 2.9 fc2_rows.1.refs_7_
  435.7 3.0 split.14
  438.6 2.0 collective-permute-start.57
  443.5 2.1 collective-permute-done.57.refs_1_
  448.6 2.4 split.15
  453.2 4.4 all-to-all-start.2
  462.2 3.7 fc1_rows.1.rest_1_
  468.6 2.0 finish.3.own_ref
  473.7 2.4 attn_rows.1
  (343 shorter events, 111.0 us)
Async XLA Ops:
  2.6 24.2 %collective-permute-start = (bf16[1,72,2304]{2,1,0:T(8,128)(2,1)}, bf16[1,72,2304]{2,1,0:T(8,128)(2,1)S(1)}, u32[]{:S(2)}, u32[]{:S(2)}) collective-permute-start(bf16[1,72,2304]{2,1,0:T(8,128)(2,1)} %attn_shard.1.rest_0_.refs_1_.refs_0_), channel_id=1, source_target_pairs={{0,8},{1,9},{2,10},{3,11},{4,12},{5,13},{6,14},{7,15},{8,0},{9,1},... | collective-permute-start | bytes 995336 | tf_op jit(solution)/shard_map/ppermute | solution.py:18
  10.7 15.4 %all-to-all-start = ((bf16[16,2,576]{2,1,0:T(2,128)(2,1)}), bf16[16,2,576]{2,1,0:T(2,128)(2,1)S(1)}, u32[]{:S(2)}, u32[]{:S(2)}) async-start(bf16[16,2,576]{2,1,0:T(2,128)(2,1)} %reshape.250), calls=%async_computation | async-start | bytes 81920 | tf_op jit(solution)/shard_map/all_to_all | solution.py:45
  29.5 7.2 %collective-permute-start.1 = (bf16[2,72,768]{2,1,0:T(8,128)(2,1)}, bf16[2,72,768]{2,1,0:T(8,128)(2,1)S(1)}, u32[]{:S(2)}, u32[]{:S(2)}) collective-permute-start(bf16[2,72,768]{2,1,0:T(8,128)(2,1)} %get-tuple-element.125.refs_0_.refs_6_.refs_1_), channel_id=1, source_target_pairs={{0,4},{1,5},{2,6},{3,7},{4,0},{5,1},{6,2},{7,3},{8,12},{9,13},{10,... | collective-permute-start | bytes 663560 | tf_op jit(solution)/shard_map/ppermute | solution.py:18
  31.5 6.3 %collective-permute-start.2 = (bf16[2,72,768]{2,1,0:T(8,128)(2,1)}, bf16[2,72,768]{2,1,0:T(8,128)(2,1)S(1)}, u32[]{:S(2)}, u32[]{:S(2)}) collective-permute-start(bf16[2,72,768]{2,1,0:T(8,128)(2,1)} %get-tuple-element.126.refs_2_.refs_7_), channel_id=1, source_target_pairs={{0,1},{1,0},{2,3},{3,2},{4,5},{5,4},{6,7},{7,6},{8,9},{9,8},{10,11... | collective-permute-start | bytes 663560 | tf_op jit(solution)/shard_map/ppermute | solution.py:18
  32.9 6.1 %collective-permute-start.3 = (bf16[2,72,768]{2,1,0:T(8,128)(2,1)}, bf16[2,72,768]{2,1,0:T(8,128)(2,1)S(1)}, u32[]{:S(2)}, u32[]{:S(2)}) collective-permute-start(bf16[2,72,768]{2,1,0:T(8,128)(2,1)} %get-tuple-element.127.refs_4_.refs_8_.refs_3_), channel_id=1, source_target_pairs={{0,2},{1,3},{2,0},{3,1},{4,6},{5,7},{6,4},{7,5},{8,10},{9,11},{10,... | collective-permute-start | bytes 663560 | tf_op jit(solution)/shard_map/ppermute | solution.py:18
  34.4 30.4 %collective-permute-start.7 = (bf16[1,72,4608]{2,1,0:T(8,128)(2,1)}, bf16[1,72,4608]{2,1,0:T(8,128)(2,1)S(1)}, u32[]{:S(2)}, u32[]{:S(2)}) collective-permute-start(bf16[1,72,4608]{2,1,0:T(8,128)(2,1)} %hold.5.refs_6_), channel_id=1, source_target_pairs={{0,8},{1,9},{2,10},{3,11},{4,12},{5,13},{6,14},{7,15},{8,0},{9,1},... | collective-permute-start | bytes 1990664 | tf_op jit(solution)/shard_map/ppermute | solution.py:18
  42.3 22.5 %collective-permute-start.4 = (bf16[4,72,768]{2,1,0:T(8,128)(2,1)}, bf16[4,72,768]{2,1,0:T(8,128)(2,1)S(1)}, u32[]{:S(2)}, u32[]{:S(2)}) collective-permute-start(bf16[4,72,768]{2,1,0:T(8,128)(2,1)} %get-tuple-element.128.refs_0_), channel_id=1, source_target_pairs={{0,2},{1,3},{2,0},{3,1},{4,6},{5,7},{6,4},{7,5},{8,10},{9,11},{10,... | collective-permute-start | bytes 1327112 | tf_op jit(solution)/shard_map/ppermute | solution.py:18
  44.1 21.3 %collective-permute-start.5 = (bf16[4,72,768]{2,1,0:T(8,128)(2,1)}, bf16[4,72,768]{2,1,0:T(8,128)(2,1)S(1)}, u32[]{:S(2)}, u32[]{:S(2)}) collective-permute-start(bf16[4,72,768]{2,1,0:T(8,128)(2,1)} %get-tuple-element.129.refs_2_), channel_id=1, source_target_pairs={{0,4},{1,5},{2,6},{3,7},{4,0},{5,1},{6,2},{7,3},{8,12},{9,13},{10,... | collective-permute-start | bytes 1327112 | tf_op jit(solution)/shard_map/ppermute | solution.py:18
  44.6 20.8 %collective-permute-start.6 = (bf16[4,72,768]{2,1,0:T(8,128)(2,1)}, bf16[4,72,768]{2,1,0:T(8,128)(2,1)S(1)}, u32[]{:S(2)}, u32[]{:S(2)}) collective-permute-start(bf16[4,72,768]{2,1,0:T(8,128)(2,1)} %get-tuple-element.130.refs_4_), channel_id=1, source_target_pairs={{0,1},{1,0},{2,3},{3,2},{4,5},{5,4},{6,7},{7,6},{8,9},{9,8},{10,11... | collective-permute-start | bytes 1327112 | tf_op jit(solution)/shard_map/ppermute | solution.py:18
  71.2 29.6 %collective-permute-start.10 = (bf16[12,72,768]{2,1,0:T(8,128)(2,1)}, bf16[12,72,768]{2,1,0:T(8,128)(2,1)S(1)}, u32[]{:S(2)}, u32[]{:S(2)}) collective-permute-start(bf16[12,72,768]{2,1,0:T(8,128)(2,1)} %get-tuple-element.132.refs_4_.refs_2_), channel_id=1, source_target_pairs={{0,2},{1,3},{2,0},{3,1},{4,6},{5,7},{6,4},{7,5},{8,10},{9,11},{10,... | collective-permute-start | bytes 3981320 | tf_op jit(solution)/shard_map/ppermute | solution.py:18
  71.4 29.3 %collective-permute-start.11 = (bf16[12,72,768]{2,1,0:T(8,128)(2,1)}, bf16[12,72,768]{2,1,0:T(8,128)(2,1)S(1)}, u32[]{:S(2)}, u32[]{:S(2)}) collective-permute-start(bf16[12,72,768]{2,1,0:T(8,128)(2,1)} %get-tuple-element.133.refs_0_.refs_4_), channel_id=1, source_target_pairs={{0,4},{1,5},{2,6},{3,7},{4,0},{5,1},{6,2},{7,3},{8,12},{9,13},{10,... | collective-permute-start | bytes 3981320 | tf_op jit(solution)/shard_map/ppermute | solution.py:18
  71.4 29.4 %collective-permute-start.9 = (bf16[12,72,768]{2,1,0:T(8,128)(2,1)}, bf16[12,72,768]{2,1,0:T(8,128)(2,1)S(1)}, u32[]{:S(2)}, u32[]{:S(2)}) collective-permute-start(bf16[12,72,768]{2,1,0:T(8,128)(2,1)} %get-tuple-element.131.refs_2_.refs_0_), channel_id=1, source_target_pairs={{0,1},{1,0},{2,3},{3,2},{4,5},{5,4},{6,7},{7,6},{8,9},{9,8},{10,11... | collective-permute-start | bytes 3981320 | tf_op jit(solution)/shard_map/ppermute | solution.py:18
  114.4 43.5 %collective-permute-start.12 = (bf16[1152,2304]{1,0:T(8,128)(2,1)}, bf16[1152,2304]{1,0:T(8,128)(2,1)}, u32[]{:S(2)}, u32[]{:S(2)}) collective-permute-start(bf16[1152,2304]{1,0:T(8,128)(2,1)} %bitcast.92), channel_id=1, source_target_pairs={{0,16},{16,0},{1,17},{17,1},{2,18},{18,2},{3,19},{19,3},{4,20},{20... | collective-permute-start | bytes 15925256 | tf_op jit(solution)/shard_map/ppermute | solution.py:22
  114.4 32.1 %collective-permute-start.13 = (bf16[4,72,1536]{2,1,0:T(8,128)(2,1)S(1)}, bf16[4,72,1536]{2,1,0:T(8,128)(2,1)}, u32[]{:S(2)}, u32[]{:S(2)}) collective-permute-start(bf16[4,72,1536]{2,1,0:T(8,128)(2,1)S(1)} %copy-done.6), channel_id=1, source_target_pairs={{0,2},{1,3},{2,0},{3,1},{4,6},{5,7},{6,4},{7,5},{8,10},{9,11},{10,... | collective-permute-start | bytes 2654216 | tf_op jit(solution)/shard_map/ppermute | solution.py:18
  115.8 30.7 %collective-permute-start.14 = (bf16[4,72,1536]{2,1,0:T(8,128)(2,1)S(1)}, bf16[4,72,1536]{2,1,0:T(8,128)(2,1)}, u32[]{:S(2)}, u32[]{:S(2)}) collective-permute-start(bf16[4,72,1536]{2,1,0:T(8,128)(2,1)S(1)} %copy-done.7), channel_id=1, source_target_pairs={{0,4},{1,5},{2,6},{3,7},{4,0},{5,1},{6,2},{7,3},{8,12},{9,13},{10,... | collective-permute-start | bytes 2654216 | tf_op jit(solution)/shard_map/ppermute | solution.py:18
  116.5 30.1 %collective-permute-start.15 = (bf16[4,72,1536]{2,1,0:T(8,128)(2,1)}, bf16[4,72,1536]{2,1,0:T(8,128)(2,1)}, u32[]{:S(2)}, u32[]{:S(2)}) collective-permute-start(bf16[4,72,1536]{2,1,0:T(8,128)(2,1)} %get-tuple-element.136.refs_8_.refs_4_), channel_id=1, source_target_pairs={{0,1},{1,0},{2,3},{3,2},{4,5},{5,4},{6,7},{7,6},{8,9},{9,8},{10,11... | collective-permute-start | bytes 2654216 | tf_op jit(solution)/shard_map/ppermute | solution.py:18
  120.1 25.6 %all-to-all-start.1 = ((f32[16,1,6912]{2,1,0:T(1,128)}), f32[16,1,6912]{2,1,0:T(1,128)S(1)}, u32[]{:S(2)}, u32[]{:S(2)}) async-start(f32[16,1,6912]{2,1,0:T(1,128)} %copy.77), calls=%async_computation.1 | async-start | bytes 884736 | tf_op jit(solution)/shard_map/all_to_all | solution.py:45
  151.7 39.9 %collective-permute-start.16 = (bf16[8,72,1536]{2,1,0:T(8,128)(2,1)}, bf16[8,72,1536]{2,1,0:T(8,128)(2,1)}, u32[]{:S(2)}, u32[]{:S(2)}) collective-permute-start(bf16[8,72,1536]{2,1,0:T(8,128)(2,1)} %get-tuple-element.138.refs_0_), channel_id=1, source_target_pairs={{0,1},{1,0},{2,3},{3,2},{4,5},{5,4},{6,7},{7,6},{8,9},{9,8},{10,11... | collective-permute-start | bytes 5308424 | tf_op jit(solution)/shard_map/ppermute | solution.py:18
  152.0 39.9 %collective-permute-start.17 = (bf16[8,72,1536]{2,1,0:T(8,128)(2,1)}, bf16[8,72,1536]{2,1,0:T(8,128)(2,1)}, u32[]{:S(2)}, u32[]{:S(2)}) collective-permute-start(bf16[8,72,1536]{2,1,0:T(8,128)(2,1)} %get-tuple-element.139.refs_2_), channel_id=1, source_target_pairs={{0,2},{1,3},{2,0},{3,1},{4,6},{5,7},{6,4},{7,5},{8,10},{9,11},{10,... | collective-permute-start | bytes 5308424 | tf_op jit(solution)/shard_map/ppermute | solution.py:18
  153.6 38.8 %collective-permute-start.18 = (bf16[8,72,1536]{2,1,0:T(8,128)(2,1)}, bf16[8,72,1536]{2,1,0:T(8,128)(2,1)}, u32[]{:S(2)}, u32[]{:S(2)}) collective-permute-start(bf16[8,72,1536]{2,1,0:T(8,128)(2,1)} %get-tuple-element.140.refs_4_), channel_id=1, source_target_pairs={{0,4},{1,5},{2,6},{3,7},{4,0},{5,1},{6,2},{7,3},{8,12},{9,13},{10,... | collective-permute-start | bytes 5308424 | tf_op jit(solution)/shard_map/ppermute | solution.py:18
  201.1 16.7 %collective-permute-start.19 = (bf16[1152,4608]{1,0:T(8,128)(2,1)}, bf16[1152,4608]{1,0:T(8,128)(2,1)}, u32[]{:S(2)}, u32[]{:S(2)}) collective-permute-start(bf16[1152,4608]{1,0:T(8,128)(2,1)} %bitcast.85), channel_id=1, source_target_pairs={{0,16},{16,0},{1,17},{17,1},{2,18},{18,2},{3,19},{19,3},{4,20},{20... | collective-permute-start | bytes 31850504 | tf_op jit(solution)/shard_map/ppermute | solution.py:22
  229.6 5.1 %collective-permute-start.20 = (bf16[256,2304]{1,0:T(8,128)(2,1)}, bf16[256,2304]{1,0:T(8,128)(2,1)S(1)}, u32[]{:S(2)}, u32[]{:S(2)}) collective-permute-start(bf16[256,2304]{1,0:T(8,128)(2,1)} %get-tuple-element.153), channel_id=1, source_target_pairs={{0,16},{16,0},{1,17},{17,1},{2,18},{18,2},{3,19},{19,3},{4,20},{20... | collective-permute-start | bytes 3538952 | tf_op jit(solution)/shard_map/ppermute | solution.py:22
  229.8 19.8 %collective-permute-start.22 = (bf16[256,2304]{1,0:T(8,128)(2,1)S(1)}, bf16[256,2304]{1,0:T(8,128)(2,1)S(1)}, u32[]{:S(2)}, u32[]{:S(2)}) collective-permute-start(bf16[256,2304]{1,0:T(8,128)(2,1)S(1)} %copy-done.70), channel_id=1, source_target_pairs={{0,16},{16,0},{1,17},{17,1},{2,18},{18,2},{3,19},{19,3},{4,20},{20... | collective-permute-start | bytes 3538952 | tf_op jit(solution)/shard_map/ppermute | solution.py:22
  230.2 4.5 collective-permute-start.21
  230.3 19.2 %collective-permute-start.23 = (bf16[256,1152]{1,0:T(8,128)(2,1)S(1)}, bf16[256,1152]{1,0:T(8,128)(2,1)S(1)}, u32[]{:S(2)}, u32[]{:S(2)}) collective-permute-start(bf16[256,1152]{1,0:T(8,128)(2,1)S(1)} %copy-done.5), channel_id=1, source_target_pairs={{0,16},{16,0},{1,17},{17,1},{2,18},{18,2},{3,19},{19,3},{4,20},{20... | collective-permute-start | bytes 1769480 | tf_op jit(solution)/shard_map/ppermute | solution.py:22
  246.5 24.1 %collective-permute-start.24 = (bf16[8,72,768]{2,1,0:T(8,128)(2,1)}, bf16[8,72,768]{2,1,0:T(8,128)(2,1)S(1)}, u32[]{:S(2)}, u32[]{:S(2)}) collective-permute-start(bf16[8,72,768]{2,1,0:T(8,128)(2,1)} %get-tuple-element.158), channel_id=1, source_target_pairs={{0,1},{1,0},{2,3},{3,2},{4,5},{5,4},{6,7},{7,6},{8,9},{9,8},{10,11... | collective-permute-start | bytes 2654216 | tf_op jit(solution)/shard_map/ppermute | solution.py:18
  247.5 23.1 %collective-permute-start.25 = (bf16[8,72,768]{2,1,0:T(8,128)(2,1)}, bf16[8,72,768]{2,1,0:T(8,128)(2,1)S(1)}, u32[]{:S(2)}, u32[]{:S(2)}) collective-permute-start(bf16[8,72,768]{2,1,0:T(8,128)(2,1)} %get-tuple-element.160), channel_id=1, source_target_pairs={{0,2},{1,3},{2,0},{3,1},{4,6},{5,7},{6,4},{7,5},{8,10},{9,11},{10,... | collective-permute-start | bytes 2654216 | tf_op jit(solution)/shard_map/ppermute | solution.py:18
  249.3 21.3 %collective-permute-start.26 = (bf16[8,72,768]{2,1,0:T(8,128)(2,1)}, bf16[8,72,768]{2,1,0:T(8,128)(2,1)S(1)}, u32[]{:S(2)}, u32[]{:S(2)}) collective-permute-start(bf16[8,72,768]{2,1,0:T(8,128)(2,1)} %get-tuple-element.162), channel_id=1, source_target_pairs={{0,4},{1,5},{2,6},{3,7},{4,0},{5,1},{6,2},{7,3},{8,12},{9,13},{10,... | collective-permute-start | bytes 2654216 | tf_op jit(solution)/shard_map/ppermute | solution.py:18
  270.5 9.2 %collective-permute-start.27 = (bf16[256,2304]{1,0:T(8,128)(2,1)}, bf16[256,2304]{1,0:T(8,128)(2,1)S(1)}, u32[]{:S(2)}, u32[]{:S(2)}) collective-permute-start(bf16[256,2304]{1,0:T(8,128)(2,1)} %get-tuple-element.166), channel_id=1, source_target_pairs={{0,16},{16,0},{1,17},{17,1},{2,18},{18,2},{3,19},{19,3},{4,20},{20... | collective-permute-start | bytes 3538952 | tf_op jit(solution)/shard_map/ppermute | solution.py:22
  276.6 13.9 %collective-permute-start.28 = (bf16[4,72,768]{2,1,0:T(8,128)(2,1)}, bf16[4,72,768]{2,1,0:T(8,128)(2,1)S(1)}, u32[]{:S(2)}, u32[]{:S(2)}) collective-permute-start(bf16[4,72,768]{2,1,0:T(8,128)(2,1)} %get-tuple-element.172), channel_id=1, source_target_pairs={{0,2},{1,3},{2,0},{3,1},{4,6},{5,7},{6,4},{7,5},{8,10},{9,11},{10,... | collective-permute-start | bytes 1327112 | tf_op jit(solution)/shard_map/ppermute | solution.py:18
  277.1 13.4 %collective-permute-start.29 = (bf16[4,72,768]{2,1,0:T(8,128)(2,1)}, bf16[4,72,768]{2,1,0:T(8,128)(2,1)S(1)}, u32[]{:S(2)}, u32[]{:S(2)}) collective-permute-start(bf16[4,72,768]{2,1,0:T(8,128)(2,1)} %get-tuple-element.173), channel_id=1, source_target_pairs={{0,4},{1,5},{2,6},{3,7},{4,0},{5,1},{6,2},{7,3},{8,12},{9,13},{10,... | collective-permute-start | bytes 1327112 | tf_op jit(solution)/shard_map/ppermute | solution.py:18
  278.6 12.3 %collective-permute-start.30 = (bf16[4,72,768]{2,1,0:T(8,128)(2,1)}, bf16[4,72,768]{2,1,0:T(8,128)(2,1)S(1)}, u32[]{:S(2)}, u32[]{:S(2)}) collective-permute-start(bf16[4,72,768]{2,1,0:T(8,128)(2,1)} %get-tuple-element.174), channel_id=1, source_target_pairs={{0,1},{1,0},{2,3},{3,2},{4,5},{5,4},{6,7},{7,6},{8,9},{9,8},{10,11... | collective-permute-start | bytes 1327112 | tf_op jit(solution)/shard_map/ppermute | solution.py:18
  304.6 21.3 %collective-permute-start.31 = (bf16[8,72,768]{2,1,0:T(8,128)(2,1)}, bf16[8,72,768]{2,1,0:T(8,128)(2,1)S(1)}, u32[]{:S(2)}, u32[]{:S(2)}) collective-permute-start(bf16[8,72,768]{2,1,0:T(8,128)(2,1)} %get-tuple-element.183), channel_id=1, source_target_pairs={{0,1},{1,0},{2,3},{3,2},{4,5},{5,4},{6,7},{7,6},{8,9},{9,8},{10,11... | collective-permute-start | bytes 2654216 | tf_op jit(solution)/shard_map/ppermute | solution.py:18
  305.5 21.2 %collective-permute-start.32 = (bf16[8,72,768]{2,1,0:T(8,128)(2,1)}, bf16[8,72,768]{2,1,0:T(8,128)(2,1)S(1)}, u32[]{:S(2)}, u32[]{:S(2)}) collective-permute-start(bf16[8,72,768]{2,1,0:T(8,128)(2,1)} %get-tuple-element.185), channel_id=1, source_target_pairs={{0,2},{1,3},{2,0},{3,1},{4,6},{5,7},{6,4},{7,5},{8,10},{9,11},{10,... | collective-permute-start | bytes 2654216 | tf_op jit(solution)/shard_map/ppermute | solution.py:18
  307.3 20.9 %collective-permute-start.33 = (bf16[8,72,768]{2,1,0:T(8,128)(2,1)}, bf16[8,72,768]{2,1,0:T(8,128)(2,1)S(1)}, u32[]{:S(2)}, u32[]{:S(2)}) collective-permute-start(bf16[8,72,768]{2,1,0:T(8,128)(2,1)} %get-tuple-element.187), channel_id=1, source_target_pairs={{0,4},{1,5},{2,6},{3,7},{4,0},{5,1},{6,2},{7,3},{8,12},{9,13},{10,... | collective-permute-start | bytes 2654216 | tf_op jit(solution)/shard_map/ppermute | solution.py:18
  320.2 15.9 %collective-permute-start.34 = (bf16[128,2304]{1,0:T(8,128)(2,1)}, bf16[128,2304]{1,0:T(8,128)(2,1)S(1)}, u32[]{:S(2)}, u32[]{:S(2)}) collective-permute-start(bf16[128,2304]{1,0:T(8,128)(2,1)} %get-tuple-element.180.top_ref), channel_id=1, source_target_pairs={{0,16},{16,0},{1,17},{17,1},{2,18},{18,2},{3,19},{19,3},{4,20},{20... | collective-permute-start | bytes 1769480 | tf_op jit(solution)/shard_map/ppermute | solution.py:22
  320.2 16.9 %collective-permute-start.35 = (bf16[128,2304]{1,0:T(8,128)(2,1)}, bf16[128,2304]{1,0:T(8,128)(2,1)S(1)}, u32[]{:S(2)}, u32[]{:S(2)}) collective-permute-start(bf16[128,2304]{1,0:T(8,128)(2,1)} %get-tuple-element.181.low_ref), channel_id=1, source_target_pairs={{0,16},{16,0},{1,17},{17,1},{2,18},{18,2},{3,19},{19,3},{4,20},{20... | collective-permute-start | bytes 1769480 | tf_op jit(solution)/shard_map/ppermute | solution.py:22
  333.7 14.4 %collective-permute-start.36 = (bf16[4,72,768]{2,1,0:T(8,128)(2,1)}, bf16[4,72,768]{2,1,0:T(8,128)(2,1)S(1)}, u32[]{:S(2)}, u32[]{:S(2)}) collective-permute-start(bf16[4,72,768]{2,1,0:T(8,128)(2,1)} %get-tuple-element.199), channel_id=1, source_target_pairs={{0,2},{1,3},{2,0},{3,1},{4,6},{5,7},{6,4},{7,5},{8,10},{9,11},{10,... | collective-permute-start | bytes 1327112 | tf_op jit(solution)/shard_map/ppermute | solution.py:18
  334.3 15.4 %collective-permute-start.37 = (bf16[4,72,768]{2,1,0:T(8,128)(2,1)}, bf16[4,72,768]{2,1,0:T(8,128)(2,1)S(1)}, u32[]{:S(2)}, u32[]{:S(2)}) collective-permute-start(bf16[4,72,768]{2,1,0:T(8,128)(2,1)} %get-tuple-element.200), channel_id=1, source_target_pairs={{0,4},{1,5},{2,6},{3,7},{4,0},{5,1},{6,2},{7,3},{8,12},{9,13},{10,... | collective-permute-start | bytes 1327112 | tf_op jit(solution)/shard_map/ppermute | solution.py:18
  334.5 15.1 %collective-permute-start.38 = (bf16[4,72,768]{2,1,0:T(8,128)(2,1)}, bf16[4,72,768]{2,1,0:T(8,128)(2,1)S(1)}, u32[]{:S(2)}, u32[]{:S(2)}) collective-permute-start(bf16[4,72,768]{2,1,0:T(8,128)(2,1)} %get-tuple-element.201), channel_id=1, source_target_pairs={{0,1},{1,0},{2,3},{3,2},{4,5},{5,4},{6,7},{7,6},{8,9},{9,8},{10,11... | collective-permute-start | bytes 1327112 | tf_op jit(solution)/shard_map/ppermute | solution.py:18
  336.1 18.6 %collective-permute-start.40 = (bf16[2,72,768]{2,1,0:T(8,128)(2,1)S(1)}, bf16[2,72,768]{2,1,0:T(8,128)(2,1)S(1)}, u32[]{:S(2)}, u32[]{:S(2)}) collective-permute-start(bf16[2,72,768]{2,1,0:T(8,128)(2,1)S(1)} %copy-done.76), channel_id=1, source_target_pairs={{0,4},{1,5},{2,6},{3,7},{4,0},{5,1},{6,2},{7,3},{8,12},{9,13},{10,... | collective-permute-start | bytes 663560 | tf_op jit(solution)/shard_map/ppermute | solution.py:18
  337.1 20.4 %collective-permute-start.41 = (bf16[2,72,768]{2,1,0:T(8,128)(2,1)S(1)}, bf16[2,72,768]{2,1,0:T(8,128)(2,1)S(1)}, u32[]{:S(2)}, u32[]{:S(2)}) collective-permute-start(bf16[2,72,768]{2,1,0:T(8,128)(2,1)S(1)} %copy-done.75), channel_id=1, source_target_pairs={{0,1},{1,0},{2,3},{3,2},{4,5},{5,4},{6,7},{7,6},{8,9},{9,8},{10,11... | collective-permute-start | bytes 663560 | tf_op jit(solution)/shard_map/ppermute | solution.py:18
  348.1 11.7 %collective-permute-start.42 = (bf16[2,72,768]{2,1,0:T(8,128)(2,1)S(1)}, bf16[2,72,768]{2,1,0:T(8,128)(2,1)S(1)}, u32[]{:S(2)}, u32[]{:S(2)}) collective-permute-start(bf16[2,72,768]{2,1,0:T(8,128)(2,1)S(1)} %copy-done.74), channel_id=1, source_target_pairs={{0,2},{1,3},{2,0},{3,1},{4,6},{5,7},{6,4},{7,5},{8,10},{9,11},{10,... | collective-permute-start | bytes 663560 | tf_op jit(solution)/shard_map/ppermute | solution.py:18
  353.5 7.5 %collective-permute-start.43 = (bf16[2,72,768]{2,1,0:T(8,128)(2,1)}, bf16[2,72,768]{2,1,0:T(8,128)(2,1)S(1)}, u32[]{:S(2)}, u32[]{:S(2)}) collective-permute-start(bf16[2,72,768]{2,1,0:T(8,128)(2,1)} %get-tuple-element.208), channel_id=1, source_target_pairs={{0,4},{1,5},{2,6},{3,7},{4,0},{5,1},{6,2},{7,3},{8,12},{9,13},{10,... | collective-permute-start | bytes 663560 | tf_op jit(solution)/shard_map/ppermute | solution.py:18
  353.8 7.3 %collective-permute-start.44 = (bf16[2,72,768]{2,1,0:T(8,128)(2,1)}, bf16[2,72,768]{2,1,0:T(8,128)(2,1)S(1)}, u32[]{:S(2)}, u32[]{:S(2)}) collective-permute-start(bf16[2,72,768]{2,1,0:T(8,128)(2,1)} %get-tuple-element.209), channel_id=1, source_target_pairs={{0,1},{1,0},{2,3},{3,2},{4,5},{5,4},{6,7},{7,6},{8,9},{9,8},{10,11... | collective-permute-start | bytes 663560 | tf_op jit(solution)/shard_map/ppermute | solution.py:18
  354.8 6.3 %collective-permute-start.45 = (bf16[2,72,768]{2,1,0:T(8,128)(2,1)}, bf16[2,72,768]{2,1,0:T(8,128)(2,1)S(1)}, u32[]{:S(2)}, u32[]{:S(2)}) collective-permute-start(bf16[2,72,768]{2,1,0:T(8,128)(2,1)} %get-tuple-element.210), channel_id=1, source_target_pairs={{0,2},{1,3},{2,0},{3,1},{4,6},{5,7},{6,4},{7,5},{8,10},{9,11},{10,... | collective-permute-start | bytes 663560 | tf_op jit(solution)/shard_map/ppermute | solution.py:18
  357.5 8.3 %collective-permute-start.39 = (f32[256,128]{1,0:T(8,128)}, f32[256,128]{1,0:T(8,128)S(1)}, u32[]{:S(2)}, u32[]{:S(2)}) collective-permute-start(f32[256,128]{1,0:T(8,128)} %pack.1.refs_12_.v_ref), channel_id=1, source_target_pairs={{0,8},{1,9},{2,10},{3,11},{4,12},{5,13},{6,14},{7,15},{8,0},{9,1},... | collective-permute-start | bytes 393224 | tf_op jit(solution)/shard_map/ppermute | solution.py:18
  368.2 6.5 %collective-permute-start.46 = (f32[312,128]{1,0:T(8,128)}, f32[312,128]{1,0:T(8,128)S(1)}, u32[]{:S(2)}, u32[]{:S(2)}) collective-permute-start(f32[312,128]{1,0:T(8,128)} %meet.4.v_ref), channel_id=1, source_target_pairs={{0,4},{1,5},{2,6},{3,7},{4,0},{5,1},{6,2},{7,3},{8,12},{9,13},{10,... | collective-permute-start | bytes 479240 | tf_op jit(solution)/shard_map/ppermute | solution.py:18
  368.8 28.9 %collective-permute-start.52 = (bf16[1,72,4608]{2,1,0:T(8,128)(2,1)}, bf16[1,72,4608]{2,1,0:T(8,128)(2,1)S(1)}, u32[]{:S(2)}, u32[]{:S(2)}) collective-permute-start(bf16[1,72,4608]{2,1,0:T(8,128)(2,1)} %get-tuple-element.219), channel_id=1, source_target_pairs={{0,8},{1,9},{2,10},{3,11},{4,12},{5,13},{6,14},{7,15},{8,0},{9,1},... | collective-permute-start | bytes 1990664 | tf_op jit(solution)/shard_map/ppermute | solution.py:18
  377.0 11.3 %collective-permute-start.47 = (f32[424,128]{1,0:T(8,128)}, f32[424,128]{1,0:T(8,128)S(1)}, u32[]{:S(2)}, u32[]{:S(2)}) collective-permute-start(f32[424,128]{1,0:T(8,128)} %meet.5.rest_3_.v_ref), channel_id=1, source_target_pairs={{0,2},{1,3},{2,0},{3,1},{4,6},{5,7},{6,4},{7,5},{8,10},{9,11},{10,... | collective-permute-start | bytes 651272 | tf_op jit(solution)/shard_map/ppermute | solution.py:18
  390.7 10.9 %collective-permute-start.48 = (f32[648,128]{1,0:T(8,128)}, f32[648,128]{1,0:T(8,128)S(1)}, u32[]{:S(2)}, u32[]{:S(2)}) collective-permute-start(f32[648,128]{1,0:T(8,128)} %meet.6.v_ref), channel_id=1, source_target_pairs={{0,1},{1,0},{2,3},{3,2},{4,5},{5,4},{6,7},{7,6},{8,9},{9,8},{10,11... | collective-permute-start | bytes 995336 | tf_op jit(solution)/shard_map/ppermute | solution.py:18
  391.6 22.5 %collective-permute-start.49 = (bf16[8,72,768]{2,1,0:T(8,128)(2,1)}, bf16[8,72,768]{2,1,0:T(8,128)(2,1)S(1)}, u32[]{:S(2)}, u32[]{:S(2)}) collective-permute-start(bf16[8,72,768]{2,1,0:T(8,128)(2,1)} %get-tuple-element.214), channel_id=1, source_target_pairs={{0,1},{1,0},{2,3},{3,2},{4,5},{5,4},{6,7},{7,6},{8,9},{9,8},{10,11... | collective-permute-start | bytes 2654216 | tf_op jit(solution)/shard_map/ppermute | solution.py:18
  392.8 21.3 %collective-permute-start.50 = (bf16[8,72,768]{2,1,0:T(8,128)(2,1)}, bf16[8,72,768]{2,1,0:T(8,128)(2,1)S(1)}, u32[]{:S(2)}, u32[]{:S(2)}) collective-permute-start(bf16[8,72,768]{2,1,0:T(8,128)(2,1)} %get-tuple-element.216), channel_id=1, source_target_pairs={{0,2},{1,3},{2,0},{3,1},{4,6},{5,7},{6,4},{7,5},{8,10},{9,11},{10,... | collective-permute-start | bytes 2654216 | tf_op jit(solution)/shard_map/ppermute | solution.py:18
  394.8 21.8 %collective-permute-start.51 = (bf16[8,72,768]{2,1,0:T(8,128)(2,1)S(1)}, bf16[8,72,768]{2,1,0:T(8,128)(2,1)S(1)}, u32[]{:S(2)}, u32[]{:S(2)}) collective-permute-start(bf16[8,72,768]{2,1,0:T(8,128)(2,1)S(1)} %copy-done.72), channel_id=1, source_target_pairs={{0,4},{1,5},{2,6},{3,7},{4,0},{5,1},{6,2},{7,3},{8,12},{9,13},{10,... | collective-permute-start | bytes 2654216 | tf_op jit(solution)/shard_map/ppermute | solution.py:18
  401.0 31.7 %collective-permute-start.56 = (f32[72,4608]{1,0:T(8,128)}, f32[72,4608]{1,0:T(8,128)}, u32[]{:S(2)}, u32[]{:S(2)}) collective-permute-start(f32[72,4608]{1,0:T(8,128)} %finish.2.refs_7_.own_ref), channel_id=1, source_target_pairs={{0,16},{16,0},{1,17},{17,1},{2,18},{18,2},{3,19},{19,3},{4,20},{20... | collective-permute-start | bytes 3981320 | tf_op jit(solution)/shard_map/ppermute | solution.py:22
  404.4 19.4 %collective-permute-start.60 = (f32[1096,128]{1,0:T(8,128)}, f32[1096,128]{1,0:T(8,128)S(1)}, u32[]{:S(2)}, u32[]{:S(2)}) collective-permute-start(f32[1096,128]{1,0:T(8,128)} %meet.7.refs_6_), channel_id=1, source_target_pairs={{0,16},{16,0},{1,17},{17,1},{2,18},{18,2},{3,19},{19,3},{4,20},{20... | collective-permute-start | bytes 1683464 | tf_op jit(solution)/shard_map/ppermute | solution.py:22
  421.9 13.7 %collective-permute-start.53 = (bf16[4,72,768]{2,1,0:T(8,128)(2,1)}, bf16[4,72,768]{2,1,0:T(8,128)(2,1)}, u32[]{:S(2)}, u32[]{:S(2)}) collective-permute-start(bf16[4,72,768]{2,1,0:T(8,128)(2,1)} %get-tuple-element.221), channel_id=1, source_target_pairs={{0,2},{1,3},{2,0},{3,1},{4,6},{5,7},{6,4},{7,5},{8,10},{9,11},{10,... | collective-permute-start | bytes 1327112 | tf_op jit(solution)/shard_map/ppermute | solution.py:18
  422.8 12.9 %collective-permute-start.54 = (bf16[4,72,768]{2,1,0:T(8,128)(2,1)}, bf16[4,72,768]{2,1,0:T(8,128)(2,1)}, u32[]{:S(2)}, u32[]{:S(2)}) collective-permute-start(bf16[4,72,768]{2,1,0:T(8,128)(2,1)} %get-tuple-element.223), channel_id=1, source_target_pairs={{0,4},{1,5},{2,6},{3,7},{4,0},{5,1},{6,2},{7,3},{8,12},{9,13},{10,... | collective-permute-start | bytes 1327112 | tf_op jit(solution)/shard_map/ppermute | solution.py:18
  422.8 12.9 %collective-permute-start.55 = (bf16[4,72,768]{2,1,0:T(8,128)(2,1)}, bf16[4,72,768]{2,1,0:T(8,128)(2,1)}, u32[]{:S(2)}, u32[]{:S(2)}) collective-permute-start(bf16[4,72,768]{2,1,0:T(8,128)(2,1)} %get-tuple-element.225), channel_id=1, source_target_pairs={{0,1},{1,0},{2,3},{3,2},{4,5},{5,4},{6,7},{7,6},{8,9},{9,8},{10,11... | collective-permute-start | bytes 1327112 | tf_op jit(solution)/shard_map/ppermute | solution.py:18
  438.6 6.9 %collective-permute-start.57 = (bf16[2,72,768]{2,1,0:T(8,128)(2,1)}, bf16[2,72,768]{2,1,0:T(8,128)(2,1)S(1)}, u32[]{:S(2)}, u32[]{:S(2)}) collective-permute-start(bf16[2,72,768]{2,1,0:T(8,128)(2,1)} %get-tuple-element.227), channel_id=1, source_target_pairs={{0,4},{1,5},{2,6},{3,7},{4,0},{5,1},{6,2},{7,3},{8,12},{9,13},{10,... | collective-permute-start | bytes 663560 | tf_op jit(solution)/shard_map/ppermute | solution.py:18
  440.7 6.4 %collective-permute-start.58 = (bf16[2,72,768]{2,1,0:T(8,128)(2,1)}, bf16[2,72,768]{2,1,0:T(8,128)(2,1)S(1)}, u32[]{:S(2)}, u32[]{:S(2)}) collective-permute-start(bf16[2,72,768]{2,1,0:T(8,128)(2,1)} %get-tuple-element.229), channel_id=1, source_target_pairs={{0,1},{1,0},{2,3},{3,2},{4,5},{5,4},{6,7},{7,6},{8,9},{9,8},{10,11... | collective-permute-start | bytes 663560 | tf_op jit(solution)/shard_map/ppermute | solution.py:18
  441.7 6.2 %collective-permute-start.59 = (bf16[2,72,768]{2,1,0:T(8,128)(2,1)}, bf16[2,72,768]{2,1,0:T(8,128)(2,1)S(1)}, u32[]{:S(2)}, u32[]{:S(2)}) collective-permute-start(bf16[2,72,768]{2,1,0:T(8,128)(2,1)} %get-tuple-element.231), channel_id=1, source_target_pairs={{0,2},{1,3},{2,0},{3,1},{4,6},{5,7},{6,4},{7,5},{8,10},{9,11},{10,... | collective-permute-start | bytes 663560 | tf_op jit(solution)/shard_map/ppermute | solution.py:18
  450.9 16.9 %collective-permute-start.61 = (bf16[1,72,2304]{2,1,0:T(8,128)(2,1)}, bf16[1,72,2304]{2,1,0:T(8,128)(2,1)S(1)}, u32[]{:S(2)}, u32[]{:S(2)}) collective-permute-start(bf16[1,72,2304]{2,1,0:T(8,128)(2,1)} %get-tuple-element.233), channel_id=1, source_target_pairs={{0,8},{1,9},{2,10},{3,11},{4,12},{5,13},{6,14},{7,15},{8,0},{9,1},... | collective-permute-start | bytes 995336 | tf_op jit(solution)/shard_map/ppermute | solution.py:18
  453.2 13.9 %all-to-all-start.2 = ((f32[16,1,72]{2,1,0:T(1,128)}), f32[16,1,72]{2,1,0:T(1,128)S(1)}, u32[]{:S(2)}, u32[]{:S(2)}) async-start(f32[16,1,72]{2,1,0:T(1,128)} %bitcast.113), calls=%async_computation.2 | async-start | bytes 16384 | tf_op jit(solution)/shard_map/all_to_all | solution.py:45
  (79 other events, 412.4 us)

commit v2 on v1

--- a/solution.py
+++ b/solution.py
@@ -411,64 +411,63 @@
     return outs, small_result, large_on
 
 
-def product_kernel(n, firsts, steps, half_step, count, chip_ref, l0_ref, l1_ref, *rest):
-    turned_ref = rest[-1]
-    r_refs = rest[:count]
-    outs = rest[-7:-1]
-    t = pl.program_id(0)
+def product_kernel(n, firsts, two_l, two_r, count, chip_ref, l0_ref, l1_ref, *rest):
+    r_refs, outs, (turned_ref, buf_ref, sem) = rest[:count], rest[-9:-3], rest[-3:]
     length = l0_ref.shape[0]
     width = turned_ref.shape[1]
     rows = width // n
-
-    @pl.when(t == 0)
-    def _():
-        for k in range(turned_ref.shape[0]):
-            cols = slice(k * width, (k + 1) * width)
-            turned_ref[k, :, 0:length] = l0_ref[:, cols].T
-            turned_ref[k, :, length:] = l1_ref[:, cols].T
-
-    slot = jnp.where(t >= half_step, turned_ref.shape[0] - 1, 0)
-    value, at = 0.0, 0
-    for r_ref in r_refs:
-        rows_here = r_ref.shape[0]
-        value = value + mm(turned_ref[slot, :, at : at + rows_here], r_ref[...])
-        at += rows_here
-    for part, (bit, (lo, hi)) in enumerate(zip(firsts, steps)):
-        pos = bit.bit_length() - 1
-        for up in range(2):
-
-            @pl.when((t >= lo) & (t < hi) & ((chip_ref[0] & bit) // bit == up))
-            def _():
-                for i in range(n // 2):
-                    at = put(i, pos)
-                    for goes, ref in ((up, outs[2 * part]), (1 - up, outs[2 * part + 1])):
-                        k = at + goes * bit
-                        ref[i] = value[k * rows : (k + 1) * rows].astype(BF)
+    tile = width // 3
+    for k in range(turned_ref.shape[0]):
+        cols = slice(k * width, (k + 1) * width)
+        turned_ref[k, :, 0:length] = l0_ref[:, cols].T
+        turned_ref[k, :, length:] = l1_ref[:, cols].T
+
+    def times(slot, lo, w):
+        total, at = None, 0
+        for r_ref in r_refs:
+            m = r_ref.shape[0]
+            term = mm(turned_ref[slot, :, at : at + m], r_ref[:, lo : lo + w])
+            total = term if total is None else total + term
+            at += m
+        return total
+
+    copies = []
+    for t, bit in enumerate(firsts):
+        (s0, c0), (s1, c1) = (
+            (q // 3 if two_l else 0, (q if two_r else q % 3) * tile) for q in (2 * t, 2 * t + 1)
+        )
+        if s0 == s1 and c1 == c0 + tile:
+            value = times(s0, c0, 2 * tile)
+        else:
+            value = jnp.concatenate([times(s0, c0, tile), times(s1, c1, tile)], axis=1)
+        up = (chip_ref[0] & bit) // bit
+        for k in range(n):
+            at = (k // (2 * bit)) * bit + k % bit
+            goes = 1 - up if k & bit else up
+            buf_ref[t, goes, at] = value[k * rows : (k + 1) * rows].astype(BF)
+        for goes in range(2):
+            copy = pltpu.make_async_copy(buf_ref.at[t, goes], outs[2 * t + goes], sem.at[2 * t + goes])
+            copy.start()
+            copies.append(copy)
+    for copy in copies:
+        copy.wait()
 
 
 def product(chip, l0, l1, r0, r1, width, n, firsts, after=()):
     length = l0.shape[0]
-    tile = width // 3
-    per = width // tile
     rights = (r0,) + (r1 if isinstance(r1, tuple) else (r1,))
     two_l, two_r = l0.shape[1] > width, r0.shape[1] > width
-    cols = (2 * width // 3,) * 3
-    steps = []
-    for c in cols:
-        lo = steps[-1][1] if steps else 0
-        steps.append((lo, lo + c // tile))
-    left = pl.BlockSpec(l0.shape, lambda t: (0, 0))
-    right = [pl.BlockSpec((r.shape[0], tile), lambda t: (0, t if two_r else t % per)) for r in rights]
-    spec = lambda lo, hi: pl.BlockSpec(
-        (n // 2, width // n, tile), lambda t: (0, 0, jnp.clip(t - lo, 0, hi - lo - 1))
-    )
+    block = (n // 2, width // n, 2 * width // 3)
     out = pl.pallas_call(
-        functools.partial(product_kernel, n, firsts, steps, per, len(rights)),
-        grid=(2 * per,),
-        out_shape=tuple(shape((n // 2, width // n, c), BF) for c in cols for _ in range(2)),
-        in_specs=[SCALAR, left, left] + right + [HBM] * len(after),
-        out_specs=tuple(spec(*s) for s in steps for _ in range(2)),
-        scratch_shapes=[pltpu.VMEM((1 + two_l, width, 2 * length), BF)],
+        functools.partial(product_kernel, n, firsts, two_l, two_r, len(rights)),
+        out_shape=(shape(block, BF),) * 6,
+        in_specs=[SCALAR] + [WHOLE] * (2 + len(rights)) + [HBM] * len(after),
+        out_specs=(HBM,) * 6,
+        scratch_shapes=[
+            pltpu.VMEM((1 + two_l, width, 2 * length), BF),
+            pltpu.VMEM((3, 2) + block, BF),
+            pltpu.SemaphoreType.DMA((6,)),
+        ],
         compiler_params=params(),
         cost_estimate=cost(8 * length * width * width, 12e6),
         name="product",

time: 483 us -> 476 us (0.986)
  Pallas kernels: 223 us -> 213 us
    pallas_call x3, Pallas kernels: 31.7 us -> 21.2 us  [product(): pl.pallas_call(functools.partial(product_kernel, n, firsts, two_l, two_r,...]
  transfers between devices with their start and end apart: 66 -> 66, of which waited for: 28 -> 27; matrix products, arithmetic and copies ran while one was open for 9% -> 9% of each run, Pallas kernels for 33% -> 32%
where the time goes in v2:
time: 476 us; the launch traced here: 470 us
  Pallas kernels  213 us (45%)
  waiting for transfers between devices  116 us (24%)
  starting transfers between devices  75.8 us (16%)
  local copies, waits for them, and re-layouts  47.7 us (10%)
  other arithmetic  8.58 us (2%)
  matrix products  6.91 us (1%)
    ppermute x50, waiting for transfers between devices, swap(): return lax.ppermute(v, 'dp', [(i, i ^ bit) for i in range(n)])  86 us
    ppermute x50, starting transfers between devices, swap(): return lax.ppermute(v, 'dp', [(i, i ^ bit) for i in range(n)])  58.9 us
    pallas_call x8, Pallas kernels, split(): pl.pallas_call(functools.partial(split_kernel, plan), out_shape=tuple(out...  28.3 us
    pallas_call x1, Pallas kernels, attention(): pl.pallas_call(attention_kernel, out_shape=(per_head, per_head, per_head,...  27.1 us
    unnamed x159, local copies, waits for them, and re-layouts  25.1 us
    pallas_call x2, Pallas kernels, mlp(): pl.pallas_call(mlp_last_kernel if last else mlp_first_kernel, grid=(half...  21.8 us
    pallas_call x3, Pallas kernels, product(): pl.pallas_call(functools.partial(product_kernel, n, firsts, two_l, two_r,...  21.2 us
    pallas_call x1, Pallas kernels, mlp_back(): pl.pallas_call(mlp_back_kernel, grid=(half // tile,), out_shape=(shape((l...  19.7 us
  transfers between devices with their start and end apart: 66, of which 27 were waited for; matrix products, arithmetic and copies ran while one was open for 9% of the time, Pallas kernels for 32%

profile of v2, /device:TPU:0, one launch (start us, length us, event | category | flops | bytes accessed | tf_op | source)
XLA Modules:
  0.0 469.7 jit_solution(6809507497979854062)
XLA Ops:
  0.7 1.9 attn_shard.1.rest_0_.refs_1_.refs_0_
  2.6 4.0 collective-permute-start
  10.7 4.8 %all-to-all-start = ((bf16[16,2,576]{2,1,0:T(2,128)(2,1)}), bf16[16,2,576]{2,1,0:T(2,128)(2,1)S(1)}, u32[]{:S(2)}, u32[]{:S(2)}) async-start(bf16[16,2,576]{2,1,0:T(2,128)(2,1)} %reshape.250), calls=%async_computation | async-start | bytes 81920 | tf_op jit(solution)/shard_map/all_to_all | solution.py:45
  21.6 2.5 mlp_shard.1.refs_2_.refs_0_
  24.1 2.0 bias_strip.1.refs_3_.strip_ref
  27.6 1.9 join.3
  29.5 1.9 collective-permute-start.1
  34.4 2.4 collective-permute-start.7
  39.8 2.5 join.4
  42.3 1.8 collective-permute-start.4
  44.6 2.7 collective-permute-start.6
  48.5 16.3 %collective-permute-done.7.refs_7_ = bf16[1,72,4608]{2,1,0:T(8,128)(2,1)S(1)} collective-permute-done((bf16[1,72,4608]{2,1,0:T(8,128)(2,1)}, bf16[1,72,4608]{2,1,0:T(8,128)(2,1)S(1)}, u32[]{:S(2)}, u32[]{:S(2)}) %collective-permute-start.7) | collective-permute-done | bytes 663584 | tf_op jit(solution)/shard_map/ppermute | solution.py:18
  66.9 4.3 merge.1
  72.9 27.9 %collective-permute-done.10.refs_5_.refs_3_ = bf16[12,72,768]{2,1,0:T(8,128)(2,1)S(1)} collective-permute-done((bf16[12,72,768]{2,1,0:T(8,128)(2,1)}, bf16[12,72,768]{2,1,0:T(8,128)(2,1)S(1)}, u32[]{:S(2)}, u32[]{:S(2)}) %collective-permute-start.10) | collective-permute-done | bytes 1327136 | tf_op jit(solution)/shard_map/ppermute | solution.py:18
  103.4 4.9 %cross.1 = (bf16[4,72,1536]{2,1,0:T(8,128)(2,1)}, bf16[4,72,1536]{2,1,0:T(8,128)(2,1)}, bf16[4,72,1536]{2,1,0:T(8,128)(2,1)}) custom-call(s32[1]{0:T(128)} %bitcast.1.chip_ref, bf16[12,72,768]{2,1,0:T(8,128)(2,1)} %get-tuple-element.133.refs_0_.refs_4_, bf16[12,72,768]{2,1,0:T(8,128)(2,1)} %copy-done.3, ...), custom_call_target="tpu_custom_call" | custom-call | tf_op jit(solution)/shard_map/cross/pallas_call | solution.py:398
  108.3 6.1 %assemble.2 = bf16[16,72,2304]{2,1,0:T(8,128)(2,1)} custom-call(s32[1]{0:T(128)} %bitcast.1.chip_ref, bf16[12,72,768]{2,1,0:T(8,128)(2,1)} %get-tuple-element.131.refs_2_.refs_0_, bf16[12,72,768]{2,1,0:T(8,128)(2,1)} %copy-done.4, bf16[12,72,768]{2,1,0:T(8,128)(2,1)} %get-tuple-element.132.refs_4_.refs_2_, bf16[12,72,768]{2,1,0:T(8,128)(2,1)} %copy-done.2, ...), custom_call_target="tpu_custom_call" | custom-call | tf_op jit(solution)/shard_map/assemble/pallas_call | solution.py:297
  117.8 2.3 copy.77
  120.1 5.7 %all-to-all-start.1 = ((f32[16,1,6912]{2,1,0:T(1,128)}), f32[16,1,6912]{2,1,0:T(1,128)S(1)}, u32[]{:S(2)}, u32[]{:S(2)}) async-start(f32[16,1,6912]{2,1,0:T(1,128)} %copy.77), calls=%async_computation.1 | async-start | bytes 884736 | tf_op jit(solution)/shard_map/all_to_all | solution.py:45
  130.1 15.6 %all-to-all-done.1 = f32[16,1,6912]{2,1,0:T(1,128)S(1)} async-done(((f32[16,1,6912]{2,1,0:T(1,128)}), f32[16,1,6912]{2,1,0:T(1,128)S(1)}, u32[]{:S(2)}, u32[]{:S(2)}) %all-to-all-start.1) | async-done | bytes 442400 | tf_op jit(solution)/shard_map/all_to_all | solution.py:45
  146.5 5.2 %join.5 = (bf16[8,72,1536]{2,1,0:T(8,128)(2,1)}, bf16[8,72,1536]{2,1,0:T(8,128)(2,1)}, bf16[8,72,1536]{2,1,0:T(8,128)(2,1)}) custom-call(s32[1]{0:T(128)} %bitcast.1.chip_ref, bf16[4,72,1536]{2,1,0:T(8,128)(2,1)} %get-tuple-element.134.refs_6_.refs_0_, bf16[4,72,1536]{2,1,0:T(8,128)(2,1)} %collective-permute-done.13.refs_1_, ...), custom_call_target="tpu_custom_call" | custom-call | tf_op jit(solution)/shard_map/join/pallas_call | solution.py:264
  157.9 27.1 %attention.1 = (bf16[16,256,72]{2,1,0:T(8,128)(2,1)}, bf16[16,256,72]{2,1,0:T(8,128)(2,1)}, bf16[16,256,72]{2,1,0:T(8,128)(2,1)}, bf16[256,2304]{1,0:T(8,128)(2,...) custom-call(s32[1]{0:T(128)} %bitcast.side_ref, ...), custom_call_target="tpu_custom_call" | custom-call | flops 3019898880 | bytes 24000000 | tf_op jit(solution)/shard_map/attention/pallas_call | solution.py:807
  185.0 6.7 %collective-permute-done.16.refs_1_ = bf16[8,72,1536]{2,1,0:T(8,128)(2,1)} collective-permute-done((bf16[8,72,1536]{2,1,0:T(8,128)(2,1)}, bf16[8,72,1536]{2,1,0:T(8,128)(2,1)}, u32[]{:S(2)}, u32[]{:S(2)}) %collective-permute-start.16) | collective-permute-done | bytes 1769504 | tf_op jit(solution)/shard_map/ppermute | solution.py:18
  192.4 8.7 %assemble.3 = bf16[16,72,4608]{2,1,0:T(8,128)(2,1)} custom-call(s32[1]{0:T(128)} %bitcast.1.chip_ref, bf16[8,72,1536]{2,1,0:T(8,128)(2,1)} %get-tuple-element.138.refs_0_, bf16[8,72,1536]{2,1,0:T(8,128)(2,1)} %collective-permute-done.16.refs_1_, bf16[8,72,1536]{2,1,0:T(8,128)(2,1)} %get-tuple-element.139.refs_2_, ...), custom_call_target="tpu_custom_call" | custom-call | tf_op jit(solution)/shard_map/assemble/pallas_call | solution.py:297
  201.1 10.0 %mlp.2 = (bf16[256,2304]{1,0:T(8,128)(2,1)}, f32[256,2304]{1,0:T(8,128)}, f32[256,1152]{1,0:T(8,128)}) custom-call(bf16[256,1152]{1,0:T(8,128)(2,1)} %get-tuple-element.137.refs_6_.normed_two_ref.l0_ref, bf16[1152,4608]{1,0:T(8,128)(2,1)} %bitcast.86, bf16[1152,4608]{1,0:T(8,128)(2,1)} %bitcast.87, bf16[1152,4608]{1,0:T(8,128)(2,1)} %bitcast.88, ...), custom_call_target="tpu_custom_call" | custom-call | flops 2717908992 | bytes 16000000 | tf_op jit(solution)/shard_map/mlp/pallas_call | solution.py:920
  211.1 6.7 %collective-permute-done.19.b_ref.c0_ref.c1_ref.b1_ref.c10_ref.c11_ref = bf16[1152,4608]{1,0:T(8,128)(2,1)} collective-permute-done((bf16[1152,4608]{1,0:T(8,128)(2,1)}, bf16[1152,4608]{1,0:T(8,128)(2,1)}, u32[]{:S(2)}, u32[]{:S(2)}) %collective-permute-start.19) | collective-permute-done | bytes 10616864 | tf_op jit(solution)/shard_map/ppermute | solution.py:22
  217.8 11.8 %mlp.3 = (bf16[256,2304]{1,0:T(8,128)(2,1)}, f32[256,2304]{1,0:T(8,128)}, bf16[256,1152]{1,0:T(8,128)(2,1)}, bf16[256,1152]{1,0:T(8,128)(2,1)}, f32[8,1152]{1,0:T(8,128)}) custom-call(bf16[256,1152]{1,0:T(8,128)(2,1)} %get-tuple-element.137.refs_6_.normed_two_ref.l0_ref, ...), custom_call_target="tpu_custom_call" | custom-call | flops 2717908992 | bytes 16000000 | tf_op jit(solution)/shard_map/mlp/pallas_call | solution.py:920
  230.7 4.0 collective-permute-done.21.rest_1_
  235.9 6.7 %product.3 = (bf16[8,72,768]{2,1,0:T(8,128)(2,1)}, bf16[8,72,768]{2,1,0:T(8,128)(2,1)}, bf16[8,72,768]{2,1,0:T(8,128)(2,1)}, bf16[8,72,768]{2,1,0:T(8,128)(2,1)}...) custom-call(s32[1]{0:T(128)} %bitcast.1.chip_ref, bf16[256,2304]{1,0:T(8,128)(2,1)} %get-tuple-element.152.l0_ref, ...), custom_call_target="tpu_custom_call" | custom-call | flops 2717908992 | bytes 12000000 | tf_op jit(solution)/shard_map/product/pallas_call | solution.py:461
  243.6 1.8 collective-permute-start.25
  246.9 19.7 %mlp_back.1 = (bf16[256,2304]{1,0:T(8,128)(2,1)}, bf16[256,2304]{1,0:T(8,128)(2,1)}, f32[2,2304]{1,0:T(2,128)}, f32[256,1152]{1,0:T(8,128)}, bf16[256,1152]{1,0:...) custom-call(bf16[256,1152]{1,0:T(8,128)(2,1)} %get-tuple-element.147.rest_0_.g_branch_ref, ...), custom_call_target="tpu_custom_call" | custom-call | flops 5435817984 | bytes 32000000 | tf_op jit(solution)/shard_map/mlp_back/pallas_call | solution.py:998
  268.2 4.5 split.8
  276.8 9.9 %first_heads.1 = (bf16[8,256,72]{2,1,0:T(8,128)(2,1)}, bf16[8,256,72]{2,1,0:T(8,128)(2,1)}, bf16[8,256,72]{2,1,0:T(8,128)(2,1)}, f32[8,16,512]{2,1,0:T(8,128)}) custom-call(bf16[16,256,72]{2,1,0:T(8,128)(2,1)} %get-tuple-element.144.qh_ref, bf16[16,256,72]{2,1,0:T(8,128)(2,1)} %get-tuple-element.145.kh_ref, bf16[16,256,72]{2,1,0:T(8,128)(2,1)} %get-tuple-element.146.vh_ref, ...), custom_call_target="tpu_custom_call" | custom-call | flops 377487360 | bytes 16000000 | tf_op jit(solution)/shard_map/first_heads/pallas_call | solution.py:1098
  287.9 3.0 split.9
  290.9 6.3 %product.4 = (bf16[8,72,768]{2,1,0:T(8,128)(2,1)}, bf16[8,72,768]{2,1,0:T(8,128)(2,1)}, bf16[8,72,768]{2,1,0:T(8,128)(2,1)}, bf16[8,72,768]{2,1,0:T(8,128)(2,1)}...) custom-call(s32[1]{0:T(128)} %bitcast.1.chip_ref, ...), custom_call_target="tpu_custom_call" | custom-call | flops 2717908992 | bytes 12000000 | tf_op jit(solution)/shard_map/product/pallas_call | solution.py:461
  298.2 1.8 collective-permute-start.32
  300.2 12.8 %last_heads.1 = (bf16[256,2304]{1,0:T(8,128)(2,1)}, bf16[128,2304]{1,0:T(8,128)(2,1)}, bf16[128,2304]{1,0:T(8,128)(2,1)}, f32[16,512]{1,0:T(8,128)}, f32[16,512]{1,0:T(8,128)}, /*index=5*/f32[8,1152]{1,0:T(8,128)}) custom-call(s32[1]{0:T(128)} %bitcast.side_ref, bf16[16,256,72]{2,1,0:T(8,128)(2,1)} %get-tuple-element.144.qh_ref, ...), custom_call_target="tpu_custom_call" | custom-call | flops 377487360 | bytes 16000000 | tf_op jit(solution)/shard_map/last_heads/pallas_call | solution.py:1173
  313.6 5.0 %collective-permute-done.31.refs_1_ = bf16[8,72,768]{2,1,0:T(8,128)(2,1)S(1)} collective-permute-done((bf16[8,72,768]{2,1,0:T(8,128)(2,1)}, bf16[8,72,768]{2,1,0:T(8,128)(2,1)S(1)}, u32[]{:S(2)}, u32[]{:S(2)}) %collective-permute-start.31) | collective-permute-done | bytes 884768 | tf_op jit(solution)/shard_map/ppermute | solution.py:18
  321.8 4.7 split.10
  331.2 9.6 %tokens_back.1 = (bf16[256,1152]{1,0:T(8,128)(2,1)}, f32[8,1152]{1,0:T(8,128)}) custom-call(s32[1]{0:T(128)} %bitcast.side_ref, bf16[1152,2304]{1,0:T(8,128)(2,1)} %bitcast.95, bf16[1152,2304]{1,0:T(8,128)(2,1)} %collective-permute-done.12.other_ref, bf16[256,2304]{1,0:T(8,128)(2,1)} %get-tuple-element.179.refs_6_.mine_ref.rest_0_, ...), custom_call_target="tpu_custom_call" | custom-call | flops 2038431744 | bytes 16000000 | tf_op jit(solution)/shard_map/tokens_back/pallas_call | solution.py:1236
  343.3 3.0 split.11
  350.2 2.3 collective-permute-start.39
  355.3 3.3 split.12
  361.5 2.0 collective-permute-start.52
  363.5 3.9 collective-permute-done.46.r_ref
  369.7 8.2 %product.5 = (bf16[8,72,768]{2,1,0:T(8,128)(2,1)}, bf16[8,72,768]{2,1,0:T(8,128)(2,1)}, bf16[8,72,768]{2,1,0:T(8,128)(2,1)}, bf16[8,72,768]{2,1,0:T(8,128)(2,1)}...) custom-call(s32[1]{0:T(128)} %bitcast.1.chip_ref, bf16[256,2304]{1,0:T(8,128)(2,1)} %get-tuple-element.212.l0_ref, ...), custom_call_target="tpu_custom_call" | custom-call | flops 2717908992 | bytes 12000000 | tf_op jit(solution)/shard_map/product/pallas_call | solution.py:461
  378.6 1.8 meet.6.v_ref
  382.5 2.0 collective-permute-start.50
  385.9 4.5 collective-permute-done.52.r_ref
  391.3 2.5 finish.2.refs_7_.own_ref
  394.5 2.0 meet.7.refs_6_
  399.5 4.3 collective-permute-done.49.refs_1_
  403.8 5.5 %collective-permute-done.51.refs_5_ = bf16[8,72,768]{2,1,0:T(8,128)(2,1)S(1)} collective-permute-done((bf16[8,72,768]{2,1,0:T(8,128)(2,1)S(1)}, bf16[8,72,768]{2,1,0:T(8,128)(2,1)S(1)}, u32[]{:S(2)}, u32[]{:S(2)}) %collective-permute-start.51) | collective-permute-done | bytes 884768 | tf_op jit(solution)/shard_map/ppermute | solution.py:18
  410.2 4.5 split.13
  423.8 1.7 convolution_add_fusion.refs_9_
  425.5 2.9 fc2_rows.1.refs_7_
  428.4 3.0 split.14
  431.4 2.0 collective-permute-start.57
  436.2 2.1 collective-permute-done.57.refs_1_
  441.3 2.4 split.15
  446.2 4.2 all-to-all-start.2
  454.9 3.7 fc1_rows.1.rest_1_
  458.6 1.9 all-to-all-done.2
  461.9 2.0 finish.3.own_ref
  467.1 2.4 attn_rows.1
  (343 shorter events, 111.8 us)
Async XLA Ops:
  2.6 24.2 %collective-permute-start = (bf16[1,72,2304]{2,1,0:T(8,128)(2,1)}, bf16[1,72,2304]{2,1,0:T(8,128)(2,1)S(1)}, u32[]{:S(2)}, u32[]{:S(2)}) collective-permute-start(bf16[1,72,2304]{2,1,0:T(8,128)(2,1)} %attn_shard.1.rest_0_.refs_1_.refs_0_), channel_id=1, source_target_pairs={{0,8},{1,9},{2,10},{3,11},{4,12},{5,13},{6,14},{7,15},{8,0},{9,1},... | collective-permute-start | bytes 995336 | tf_op jit(solution)/shard_map/ppermute | solution.py:18
  10.7 15.4 %all-to-all-start = ((bf16[16,2,576]{2,1,0:T(2,128)(2,1)}), bf16[16,2,576]{2,1,0:T(2,128)(2,1)S(1)}, u32[]{:S(2)}, u32[]{:S(2)}) async-start(bf16[16,2,576]{2,1,0:T(2,128)(2,1)} %reshape.250), calls=%async_computation | async-start | bytes 81920 | tf_op jit(solution)/shard_map/all_to_all | solution.py:45
  29.5 7.2 %collective-permute-start.1 = (bf16[2,72,768]{2,1,0:T(8,128)(2,1)}, bf16[2,72,768]{2,1,0:T(8,128)(2,1)S(1)}, u32[]{:S(2)}, u32[]{:S(2)}) collective-permute-start(bf16[2,72,768]{2,1,0:T(8,128)(2,1)} %get-tuple-element.125.refs_0_.refs_6_.refs_1_), channel_id=1, source_target_pairs={{0,4},{1,5},{2,6},{3,7},{4,0},{5,1},{6,2},{7,3},{8,12},{9,13},{10,... | collective-permute-start | bytes 663560 | tf_op jit(solution)/shard_map/ppermute | solution.py:18
  31.5 6.3 %collective-permute-start.2 = (bf16[2,72,768]{2,1,0:T(8,128)(2,1)}, bf16[2,72,768]{2,1,0:T(8,128)(2,1)S(1)}, u32[]{:S(2)}, u32[]{:S(2)}) collective-permute-start(bf16[2,72,768]{2,1,0:T(8,128)(2,1)} %get-tuple-element.126.refs_2_.refs_7_), channel_id=1, source_target_pairs={{0,1},{1,0},{2,3},{3,2},{4,5},{5,4},{6,7},{7,6},{8,9},{9,8},{10,11... | collective-permute-start | bytes 663560 | tf_op jit(solution)/shard_map/ppermute | solution.py:18
  32.9 6.1 %collective-permute-start.3 = (bf16[2,72,768]{2,1,0:T(8,128)(2,1)}, bf16[2,72,768]{2,1,0:T(8,128)(2,1)S(1)}, u32[]{:S(2)}, u32[]{:S(2)}) collective-permute-start(bf16[2,72,768]{2,1,0:T(8,128)(2,1)} %get-tuple-element.127.refs_4_.refs_8_.refs_3_), channel_id=1, source_target_pairs={{0,2},{1,3},{2,0},{3,1},{4,6},{5,7},{6,4},{7,5},{8,10},{9,11},{10,... | collective-permute-start | bytes 663560 | tf_op jit(solution)/shard_map/ppermute | solution.py:18
  34.4 30.4 %collective-permute-start.7 = (bf16[1,72,4608]{2,1,0:T(8,128)(2,1)}, bf16[1,72,4608]{2,1,0:T(8,128)(2,1)S(1)}, u32[]{:S(2)}, u32[]{:S(2)}) collective-permute-start(bf16[1,72,4608]{2,1,0:T(8,128)(2,1)} %hold.5.refs_6_), channel_id=1, source_target_pairs={{0,8},{1,9},{2,10},{3,11},{4,12},{5,13},{6,14},{7,15},{8,0},{9,1},... | collective-permute-start | bytes 1990664 | tf_op jit(solution)/shard_map/ppermute | solution.py:18
  42.3 22.5 %collective-permute-start.4 = (bf16[4,72,768]{2,1,0:T(8,128)(2,1)}, bf16[4,72,768]{2,1,0:T(8,128)(2,1)S(1)}, u32[]{:S(2)}, u32[]{:S(2)}) collective-permute-start(bf16[4,72,768]{2,1,0:T(8,128)(2,1)} %get-tuple-element.128.refs_0_), channel_id=1, source_target_pairs={{0,2},{1,3},{2,0},{3,1},{4,6},{5,7},{6,4},{7,5},{8,10},{9,11},{10,... | collective-permute-start | bytes 1327112 | tf_op jit(solution)/shard_map/ppermute | solution.py:18
  44.1 21.3 %collective-permute-start.5 = (bf16[4,72,768]{2,1,0:T(8,128)(2,1)}, bf16[4,72,768]{2,1,0:T(8,128)(2,1)S(1)}, u32[]{:S(2)}, u32[]{:S(2)}) collective-permute-start(bf16[4,72,768]{2,1,0:T(8,128)(2,1)} %get-tuple-element.129.refs_2_), channel_id=1, source_target_pairs={{0,4},{1,5},{2,6},{3,7},{4,0},{5,1},{6,2},{7,3},{8,12},{9,13},{10,... | collective-permute-start | bytes 1327112 | tf_op jit(solution)/shard_map/ppermute | solution.py:18
  44.6 20.8 %collective-permute-start.6 = (bf16[4,72,768]{2,1,0:T(8,128)(2,1)}, bf16[4,72,768]{2,1,0:T(8,128)(2,1)S(1)}, u32[]{:S(2)}, u32[]{:S(2)}) collective-permute-start(bf16[4,72,768]{2,1,0:T(8,128)(2,1)} %get-tuple-element.130.refs_4_), channel_id=1, source_target_pairs={{0,1},{1,0},{2,3},{3,2},{4,5},{5,4},{6,7},{7,6},{8,9},{9,8},{10,11... | collective-permute-start | bytes 1327112 | tf_op jit(solution)/shard_map/ppermute | solution.py:18
  71.2 29.6 %collective-permute-start.10 = (bf16[12,72,768]{2,1,0:T(8,128)(2,1)}, bf16[12,72,768]{2,1,0:T(8,128)(2,1)S(1)}, u32[]{:S(2)}, u32[]{:S(2)}) collective-permute-start(bf16[12,72,768]{2,1,0:T(8,128)(2,1)} %get-tuple-element.132.refs_4_.refs_2_), channel_id=1, source_target_pairs={{0,2},{1,3},{2,0},{3,1},{4,6},{5,7},{6,4},{7,5},{8,10},{9,11},{10,... | collective-permute-start | bytes 3981320 | tf_op jit(solution)/shard_map/ppermute | solution.py:18
  71.4 29.3 %collective-permute-start.11 = (bf16[12,72,768]{2,1,0:T(8,128)(2,1)}, bf16[12,72,768]{2,1,0:T(8,128)(2,1)S(1)}, u32[]{:S(2)}, u32[]{:S(2)}) collective-permute-start(bf16[12,72,768]{2,1,0:T(8,128)(2,1)} %get-tuple-element.133.refs_0_.refs_4_), channel_id=1, source_target_pairs={{0,4},{1,5},{2,6},{3,7},{4,0},{5,1},{6,2},{7,3},{8,12},{9,13},{10,... | collective-permute-start | bytes 3981320 | tf_op jit(solution)/shard_map/ppermute | solution.py:18
  71.4 29.4 %collective-permute-start.9 = (bf16[12,72,768]{2,1,0:T(8,128)(2,1)}, bf16[12,72,768]{2,1,0:T(8,128)(2,1)S(1)}, u32[]{:S(2)}, u32[]{:S(2)}) collective-permute-start(bf16[12,72,768]{2,1,0:T(8,128)(2,1)} %get-tuple-element.131.refs_2_.refs_0_), channel_id=1, source_target_pairs={{0,1},{1,0},{2,3},{3,2},{4,5},{5,4},{6,7},{7,6},{8,9},{9,8},{10,11... | collective-permute-start | bytes 3981320 | tf_op jit(solution)/shard_map/ppermute | solution.py:18
  114.4 43.5 %collective-permute-start.12 = (bf16[1152,2304]{1,0:T(8,128)(2,1)}, bf16[1152,2304]{1,0:T(8,128)(2,1)}, u32[]{:S(2)}, u32[]{:S(2)}) collective-permute-start(bf16[1152,2304]{1,0:T(8,128)(2,1)} %bitcast.92), channel_id=1, source_target_pairs={{0,16},{16,0},{1,17},{17,1},{2,18},{18,2},{3,19},{19,3},{4,20},{20... | collective-permute-start | bytes 15925256 | tf_op jit(solution)/shard_map/ppermute | solution.py:22
  114.4 32.1 %collective-permute-start.13 = (bf16[4,72,1536]{2,1,0:T(8,128)(2,1)S(1)}, bf16[4,72,1536]{2,1,0:T(8,128)(2,1)}, u32[]{:S(2)}, u32[]{:S(2)}) collective-permute-start(bf16[4,72,1536]{2,1,0:T(8,128)(2,1)S(1)} %copy-done.6), channel_id=1, source_target_pairs={{0,2},{1,3},{2,0},{3,1},{4,6},{5,7},{6,4},{7,5},{8,10},{9,11},{10,... | collective-permute-start | bytes 2654216 | tf_op jit(solution)/shard_map/ppermute | solution.py:18
  115.8 30.7 %collective-permute-start.14 = (bf16[4,72,1536]{2,1,0:T(8,128)(2,1)S(1)}, bf16[4,72,1536]{2,1,0:T(8,128)(2,1)}, u32[]{:S(2)}, u32[]{:S(2)}) collective-permute-start(bf16[4,72,1536]{2,1,0:T(8,128)(2,1)S(1)} %copy-done.7), channel_id=1, source_target_pairs={{0,4},{1,5},{2,6},{3,7},{4,0},{5,1},{6,2},{7,3},{8,12},{9,13},{10,... | collective-permute-start | bytes 2654216 | tf_op jit(solution)/shard_map/ppermute | solution.py:18
  116.5 30.1 %collective-permute-start.15 = (bf16[4,72,1536]{2,1,0:T(8,128)(2,1)}, bf16[4,72,1536]{2,1,0:T(8,128)(2,1)}, u32[]{:S(2)}, u32[]{:S(2)}) collective-permute-start(bf16[4,72,1536]{2,1,0:T(8,128)(2,1)} %get-tuple-element.136.refs_8_.refs_4_), channel_id=1, source_target_pairs={{0,1},{1,0},{2,3},{3,2},{4,5},{5,4},{6,7},{7,6},{8,9},{9,8},{10,11... | collective-permute-start | bytes 2654216 | tf_op jit(solution)/shard_map/ppermute | solution.py:18
  120.1 25.6 %all-to-all-start.1 = ((f32[16,1,6912]{2,1,0:T(1,128)}), f32[16,1,6912]{2,1,0:T(1,128)S(1)}, u32[]{:S(2)}, u32[]{:S(2)}) async-start(f32[16,1,6912]{2,1,0:T(1,128)} %copy.77), calls=%async_computation.1 | async-start | bytes 884736 | tf_op jit(solution)/shard_map/all_to_all | solution.py:45
  151.7 39.9 %collective-permute-start.16 = (bf16[8,72,1536]{2,1,0:T(8,128)(2,1)}, bf16[8,72,1536]{2,1,0:T(8,128)(2,1)}, u32[]{:S(2)}, u32[]{:S(2)}) collective-permute-start(bf16[8,72,1536]{2,1,0:T(8,128)(2,1)} %get-tuple-element.138.refs_0_), channel_id=1, source_target_pairs={{0,1},{1,0},{2,3},{3,2},{4,5},{5,4},{6,7},{7,6},{8,9},{9,8},{10,11... | collective-permute-start | bytes 5308424 | tf_op jit(solution)/shard_map/ppermute | solution.py:18
  152.0 39.9 %collective-permute-start.17 = (bf16[8,72,1536]{2,1,0:T(8,128)(2,1)}, bf16[8,72,1536]{2,1,0:T(8,128)(2,1)}, u32[]{:S(2)}, u32[]{:S(2)}) collective-permute-start(bf16[8,72,1536]{2,1,0:T(8,128)(2,1)} %get-tuple-element.139.refs_2_), channel_id=1, source_target_pairs={{0,2},{1,3},{2,0},{3,1},{4,6},{5,7},{6,4},{7,5},{8,10},{9,11},{10,... | collective-permute-start | bytes 5308424 | tf_op jit(solution)/shard_map/ppermute | solution.py:18
  153.6 38.8 %collective-permute-start.18 = (bf16[8,72,1536]{2,1,0:T(8,128)(2,1)}, bf16[8,72,1536]{2,1,0:T(8,128)(2,1)}, u32[]{:S(2)}, u32[]{:S(2)}) collective-permute-start(bf16[8,72,1536]{2,1,0:T(8,128)(2,1)} %get-tuple-element.140.refs_4_), channel_id=1, source_target_pairs={{0,4},{1,5},{2,6},{3,7},{4,0},{5,1},{6,2},{7,3},{8,12},{9,13},{10,... | collective-permute-start | bytes 5308424 | tf_op jit(solution)/shard_map/ppermute | solution.py:18
  201.1 16.7 %collective-permute-start.19 = (bf16[1152,4608]{1,0:T(8,128)(2,1)}, bf16[1152,4608]{1,0:T(8,128)(2,1)}, u32[]{:S(2)}, u32[]{:S(2)}) collective-permute-start(bf16[1152,4608]{1,0:T(8,128)(2,1)} %bitcast.85), channel_id=1, source_target_pairs={{0,16},{16,0},{1,17},{17,1},{2,18},{18,2},{3,19},{19,3},{4,20},{20... | collective-permute-start | bytes 31850504 | tf_op jit(solution)/shard_map/ppermute | solution.py:22
  229.6 5.1 %collective-permute-start.20 = (bf16[256,2304]{1,0:T(8,128)(2,1)}, bf16[256,2304]{1,0:T(8,128)(2,1)S(1)}, u32[]{:S(2)}, u32[]{:S(2)}) collective-permute-start(bf16[256,2304]{1,0:T(8,128)(2,1)} %get-tuple-element.153), channel_id=1, source_target_pairs={{0,16},{16,0},{1,17},{17,1},{2,18},{18,2},{3,19},{19,3},{4,20},{20... | collective-permute-start | bytes 3538952 | tf_op jit(solution)/shard_map/ppermute | solution.py:22
  229.8 15.9 %collective-permute-start.22 = (bf16[256,2304]{1,0:T(8,128)(2,1)S(1)}, bf16[256,2304]{1,0:T(8,128)(2,1)S(1)}, u32[]{:S(2)}, u32[]{:S(2)}) collective-permute-start(bf16[256,2304]{1,0:T(8,128)(2,1)S(1)} %copy-done.70), channel_id=1, source_target_pairs={{0,16},{16,0},{1,17},{17,1},{2,18},{18,2},{3,19},{19,3},{4,20},{20... | collective-permute-start | bytes 3538952 | tf_op jit(solution)/shard_map/ppermute | solution.py:22
  230.2 4.5 collective-permute-start.21
  230.3 15.4 %collective-permute-start.23 = (bf16[256,1152]{1,0:T(8,128)(2,1)S(1)}, bf16[256,1152]{1,0:T(8,128)(2,1)S(1)}, u32[]{:S(2)}, u32[]{:S(2)}) collective-permute-start(bf16[256,1152]{1,0:T(8,128)(2,1)S(1)} %copy-done.5), channel_id=1, source_target_pairs={{0,16},{16,0},{1,17},{17,1},{2,18},{18,2},{3,19},{19,3},{4,20},{20... | collective-permute-start | bytes 1769480 | tf_op jit(solution)/shard_map/ppermute | solution.py:22
  242.5 24.2 %collective-permute-start.24 = (bf16[8,72,768]{2,1,0:T(8,128)(2,1)}, bf16[8,72,768]{2,1,0:T(8,128)(2,1)S(1)}, u32[]{:S(2)}, u32[]{:S(2)}) collective-permute-start(bf16[8,72,768]{2,1,0:T(8,128)(2,1)} %get-tuple-element.158), channel_id=1, source_target_pairs={{0,1},{1,0},{2,3},{3,2},{4,5},{5,4},{6,7},{7,6},{8,9},{9,8},{10,11... | collective-permute-start | bytes 2654216 | tf_op jit(solution)/shard_map/ppermute | solution.py:18
  243.6 23.1 %collective-permute-start.25 = (bf16[8,72,768]{2,1,0:T(8,128)(2,1)}, bf16[8,72,768]{2,1,0:T(8,128)(2,1)S(1)}, u32[]{:S(2)}, u32[]{:S(2)}) collective-permute-start(bf16[8,72,768]{2,1,0:T(8,128)(2,1)} %get-tuple-element.160), channel_id=1, source_target_pairs={{0,2},{1,3},{2,0},{3,1},{4,6},{5,7},{6,4},{7,5},{8,10},{9,11},{10,... | collective-permute-start | bytes 2654216 | tf_op jit(solution)/shard_map/ppermute | solution.py:18
  245.4 21.3 %collective-permute-start.26 = (bf16[8,72,768]{2,1,0:T(8,128)(2,1)}, bf16[8,72,768]{2,1,0:T(8,128)(2,1)S(1)}, u32[]{:S(2)}, u32[]{:S(2)}) collective-permute-start(bf16[8,72,768]{2,1,0:T(8,128)(2,1)} %get-tuple-element.162), channel_id=1, source_target_pairs={{0,4},{1,5},{2,6},{3,7},{4,0},{5,1},{6,2},{7,3},{8,12},{9,13},{10,... | collective-permute-start | bytes 2654216 | tf_op jit(solution)/shard_map/ppermute | solution.py:18
  266.6 9.1 %collective-permute-start.27 = (bf16[256,2304]{1,0:T(8,128)(2,1)}, bf16[256,2304]{1,0:T(8,128)(2,1)S(1)}, u32[]{:S(2)}, u32[]{:S(2)}) collective-permute-start(bf16[256,2304]{1,0:T(8,128)(2,1)} %get-tuple-element.166), channel_id=1, source_target_pairs={{0,16},{16,0},{1,17},{17,1},{2,18},{18,2},{3,19},{19,3},{4,20},{20... | collective-permute-start | bytes 3538952 | tf_op jit(solution)/shard_map/ppermute | solution.py:22
  272.8 13.9 %collective-permute-start.28 = (bf16[4,72,768]{2,1,0:T(8,128)(2,1)}, bf16[4,72,768]{2,1,0:T(8,128)(2,1)S(1)}, u32[]{:S(2)}, u32[]{:S(2)}) collective-permute-start(bf16[4,72,768]{2,1,0:T(8,128)(2,1)} %get-tuple-element.172), channel_id=1, source_target_pairs={{0,2},{1,3},{2,0},{3,1},{4,6},{5,7},{6,4},{7,5},{8,10},{9,11},{10,... | collective-permute-start | bytes 1327112 | tf_op jit(solution)/shard_map/ppermute | solution.py:18
  273.3 13.4 %collective-permute-start.29 = (bf16[4,72,768]{2,1,0:T(8,128)(2,1)}, bf16[4,72,768]{2,1,0:T(8,128)(2,1)S(1)}, u32[]{:S(2)}, u32[]{:S(2)}) collective-permute-start(bf16[4,72,768]{2,1,0:T(8,128)(2,1)} %get-tuple-element.173), channel_id=1, source_target_pairs={{0,4},{1,5},{2,6},{3,7},{4,0},{5,1},{6,2},{7,3},{8,12},{9,13},{10,... | collective-permute-start | bytes 1327112 | tf_op jit(solution)/shard_map/ppermute | solution.py:18
  274.8 12.3 %collective-permute-start.30 = (bf16[4,72,768]{2,1,0:T(8,128)(2,1)}, bf16[4,72,768]{2,1,0:T(8,128)(2,1)S(1)}, u32[]{:S(2)}, u32[]{:S(2)}) collective-permute-start(bf16[4,72,768]{2,1,0:T(8,128)(2,1)} %get-tuple-element.174), channel_id=1, source_target_pairs={{0,1},{1,0},{2,3},{3,2},{4,5},{5,4},{6,7},{7,6},{8,9},{9,8},{10,11... | collective-permute-start | bytes 1327112 | tf_op jit(solution)/shard_map/ppermute | solution.py:18
  297.2 21.3 %collective-permute-start.31 = (bf16[8,72,768]{2,1,0:T(8,128)(2,1)}, bf16[8,72,768]{2,1,0:T(8,128)(2,1)S(1)}, u32[]{:S(2)}, u32[]{:S(2)}) collective-permute-start(bf16[8,72,768]{2,1,0:T(8,128)(2,1)} %get-tuple-element.183), channel_id=1, source_target_pairs={{0,1},{1,0},{2,3},{3,2},{4,5},{5,4},{6,7},{7,6},{8,9},{9,8},{10,11... | collective-permute-start | bytes 2654216 | tf_op jit(solution)/shard_map/ppermute | solution.py:18
  298.2 21.2 %collective-permute-start.32 = (bf16[8,72,768]{2,1,0:T(8,128)(2,1)}, bf16[8,72,768]{2,1,0:T(8,128)(2,1)S(1)}, u32[]{:S(2)}, u32[]{:S(2)}) collective-permute-start(bf16[8,72,768]{2,1,0:T(8,128)(2,1)} %get-tuple-element.185), channel_id=1, source_target_pairs={{0,2},{1,3},{2,0},{3,1},{4,6},{5,7},{6,4},{7,5},{8,10},{9,11},{10,... | collective-permute-start | bytes 2654216 | tf_op jit(solution)/shard_map/ppermute | solution.py:18
  300.0 20.9 %collective-permute-start.33 = (bf16[8,72,768]{2,1,0:T(8,128)(2,1)}, bf16[8,72,768]{2,1,0:T(8,128)(2,1)S(1)}, u32[]{:S(2)}, u32[]{:S(2)}) collective-permute-start(bf16[8,72,768]{2,1,0:T(8,128)(2,1)} %get-tuple-element.187), channel_id=1, source_target_pairs={{0,4},{1,5},{2,6},{3,7},{4,0},{5,1},{6,2},{7,3},{8,12},{9,13},{10,... | collective-permute-start | bytes 2654216 | tf_op jit(solution)/shard_map/ppermute | solution.py:18
  313.1 15.8 %collective-permute-start.34 = (bf16[128,2304]{1,0:T(8,128)(2,1)}, bf16[128,2304]{1,0:T(8,128)(2,1)S(1)}, u32[]{:S(2)}, u32[]{:S(2)}) collective-permute-start(bf16[128,2304]{1,0:T(8,128)(2,1)} %get-tuple-element.180.top_ref), channel_id=1, source_target_pairs={{0,16},{16,0},{1,17},{17,1},{2,18},{18,2},{3,19},{19,3},{4,20},{20... | collective-permute-start | bytes 1769480 | tf_op jit(solution)/shard_map/ppermute | solution.py:22
  313.1 16.7 %collective-permute-start.35 = (bf16[128,2304]{1,0:T(8,128)(2,1)}, bf16[128,2304]{1,0:T(8,128)(2,1)S(1)}, u32[]{:S(2)}, u32[]{:S(2)}) collective-permute-start(bf16[128,2304]{1,0:T(8,128)(2,1)} %get-tuple-element.181.low_ref), channel_id=1, source_target_pairs={{0,16},{16,0},{1,17},{17,1},{2,18},{18,2},{3,19},{19,3},{4,20},{20... | collective-permute-start | bytes 1769480 | tf_op jit(solution)/shard_map/ppermute | solution.py:22
  326.4 14.4 %collective-permute-start.36 = (bf16[4,72,768]{2,1,0:T(8,128)(2,1)}, bf16[4,72,768]{2,1,0:T(8,128)(2,1)S(1)}, u32[]{:S(2)}, u32[]{:S(2)}) collective-permute-start(bf16[4,72,768]{2,1,0:T(8,128)(2,1)} %get-tuple-element.199), channel_id=1, source_target_pairs={{0,2},{1,3},{2,0},{3,1},{4,6},{5,7},{6,4},{7,5},{8,10},{9,11},{10,... | collective-permute-start | bytes 1327112 | tf_op jit(solution)/shard_map/ppermute | solution.py:18
  327.0 15.4 %collective-permute-start.37 = (bf16[4,72,768]{2,1,0:T(8,128)(2,1)}, bf16[4,72,768]{2,1,0:T(8,128)(2,1)S(1)}, u32[]{:S(2)}, u32[]{:S(2)}) collective-permute-start(bf16[4,72,768]{2,1,0:T(8,128)(2,1)} %get-tuple-element.200), channel_id=1, source_target_pairs={{0,4},{1,5},{2,6},{3,7},{4,0},{5,1},{6,2},{7,3},{8,12},{9,13},{10,... | collective-permute-start | bytes 1327112 | tf_op jit(solution)/shard_map/ppermute | solution.py:18
  327.3 15.1 %collective-permute-start.38 = (bf16[4,72,768]{2,1,0:T(8,128)(2,1)}, bf16[4,72,768]{2,1,0:T(8,128)(2,1)S(1)}, u32[]{:S(2)}, u32[]{:S(2)}) collective-permute-start(bf16[4,72,768]{2,1,0:T(8,128)(2,1)} %get-tuple-element.201), channel_id=1, source_target_pairs={{0,1},{1,0},{2,3},{3,2},{4,5},{5,4},{6,7},{7,6},{8,9},{9,8},{10,11... | collective-permute-start | bytes 1327112 | tf_op jit(solution)/shard_map/ppermute | solution.py:18
  328.9 18.6 %collective-permute-start.40 = (bf16[2,72,768]{2,1,0:T(8,128)(2,1)S(1)}, bf16[2,72,768]{2,1,0:T(8,128)(2,1)S(1)}, u32[]{:S(2)}, u32[]{:S(2)}) collective-permute-start(bf16[2,72,768]{2,1,0:T(8,128)(2,1)S(1)} %copy-done.76), channel_id=1, source_target_pairs={{0,4},{1,5},{2,6},{3,7},{4,0},{5,1},{6,2},{7,3},{8,12},{9,13},{10,... | collective-permute-start | bytes 663560 | tf_op jit(solution)/shard_map/ppermute | solution.py:18
  329.8 20.5 %collective-permute-start.41 = (bf16[2,72,768]{2,1,0:T(8,128)(2,1)S(1)}, bf16[2,72,768]{2,1,0:T(8,128)(2,1)S(1)}, u32[]{:S(2)}, u32[]{:S(2)}) collective-permute-start(bf16[2,72,768]{2,1,0:T(8,128)(2,1)S(1)} %copy-done.75), channel_id=1, source_target_pairs={{0,1},{1,0},{2,3},{3,2},{4,5},{5,4},{6,7},{7,6},{8,9},{9,8},{10,11... | collective-permute-start | bytes 663560 | tf_op jit(solution)/shard_map/ppermute | solution.py:18
  340.8 11.7 %collective-permute-start.42 = (bf16[2,72,768]{2,1,0:T(8,128)(2,1)S(1)}, bf16[2,72,768]{2,1,0:T(8,128)(2,1)S(1)}, u32[]{:S(2)}, u32[]{:S(2)}) collective-permute-start(bf16[2,72,768]{2,1,0:T(8,128)(2,1)S(1)} %copy-done.74), channel_id=1, source_target_pairs={{0,2},{1,3},{2,0},{3,1},{4,6},{5,7},{6,4},{7,5},{8,10},{9,11},{10,... | collective-permute-start | bytes 663560 | tf_op jit(solution)/shard_map/ppermute | solution.py:18
  346.3 7.5 %collective-permute-start.43 = (bf16[2,72,768]{2,1,0:T(8,128)(2,1)}, bf16[2,72,768]{2,1,0:T(8,128)(2,1)S(1)}, u32[]{:S(2)}, u32[]{:S(2)}) collective-permute-start(bf16[2,72,768]{2,1,0:T(8,128)(2,1)} %get-tuple-element.208), channel_id=1, source_target_pairs={{0,4},{1,5},{2,6},{3,7},{4,0},{5,1},{6,2},{7,3},{8,12},{9,13},{10,... | collective-permute-start | bytes 663560 | tf_op jit(solution)/shard_map/ppermute | solution.py:18
  346.6 7.3 %collective-permute-start.44 = (bf16[2,72,768]{2,1,0:T(8,128)(2,1)}, bf16[2,72,768]{2,1,0:T(8,128)(2,1)S(1)}, u32[]{:S(2)}, u32[]{:S(2)}) collective-permute-start(bf16[2,72,768]{2,1,0:T(8,128)(2,1)} %get-tuple-element.209), channel_id=1, source_target_pairs={{0,1},{1,0},{2,3},{3,2},{4,5},{5,4},{6,7},{7,6},{8,9},{9,8},{10,11... | collective-permute-start | bytes 663560 | tf_op jit(solution)/shard_map/ppermute | solution.py:18
  347.5 6.4 %collective-permute-start.45 = (bf16[2,72,768]{2,1,0:T(8,128)(2,1)}, bf16[2,72,768]{2,1,0:T(8,128)(2,1)S(1)}, u32[]{:S(2)}, u32[]{:S(2)}) collective-permute-start(bf16[2,72,768]{2,1,0:T(8,128)(2,1)} %get-tuple-element.210), channel_id=1, source_target_pairs={{0,2},{1,3},{2,0},{3,1},{4,6},{5,7},{6,4},{7,5},{8,10},{9,11},{10,... | collective-permute-start | bytes 663560 | tf_op jit(solution)/shard_map/ppermute | solution.py:18
  350.2 8.3 %collective-permute-start.39 = (f32[256,128]{1,0:T(8,128)}, f32[256,128]{1,0:T(8,128)S(1)}, u32[]{:S(2)}, u32[]{:S(2)}) collective-permute-start(f32[256,128]{1,0:T(8,128)} %pack.1.refs_12_.v_ref), channel_id=1, source_target_pairs={{0,8},{1,9},{2,10},{3,11},{4,12},{5,13},{6,14},{7,15},{8,0},{9,1},... | collective-permute-start | bytes 393224 | tf_op jit(solution)/shard_map/ppermute | solution.py:18
  360.9 6.5 %collective-permute-start.46 = (f32[312,128]{1,0:T(8,128)}, f32[312,128]{1,0:T(8,128)S(1)}, u32[]{:S(2)}, u32[]{:S(2)}) collective-permute-start(f32[312,128]{1,0:T(8,128)} %meet.4.v_ref), channel_id=1, source_target_pairs={{0,4},{1,5},{2,6},{3,7},{4,0},{5,1},{6,2},{7,3},{8,12},{9,13},{10,... | collective-permute-start | bytes 479240 | tf_op jit(solution)/shard_map/ppermute | solution.py:18
  361.5 28.9 %collective-permute-start.52 = (bf16[1,72,4608]{2,1,0:T(8,128)(2,1)}, bf16[1,72,4608]{2,1,0:T(8,128)(2,1)S(1)}, u32[]{:S(2)}, u32[]{:S(2)}) collective-permute-start(bf16[1,72,4608]{2,1,0:T(8,128)(2,1)} %get-tuple-element.219), channel_id=1, source_target_pairs={{0,8},{1,9},{2,10},{3,11},{4,12},{5,13},{6,14},{7,15},{8,0},{9,1},... | collective-permute-start | bytes 1990664 | tf_op jit(solution)/shard_map/ppermute | solution.py:18
  369.7 8.2 %collective-permute-start.47 = (f32[424,128]{1,0:T(8,128)}, f32[424,128]{1,0:T(8,128)S(1)}, u32[]{:S(2)}, u32[]{:S(2)}) collective-permute-start(f32[424,128]{1,0:T(8,128)} %meet.5.rest_3_.v_ref), channel_id=1, source_target_pairs={{0,2},{1,3},{2,0},{3,1},{4,6},{5,7},{6,4},{7,5},{8,10},{9,11},{10,... | collective-permute-start | bytes 651272 | tf_op jit(solution)/shard_map/ppermute | solution.py:18
  380.4 13.3 %collective-permute-start.48 = (f32[648,128]{1,0:T(8,128)}, f32[648,128]{1,0:T(8,128)S(1)}, u32[]{:S(2)}, u32[]{:S(2)}) collective-permute-start(f32[648,128]{1,0:T(8,128)} %meet.6.v_ref), channel_id=1, source_target_pairs={{0,1},{1,0},{2,3},{3,2},{4,5},{5,4},{6,7},{7,6},{8,9},{9,8},{10,11... | collective-permute-start | bytes 995336 | tf_op jit(solution)/shard_map/ppermute | solution.py:18
  381.3 22.5 %collective-permute-start.49 = (bf16[8,72,768]{2,1,0:T(8,128)(2,1)}, bf16[8,72,768]{2,1,0:T(8,128)(2,1)S(1)}, u32[]{:S(2)}, u32[]{:S(2)}) collective-permute-start(bf16[8,72,768]{2,1,0:T(8,128)(2,1)} %get-tuple-element.214), channel_id=1, source_target_pairs={{0,1},{1,0},{2,3},{3,2},{4,5},{5,4},{6,7},{7,6},{8,9},{9,8},{10,11... | collective-permute-start | bytes 2654216 | tf_op jit(solution)/shard_map/ppermute | solution.py:18
  382.5 21.3 %collective-permute-start.50 = (bf16[8,72,768]{2,1,0:T(8,128)(2,1)}, bf16[8,72,768]{2,1,0:T(8,128)(2,1)S(1)}, u32[]{:S(2)}, u32[]{:S(2)}) collective-permute-start(bf16[8,72,768]{2,1,0:T(8,128)(2,1)} %get-tuple-element.216), channel_id=1, source_target_pairs={{0,2},{1,3},{2,0},{3,1},{4,6},{5,7},{6,4},{7,5},{8,10},{9,11},{10,... | collective-permute-start | bytes 2654216 | tf_op jit(solution)/shard_map/ppermute | solution.py:18
  384.5 24.8 %collective-permute-start.51 = (bf16[8,72,768]{2,1,0:T(8,128)(2,1)S(1)}, bf16[8,72,768]{2,1,0:T(8,128)(2,1)S(1)}, u32[]{:S(2)}, u32[]{:S(2)}) collective-permute-start(bf16[8,72,768]{2,1,0:T(8,128)(2,1)S(1)} %copy-done.72), channel_id=1, source_target_pairs={{0,4},{1,5},{2,6},{3,7},{4,0},{5,1},{6,2},{7,3},{8,12},{9,13},{10,... | collective-permute-start | bytes 2654216 | tf_op jit(solution)/shard_map/ppermute | solution.py:18
  393.8 31.7 %collective-permute-start.56 = (f32[72,4608]{1,0:T(8,128)}, f32[72,4608]{1,0:T(8,128)}, u32[]{:S(2)}, u32[]{:S(2)}) collective-permute-start(f32[72,4608]{1,0:T(8,128)} %finish.2.refs_7_.own_ref), channel_id=1, source_target_pairs={{0,16},{16,0},{1,17},{17,1},{2,18},{18,2},{3,19},{19,3},{4,20},{20... | collective-permute-start | bytes 3981320 | tf_op jit(solution)/shard_map/ppermute | solution.py:22
  396.5 20.0 %collective-permute-start.60 = (f32[1096,128]{1,0:T(8,128)}, f32[1096,128]{1,0:T(8,128)S(1)}, u32[]{:S(2)}, u32[]{:S(2)}) collective-permute-start(f32[1096,128]{1,0:T(8,128)} %meet.7.refs_6_), channel_id=1, source_target_pairs={{0,16},{16,0},{1,17},{17,1},{2,18},{18,2},{3,19},{19,3},{4,20},{20... | collective-permute-start | bytes 1683464 | tf_op jit(solution)/shard_map/ppermute | solution.py:22
  414.7 13.7 %collective-permute-start.53 = (bf16[4,72,768]{2,1,0:T(8,128)(2,1)}, bf16[4,72,768]{2,1,0:T(8,128)(2,1)}, u32[]{:S(2)}, u32[]{:S(2)}) collective-permute-start(bf16[4,72,768]{2,1,0:T(8,128)(2,1)} %get-tuple-element.221), channel_id=1, source_target_pairs={{0,2},{1,3},{2,0},{3,1},{4,6},{5,7},{6,4},{7,5},{8,10},{9,11},{10,... | collective-permute-start | bytes 1327112 | tf_op jit(solution)/shard_map/ppermute | solution.py:18
  415.5 12.9 %collective-permute-start.54 = (bf16[4,72,768]{2,1,0:T(8,128)(2,1)}, bf16[4,72,768]{2,1,0:T(8,128)(2,1)}, u32[]{:S(2)}, u32[]{:S(2)}) collective-permute-start(bf16[4,72,768]{2,1,0:T(8,128)(2,1)} %get-tuple-element.223), channel_id=1, source_target_pairs={{0,4},{1,5},{2,6},{3,7},{4,0},{5,1},{6,2},{7,3},{8,12},{9,13},{10,... | collective-permute-start | bytes 1327112 | tf_op jit(solution)/shard_map/ppermute | solution.py:18
  415.5 12.9 %collective-permute-start.55 = (bf16[4,72,768]{2,1,0:T(8,128)(2,1)}, bf16[4,72,768]{2,1,0:T(8,128)(2,1)}, u32[]{:S(2)}, u32[]{:S(2)}) collective-permute-start(bf16[4,72,768]{2,1,0:T(8,128)(2,1)} %get-tuple-element.225), channel_id=1, source_target_pairs={{0,1},{1,0},{2,3},{3,2},{4,5},{5,4},{6,7},{7,6},{8,9},{9,8},{10,11... | collective-permute-start | bytes 1327112 | tf_op jit(solution)/shard_map/ppermute | solution.py:18
  431.4 7.0 %collective-permute-start.57 = (bf16[2,72,768]{2,1,0:T(8,128)(2,1)}, bf16[2,72,768]{2,1,0:T(8,128)(2,1)S(1)}, u32[]{:S(2)}, u32[]{:S(2)}) collective-permute-start(bf16[2,72,768]{2,1,0:T(8,128)(2,1)} %get-tuple-element.227), channel_id=1, source_target_pairs={{0,4},{1,5},{2,6},{3,7},{4,0},{5,1},{6,2},{7,3},{8,12},{9,13},{10,... | collective-permute-start | bytes 663560 | tf_op jit(solution)/shard_map/ppermute | solution.py:18
  433.4 6.4 %collective-permute-start.58 = (bf16[2,72,768]{2,1,0:T(8,128)(2,1)}, bf16[2,72,768]{2,1,0:T(8,128)(2,1)S(1)}, u32[]{:S(2)}, u32[]{:S(2)}) collective-permute-start(bf16[2,72,768]{2,1,0:T(8,128)(2,1)} %get-tuple-element.229), channel_id=1, source_target_pairs={{0,1},{1,0},{2,3},{3,2},{4,5},{5,4},{6,7},{7,6},{8,9},{9,8},{10,11... | collective-permute-start | bytes 663560 | tf_op jit(solution)/shard_map/ppermute | solution.py:18
  434.4 6.2 %collective-permute-start.59 = (bf16[2,72,768]{2,1,0:T(8,128)(2,1)}, bf16[2,72,768]{2,1,0:T(8,128)(2,1)S(1)}, u32[]{:S(2)}, u32[]{:S(2)}) collective-permute-start(bf16[2,72,768]{2,1,0:T(8,128)(2,1)} %get-tuple-element.231), channel_id=1, source_target_pairs={{0,2},{1,3},{2,0},{3,1},{4,6},{5,7},{6,4},{7,5},{8,10},{9,11},{10,... | collective-permute-start | bytes 663560 | tf_op jit(solution)/shard_map/ppermute | solution.py:18
  443.6 17.5 %collective-permute-start.61 = (bf16[1,72,2304]{2,1,0:T(8,128)(2,1)}, bf16[1,72,2304]{2,1,0:T(8,128)(2,1)S(1)}, u32[]{:S(2)}, u32[]{:S(2)}) collective-permute-start(bf16[1,72,2304]{2,1,0:T(8,128)(2,1)} %get-tuple-element.233), channel_id=1, source_target_pairs={{0,8},{1,9},{2,10},{3,11},{4,12},{5,13},{6,14},{7,15},{8,0},{9,1},... | collective-permute-start | bytes 995336 | tf_op jit(solution)/shard_map/ppermute | solution.py:18
  446.2 14.3 %all-to-all-start.2 = ((f32[16,1,72]{2,1,0:T(1,128)}), f32[16,1,72]{2,1,0:T(1,128)S(1)}, u32[]{:S(2)}, u32[]{:S(2)}) async-start(f32[16,1,72]{2,1,0:T(1,128)} %bitcast.113), calls=%async_computation.2 | async-start | bytes 16384 | tf_op jit(solution)/shard_map/all_to_all | solution.py:45
  (79 other events, 418.4 us)
